TPU v7x, 1024 devices: a whole 4x4x32 slice. The times are simulated.
1024 devices in a mesh: group: 8 (over x, core), dev: 128 (over y, z).
Axes of the slice: x: 4, y: 4, z: 32, core: 2. Of those that a mesh axis runs over, the one named last changes fastest.
Arguments:
- guess: float32 [64, 2048, 256], P('group', 'dev'), may hold values from -6 to 6
- divergence: float32 [64, 2048, 256], P('group', 'dev'), may hold values from -24 to 24
- counts: int32 [64, 2048, 256], P('group', 'dev'), may hold values from 0 to 15
Outputs:
- solution_field: float32 [64, 2048, 256], P('group', 'dev')
All inputs are finite; a program needn't handle non-finite values.
Results may differ from a plain program's by a relative error of at most 0.00002.
Values sent between devices are 32-bit elements; how exact they have to be, the bound alone decides.
No kernel may reach another device: no remote copies, remote signals or barrier semaphores. Data moves between devices by JAX's collectives and lax.ppermute only.
A program may use at most 64 MiB of HBM per device.

v0:
```python
import jax
import jax.numpy as jnp
from jax import lax
from jax.sharding import PartitionSpec as P

NU_PRE = 2
NU_POST = 2
NU_COARSE = 4


def with_halo(cells, sides, width):
    for axis, dim in sides:
        count = lax.axis_size(axis)
        ends = count - 1
        head = lax.slice_in_dim(cells, 0, width, axis=dim)
        tail = lax.slice_in_dim(cells, cells.shape[dim] - width, cells.shape[dim], axis=dim)
        cells = jnp.concatenate(
            [
                lax.ppermute(tail, axis, [(i, (i + 1) % count) for i in range(ends)]),
                cells,
                lax.ppermute(head, axis, [((i + 1) % count, i) for i in range(ends)]),
            ],
            axis=dim,
        )
    return cells


def neighbours(padded):
    deeper = jnp.pad(padded, ((0, 0), (0, 0), (1, 1)))
    beside = deeper[2:, 1:-1, 1:-1] + deeper[:-2, 1:-1, 1:-1]
    beside = beside + deeper[1:-1, 2:, 1:-1] + deeper[1:-1, :-2, 1:-1]
    beside = beside + deeper[1:-1, 1:-1, 2:] + deeper[1:-1, 1:-1, :-2]
    return beside


def fine_apply(field, diag):
    padded = with_halo(field, (("group", 0), ("dev", 1)), 1)
    return diag * field - neighbours(padded)


def spread_apply(field, diag):
    padded = with_halo(field, (("group", 0), ("dev", 1)), 1)
    return diag * field - neighbours(padded)


def block_sum(field):
    nx, ny, nz = field.shape
    return field.reshape(nx // 2, 2, ny // 2, 2, nz // 2, 2).sum(axis=(1, 3, 5))


def body(guess, divergence, counts):
    weights = counts.astype(jnp.float32)
    fine_diag = 6.0 + 0.25 * weights
    field = guess
    for sweep in range(NU_PRE):
        field = field + 0.8 * (divergence - fine_apply(field, fine_diag)) / fine_diag
    fine_residual = divergence - fine_apply(field, fine_diag)
    coarse_rhs = 0.5 * block_sum(fine_residual)
    coarse_diag = 6.0 + block_sum(weights) / 8.0
    correction = jnp.zeros_like(coarse_rhs)
    for sweep in range(NU_COARSE):
        correction = (
            correction + 0.8 * (coarse_rhs - spread_apply(correction, coarse_diag)) / coarse_diag
        )
    spread_out = jnp.repeat(jnp.repeat(jnp.repeat(correction, 2, axis=0), 2, axis=1), 2, axis=2)
    field = field + spread_out
    for sweep in range(NU_POST):
        field = field + 0.8 * (divergence - fine_apply(field, fine_diag)) / fine_diag
    return field


def solution(mesh):
    return jax.shard_map(
        body,
        mesh=mesh,
        in_specs=(P("group", "dev", None), P("group", "dev", None), P("group", "dev", None)),
        out_specs=P("group", "dev", None),
        check_vma=False,
    )
```

profile of v0, /device:TPU:25, one launch (start us, length us, event | category | flops | bytes accessed | tf_op | source)
XLA Modules:
  0.0 191.2 jit_solution(12113216409441595000)
XLA Ops:
  0.7 3.7 %collective-permute-start.1 = (f32[1,16,256]{2,1,0:T(8,128)S(1)}, f32[1,16,256]{2,1,0:T(8,128)S(1)}, u32[]{:S(2)}, u32[]{:S(2)}) collective-permute-start(f32[1,16,256]{2,1,0:T(8,128)S(1)} %get-tuple-element.24), channel_id=1, source_target_pairs={{0,128},{128,256},{256,384},{384,512},{512,640},{640,768},{768,896... | collective-permute-start | bytes 49160 | tf_op jit(solution)/shard_map/ppermute | solution.py:19
  9.5 18.6 %collective-permute-start.2 = (f32[10,1,256]{2,1,0:T(1,128)S(1)}, f32[10,1,256]{2,1,0:T(1,128)S(1)}, u32[]{:S(2)}, u32[]{:S(2)}) collective-permute-start(f32[10,1,256]{2,1,0:T(1,128)S(1)} %get-tuple-element.14), channel_id=1, source_target_pairs={{1,0},{2,1},{3,2},{4,3},{5,4},{6,5},{7,6},{8,7},{9,8},{10,9},{11,1... | collective-permute-start | bytes 30728 | tf_op jit(solution)/shard_map/ppermute | solution.py:21
  30.0 4.6 %collective-permute-done.3 = f32[10,1,256]{2,1,0:T(1,128)S(1)} collective-permute-done((f32[10,1,256]{2,1,0:T(1,128)S(1)}, f32[10,1,256]{2,1,0:T(1,128)S(1)}, u32[]{:S(2)}, u32[]{:S(2)}) %collective-permute-start.3) | collective-permute-done | bytes 10272 | tf_op jit(solution)/shard_map/ppermute | solution.py:19
  38.1 3.6 %collective-permute-start.5 = (f32[1,16,256]{2,1,0:T(8,128)S(1)}, f32[1,16,256]{2,1,0:T(8,128)S(1)}, u32[]{:S(2)}, u32[]{:S(2)}) collective-permute-start(f32[1,16,256]{2,1,0:T(8,128)S(1)} %get-tuple-element.21), channel_id=1, source_target_pairs={{0,128},{128,256},{256,384},{384,512},{512,640},{640,768},{768,896... | collective-permute-start | bytes 49160 | tf_op jit(solution)/shard_map/ppermute | solution.py:19
  44.5 3.4 %collective-permute-start.7 = (f32[10,1,256]{2,1,0:T(1,128)S(1)}, f32[10,1,256]{2,1,0:T(1,128)S(1)}, u32[]{:S(2)}, u32[]{:S(2)}) collective-permute-start(f32[10,1,256]{2,1,0:T(1,128)S(1)} %get-tuple-element.11), channel_id=1, source_target_pairs={{0,1},{1,2},{2,3},{3,4},{4,5},{5,6},{6,7},{7,8},{8,9},{9,10},{10,1... | collective-permute-start | bytes 30728 | tf_op jit(solution)/shard_map/ppermute | solution.py:19
  49.8 4.8 %collective-permute-start.13 = (f32[1,8,128]{2,1,0:T(8,128)S(1)}, f32[1,8,128]{2,1,0:T(8,128)S(1)}, u32[]{:S(2)}, u32[]{:S(2)}) collective-permute-start(f32[1,8,128]{2,1,0:T(8,128)S(1)} %broadcast.33), channel_id=1, source_target_pairs={{0,128},{128,256},{256,384},{384,512},{512,640},{640,768},{768,896... | collective-permute-start | bytes 12296 | tf_op jit(solution)/shard_map/ppermute | solution.py:19
  55.6 9.8 %reshape.16 = f32[4,2,8,2,128,2]{5,4,3,2,1,0:T(8,128)} reshape(f32[8,16,256]{2,1,0:T(8,128)S(1)} %convert_element_type.14) | data formatting | bytes 262144 | tf_op jit(solution)/shard_map/reshape | solution.py:48
  65.3 4.0 %reduce_sum.19 = f32[4,8,128]{2,1,0:T(8,128)S(1)} reduce(f32[4,2,8,2,128,2]{5,4,3,2,1,0:T(8,128)} %reshape.16, f32[]{:T(128)} %constant.8.clone.1), dimensions={1,3,5}, to_apply=%region_1.2 | reduce | flops 28672 | bytes 147460 | tf_op jit(solution)/shard_map/reduce_sum | solution.py:48
  71.7 3.6 %collective-permute-start.9 = (f32[1,16,256]{2,1,0:T(8,128)S(1)}, f32[1,16,256]{2,1,0:T(8,128)S(1)}, u32[]{:S(2)}, u32[]{:S(2)}) collective-permute-start(f32[1,16,256]{2,1,0:T(8,128)S(1)} %get-tuple-element.19), channel_id=1, source_target_pairs={{0,128},{128,256},{256,384},{384,512},{512,640},{640,768},{768,896... | collective-permute-start | bytes 49160 | tf_op jit(solution)/shard_map/ppermute | solution.py:19
  75.4 3.8 %collective-permute-start.14 = (f32[6,1,128]{2,1,0:T(1,128)S(1)}, f32[6,1,128]{2,1,0:T(1,128)S(1)}, u32[]{:S(2)}, u32[]{:S(2)}) collective-permute-start(f32[6,1,128]{2,1,0:T(1,128)S(1)} %get-tuple-element.32), channel_id=1, source_target_pairs={{1,0},{2,1},{3,2},{4,3},{5,4},{6,5},{7,6},{8,7},{9,8},{10,9},{11,1... | collective-permute-start | bytes 9224 | tf_op jit(solution)/shard_map/ppermute | solution.py:21
  81.2 5.5 %collective-permute-start.10 = (f32[10,1,256]{2,1,0:T(1,128)S(1)}, f32[10,1,256]{2,1,0:T(1,128)S(1)}, u32[]{:S(2)}, u32[]{:S(2)}) collective-permute-start(f32[10,1,256]{2,1,0:T(1,128)S(1)} %get-tuple-element.10), channel_id=1, source_target_pairs={{1,0},{2,1},{3,2},{4,3},{5,4},{6,5},{7,6},{8,7},{9,8},{10,9},{11,1... | collective-permute-start | bytes 30728 | tf_op jit(solution)/shard_map/ppermute | solution.py:21
  88.7 4.8 %collective-permute-done.11 = f32[10,1,256]{2,1,0:T(1,128)S(1)} collective-permute-done((f32[10,1,256]{2,1,0:T(1,128)S(1)}, f32[10,1,256]{2,1,0:T(1,128)S(1)}, u32[]{:S(2)}, u32[]{:S(2)}) %collective-permute-start.11) | collective-permute-done | bytes 10272 | tf_op jit(solution)/shard_map/ppermute | solution.py:19
  93.9 9.8 %reshape.15 = f32[4,2,8,2,128,2]{5,4,3,2,1,0:T(8,128)} reshape(f32[8,16,256]{2,1,0:T(8,128)S(1)} %fusion.18) | data formatting | bytes 262144 | tf_op jit(solution)/shard_map/reshape | solution.py:48
  103.7 4.0 %reduce_sum.18 = f32[4,8,128]{2,1,0:T(8,128)S(1)} reduce(f32[4,2,8,2,128,2]{5,4,3,2,1,0:T(8,128)} %reshape.15, f32[]{:T(128)} %constant.8.clone.1), dimensions={1,3,5}, to_apply=%region_0.1 | reduce | flops 28672 | bytes 147460 | tf_op jit(solution)/shard_map/reduce_sum | solution.py:48
  110.2 3.2 %collective-permute-start.17 = (f32[1,8,128]{2,1,0:T(8,128)S(1)}, f32[1,8,128]{2,1,0:T(8,128)S(1)}, u32[]{:S(2)}, u32[]{:S(2)}) collective-permute-start(f32[1,8,128]{2,1,0:T(8,128)S(1)} %get-tuple-element.37), channel_id=1, source_target_pairs={{0,128},{128,256},{256,384},{384,512},{512,640},{640,768},{768,896... | collective-permute-start | bytes 12296 | tf_op jit(solution)/shard_map/ppermute | solution.py:19
  116.0 3.4 %collective-permute-start.19 = (f32[6,1,128]{2,1,0:T(1,128)S(1)}, f32[6,1,128]{2,1,0:T(1,128)S(1)}, u32[]{:S(2)}, u32[]{:S(2)}) collective-permute-start(f32[6,1,128]{2,1,0:T(1,128)S(1)} %get-tuple-element.29), channel_id=1, source_target_pairs={{0,1},{1,2},{2,3},{3,4},{4,5},{5,6},{6,7},{7,8},{8,9},{9,10},{10,1... | collective-permute-start | bytes 9224 | tf_op jit(solution)/shard_map/ppermute | solution.py:19
  125.0 4.9 %collective-permute-start.21 = (f32[1,8,128]{2,1,0:T(8,128)S(1)}, f32[1,8,128]{2,1,0:T(8,128)S(1)}, u32[]{:S(2)}, u32[]{:S(2)}) collective-permute-start(f32[1,8,128]{2,1,0:T(8,128)S(1)} %get-tuple-element.35), channel_id=1, source_target_pairs={{0,128},{128,256},{256,384},{384,512},{512,640},{640,768},{768,896... | collective-permute-start | bytes 12296 | tf_op jit(solution)/shard_map/ppermute | solution.py:19
  132.6 3.4 %collective-permute-start.23 = (f32[6,1,128]{2,1,0:T(1,128)S(1)}, f32[6,1,128]{2,1,0:T(1,128)S(1)}, u32[]{:S(2)}, u32[]{:S(2)}) collective-permute-start(f32[6,1,128]{2,1,0:T(1,128)S(1)} %get-tuple-element.27), channel_id=1, source_target_pairs={{0,1},{1,2},{2,3},{3,4},{4,5},{5,6},{6,7},{7,8},{8,9},{9,10},{10,1... | collective-permute-start | bytes 9224 | tf_op jit(solution)/shard_map/ppermute | solution.py:19
  141.2 5.3 %collective-permute-start.25 = (f32[1,8,128]{2,1,0:T(8,128)S(1)}, f32[1,8,128]{2,1,0:T(8,128)S(1)}, u32[]{:S(2)}, u32[]{:S(2)}) collective-permute-start(f32[1,8,128]{2,1,0:T(8,128)S(1)} %get-tuple-element.33), channel_id=1, source_target_pairs={{0,128},{128,256},{256,384},{384,512},{512,640},{640,768},{768,896... | collective-permute-start | bytes 12296 | tf_op jit(solution)/shard_map/ppermute | solution.py:19
  149.2 3.4 %collective-permute-start.27 = (f32[6,1,128]{2,1,0:T(1,128)S(1)}, f32[6,1,128]{2,1,0:T(1,128)S(1)}, u32[]{:S(2)}, u32[]{:S(2)}) collective-permute-start(f32[6,1,128]{2,1,0:T(1,128)S(1)} %get-tuple-element.25), channel_id=1, source_target_pairs={{0,1},{1,2},{2,3},{3,4},{4,5},{5,6},{6,7},{7,8},{8,9},{9,10},{10,1... | collective-permute-start | bytes 9224 | tf_op jit(solution)/shard_map/ppermute | solution.py:19
  158.5 5.3 %collective-permute-start.29 = (f32[1,16,256]{2,1,0:T(8,128)S(1)}, f32[1,16,256]{2,1,0:T(8,128)S(1)}, u32[]{:S(2)}, u32[]{:S(2)}) collective-permute-start(f32[1,16,256]{2,1,0:T(8,128)S(1)} %get-tuple-element.17), channel_id=1, source_target_pairs={{0,128},{128,256},{256,384},{384,512},{512,640},{640,768},{768,896... | collective-permute-start | bytes 49160 | tf_op jit(solution)/shard_map/ppermute | solution.py:19
  166.7 3.4 %collective-permute-start.31 = (f32[10,1,256]{2,1,0:T(1,128)S(1)}, f32[10,1,256]{2,1,0:T(1,128)S(1)}, u32[]{:S(2)}, u32[]{:S(2)}) collective-permute-start(f32[10,1,256]{2,1,0:T(1,128)S(1)} %get-tuple-element.7), channel_id=1, source_target_pairs={{0,1},{1,2},{2,3},{3,4},{4,5},{5,6},{6,7},{7,8},{8,9},{9,10},{10,1... | collective-permute-start | bytes 30728 | tf_op jit(solution)/shard_map/ppermute | solution.py:19
  175.5 5.4 %collective-permute-start.33 = (f32[1,16,256]{2,1,0:T(8,128)S(1)}, f32[1,16,256]{2,1,0:T(8,128)S(1)}, u32[]{:S(2)}, u32[]{:S(2)}) collective-permute-start(f32[1,16,256]{2,1,0:T(8,128)S(1)} %get-tuple-element.15), channel_id=1, source_target_pairs={{0,128},{128,256},{256,384},{384,512},{512,640},{640,768},{768,896... | collective-permute-start | bytes 49160 | tf_op jit(solution)/shard_map/ppermute | solution.py:19
  183.7 3.4 %collective-permute-start.35 = (f32[10,1,256]{2,1,0:T(1,128)S(1)}, f32[10,1,256]{2,1,0:T(1,128)S(1)}, u32[]{:S(2)}, u32[]{:S(2)}) collective-permute-start(f32[10,1,256]{2,1,0:T(1,128)S(1)} %get-tuple-element.5), channel_id=1, source_target_pairs={{0,1},{1,2},{2,3},{3,4},{4,5},{5,6},{6,7},{7,8},{8,9},{9,10},{10,1... | collective-permute-start | bytes 30728 | tf_op jit(solution)/shard_map/ppermute | solution.py:19
  (104 shorter events, 65.7 us)
Async XLA Ops:
  9.5 20.5 %collective-permute-start.2 = (f32[10,1,256]{2,1,0:T(1,128)S(1)}, f32[10,1,256]{2,1,0:T(1,128)S(1)}, u32[]{:S(2)}, u32[]{:S(2)}) collective-permute-start(f32[10,1,256]{2,1,0:T(1,128)S(1)} %get-tuple-element.14), channel_id=1, source_target_pairs={{1,0},{2,1},{3,2},{4,3},{5,4},{6,5},{7,6},{8,7},{9,8},{10,9},{11,1... | collective-permute-start | bytes 30728 | tf_op jit(solution)/shard_map/ppermute | solution.py:21
  28.1 6.5 %collective-permute-start.3 = (f32[10,1,256]{2,1,0:T(1,128)S(1)}, f32[10,1,256]{2,1,0:T(1,128)S(1)}, u32[]{:S(2)}, u32[]{:S(2)}) collective-permute-start(f32[10,1,256]{2,1,0:T(1,128)S(1)} %get-tuple-element.13), channel_id=1, source_target_pairs={{0,1},{1,2},{2,3},{3,4},{4,5},{5,6},{6,7},{7,8},{8,9},{9,10},{10,1... | collective-permute-start | bytes 30728 | tf_op jit(solution)/shard_map/ppermute | solution.py:19
  42.6 26.8 %collective-permute-start.6 = (f32[10,1,256]{2,1,0:T(1,128)S(1)}, f32[10,1,256]{2,1,0:T(1,128)S(1)}, u32[]{:S(2)}, u32[]{:S(2)}) collective-permute-start(f32[10,1,256]{2,1,0:T(1,128)S(1)} %get-tuple-element.12), channel_id=1, source_target_pairs={{1,0},{2,1},{3,2},{4,3},{5,4},{6,5},{7,6},{8,7},{9,8},{10,9},{11,1... | collective-permute-start | bytes 30728 | tf_op jit(solution)/shard_map/ppermute | solution.py:21
  44.5 24.9 %collective-permute-start.7 = (f32[10,1,256]{2,1,0:T(1,128)S(1)}, f32[10,1,256]{2,1,0:T(1,128)S(1)}, u32[]{:S(2)}, u32[]{:S(2)}) collective-permute-start(f32[10,1,256]{2,1,0:T(1,128)S(1)} %get-tuple-element.11), channel_id=1, source_target_pairs={{0,1},{1,2},{2,3},{3,4},{4,5},{5,6},{6,7},{7,8},{8,9},{9,10},{10,1... | collective-permute-start | bytes 30728 | tf_op jit(solution)/shard_map/ppermute | solution.py:19
  47.9 27.5 %collective-permute-start.12 = (f32[1,8,128]{2,1,0:T(8,128)S(1)}, f32[1,8,128]{2,1,0:T(8,128)S(1)}, u32[]{:S(2)}, u32[]{:S(2)}) collective-permute-start(f32[1,8,128]{2,1,0:T(8,128)S(1)} %broadcast.33), channel_id=1, source_target_pairs={{128,0},{256,128},{384,256},{512,384},{640,512},{768,640},{896,768... | collective-permute-start | bytes 12296 | tf_op jit(solution)/shard_map/ppermute | solution.py:21
  49.8 25.6 %collective-permute-start.13 = (f32[1,8,128]{2,1,0:T(8,128)S(1)}, f32[1,8,128]{2,1,0:T(8,128)S(1)}, u32[]{:S(2)}, u32[]{:S(2)}) collective-permute-start(f32[1,8,128]{2,1,0:T(8,128)S(1)} %broadcast.33), channel_id=1, source_target_pairs={{0,128},{128,256},{256,384},{384,512},{512,640},{640,768},{768,896... | collective-permute-start | bytes 12296 | tf_op jit(solution)/shard_map/ppermute | solution.py:19
  69.8 11.3 %collective-permute-start.8 = (f32[1,16,256]{2,1,0:T(8,128)S(1)}, f32[1,16,256]{2,1,0:T(8,128)S(1)}, u32[]{:S(2)}, u32[]{:S(2)}) collective-permute-start(f32[1,16,256]{2,1,0:T(8,128)S(1)} %get-tuple-element.20), channel_id=1, source_target_pairs={{128,0},{256,128},{384,256},{512,384},{640,512},{768,640},{896,768... | collective-permute-start | bytes 49160 | tf_op jit(solution)/shard_map/ppermute | solution.py:21
  71.7 9.4 %collective-permute-start.9 = (f32[1,16,256]{2,1,0:T(8,128)S(1)}, f32[1,16,256]{2,1,0:T(8,128)S(1)}, u32[]{:S(2)}, u32[]{:S(2)}) collective-permute-start(f32[1,16,256]{2,1,0:T(8,128)S(1)} %get-tuple-element.19), channel_id=1, source_target_pairs={{0,128},{128,256},{256,384},{384,512},{512,640},{640,768},{768,896... | collective-permute-start | bytes 49160 | tf_op jit(solution)/shard_map/ppermute | solution.py:19
  75.4 13.2 %collective-permute-start.14 = (f32[6,1,128]{2,1,0:T(1,128)S(1)}, f32[6,1,128]{2,1,0:T(1,128)S(1)}, u32[]{:S(2)}, u32[]{:S(2)}) collective-permute-start(f32[6,1,128]{2,1,0:T(1,128)S(1)} %get-tuple-element.32), channel_id=1, source_target_pairs={{1,0},{2,1},{3,2},{4,3},{5,4},{6,5},{7,6},{8,7},{9,8},{10,9},{11,1... | collective-permute-start | bytes 9224 | tf_op jit(solution)/shard_map/ppermute | solution.py:21
  79.2 9.4 %collective-permute-start.15 = (f32[6,1,128]{2,1,0:T(1,128)S(1)}, f32[6,1,128]{2,1,0:T(1,128)S(1)}, u32[]{:S(2)}, u32[]{:S(2)}) collective-permute-start(f32[6,1,128]{2,1,0:T(1,128)S(1)} %get-tuple-element.31), channel_id=1, source_target_pairs={{0,1},{1,2},{2,3},{3,4},{4,5},{5,6},{6,7},{7,8},{8,9},{9,10},{10,1... | collective-permute-start | bytes 9224 | tf_op jit(solution)/shard_map/ppermute | solution.py:19
  81.2 7.6 %collective-permute-start.10 = (f32[10,1,256]{2,1,0:T(1,128)S(1)}, f32[10,1,256]{2,1,0:T(1,128)S(1)}, u32[]{:S(2)}, u32[]{:S(2)}) collective-permute-start(f32[10,1,256]{2,1,0:T(1,128)S(1)} %get-tuple-element.10), channel_id=1, source_target_pairs={{1,0},{2,1},{3,2},{4,3},{5,4},{6,5},{7,6},{8,7},{9,8},{10,9},{11,1... | collective-permute-start | bytes 30728 | tf_op jit(solution)/shard_map/ppermute | solution.py:21
  86.7 6.9 %collective-permute-start.11 = (f32[10,1,256]{2,1,0:T(1,128)S(1)}, f32[10,1,256]{2,1,0:T(1,128)S(1)}, u32[]{:S(2)}, u32[]{:S(2)}) collective-permute-start(f32[10,1,256]{2,1,0:T(1,128)S(1)} %get-tuple-element.9), channel_id=1, source_target_pairs={{0,1},{1,2},{2,3},{3,4},{4,5},{5,6},{6,7},{7,8},{8,9},{9,10},{10,1... | collective-permute-start | bytes 30728 | tf_op jit(solution)/shard_map/ppermute | solution.py:19
  116.0 6.5 %collective-permute-start.19 = (f32[6,1,128]{2,1,0:T(1,128)S(1)}, f32[6,1,128]{2,1,0:T(1,128)S(1)}, u32[]{:S(2)}, u32[]{:S(2)}) collective-permute-start(f32[6,1,128]{2,1,0:T(1,128)S(1)} %get-tuple-element.29), channel_id=1, source_target_pairs={{0,1},{1,2},{2,3},{3,4},{4,5},{5,6},{6,7},{7,8},{8,9},{9,10},{10,1... | collective-permute-start | bytes 9224 | tf_op jit(solution)/shard_map/ppermute | solution.py:19
  122.7 7.2 %collective-permute-start.20 = (f32[1,8,128]{2,1,0:T(8,128)S(1)}, f32[1,8,128]{2,1,0:T(8,128)S(1)}, u32[]{:S(2)}, u32[]{:S(2)}) collective-permute-start(f32[1,8,128]{2,1,0:T(8,128)S(1)} %get-tuple-element.36), channel_id=1, source_target_pairs={{128,0},{256,128},{384,256},{512,384},{640,512},{768,640},{896,768... | collective-permute-start | bytes 12296 | tf_op jit(solution)/shard_map/ppermute | solution.py:21
  132.6 6.5 %collective-permute-start.23 = (f32[6,1,128]{2,1,0:T(1,128)S(1)}, f32[6,1,128]{2,1,0:T(1,128)S(1)}, u32[]{:S(2)}, u32[]{:S(2)}) collective-permute-start(f32[6,1,128]{2,1,0:T(1,128)S(1)} %get-tuple-element.27), channel_id=1, source_target_pairs={{0,1},{1,2},{2,3},{3,4},{4,5},{5,6},{6,7},{7,8},{8,9},{9,10},{10,1... | collective-permute-start | bytes 9224 | tf_op jit(solution)/shard_map/ppermute | solution.py:19
  139.3 7.3 %collective-permute-start.24 = (f32[1,8,128]{2,1,0:T(8,128)S(1)}, f32[1,8,128]{2,1,0:T(8,128)S(1)}, u32[]{:S(2)}, u32[]{:S(2)}) collective-permute-start(f32[1,8,128]{2,1,0:T(8,128)S(1)} %get-tuple-element.34), channel_id=1, source_target_pairs={{128,0},{256,128},{384,256},{512,384},{640,512},{768,640},{896,768... | collective-permute-start | bytes 12296 | tf_op jit(solution)/shard_map/ppermute | solution.py:21
  141.2 6.1 %collective-permute-start.25 = (f32[1,8,128]{2,1,0:T(8,128)S(1)}, f32[1,8,128]{2,1,0:T(8,128)S(1)}, u32[]{:S(2)}, u32[]{:S(2)}) collective-permute-start(f32[1,8,128]{2,1,0:T(8,128)S(1)} %get-tuple-element.33), channel_id=1, source_target_pairs={{0,128},{128,256},{256,384},{384,512},{512,640},{640,768},{768,896... | collective-permute-start | bytes 12296 | tf_op jit(solution)/shard_map/ppermute | solution.py:19
  149.2 6.5 %collective-permute-start.27 = (f32[6,1,128]{2,1,0:T(1,128)S(1)}, f32[6,1,128]{2,1,0:T(1,128)S(1)}, u32[]{:S(2)}, u32[]{:S(2)}) collective-permute-start(f32[6,1,128]{2,1,0:T(1,128)S(1)} %get-tuple-element.25), channel_id=1, source_target_pairs={{0,1},{1,2},{2,3},{3,4},{4,5},{5,6},{6,7},{7,8},{8,9},{9,10},{10,1... | collective-permute-start | bytes 9224 | tf_op jit(solution)/shard_map/ppermute | solution.py:19
  156.6 7.3 %collective-permute-start.28 = (f32[1,16,256]{2,1,0:T(8,128)S(1)}, f32[1,16,256]{2,1,0:T(8,128)S(1)}, u32[]{:S(2)}, u32[]{:S(2)}) collective-permute-start(f32[1,16,256]{2,1,0:T(8,128)S(1)} %get-tuple-element.18), channel_id=1, source_target_pairs={{128,0},{256,128},{384,256},{512,384},{640,512},{768,640},{896,768... | collective-permute-start | bytes 49160 | tf_op jit(solution)/shard_map/ppermute | solution.py:21
  158.5 6.2 %collective-permute-start.29 = (f32[1,16,256]{2,1,0:T(8,128)S(1)}, f32[1,16,256]{2,1,0:T(8,128)S(1)}, u32[]{:S(2)}, u32[]{:S(2)}) collective-permute-start(f32[1,16,256]{2,1,0:T(8,128)S(1)} %get-tuple-element.17), channel_id=1, source_target_pairs={{0,128},{128,256},{256,384},{384,512},{512,640},{640,768},{768,896... | collective-permute-start | bytes 49160 | tf_op jit(solution)/shard_map/ppermute | solution.py:19
  166.7 6.5 %collective-permute-start.31 = (f32[10,1,256]{2,1,0:T(1,128)S(1)}, f32[10,1,256]{2,1,0:T(1,128)S(1)}, u32[]{:S(2)}, u32[]{:S(2)}) collective-permute-start(f32[10,1,256]{2,1,0:T(1,128)S(1)} %get-tuple-element.7), channel_id=1, source_target_pairs={{0,1},{1,2},{2,3},{3,4},{4,5},{5,6},{6,7},{7,8},{8,9},{9,10},{10,1... | collective-permute-start | bytes 30728 | tf_op jit(solution)/shard_map/ppermute | solution.py:19
  173.6 7.3 %collective-permute-start.32 = (f32[1,16,256]{2,1,0:T(8,128)S(1)}, f32[1,16,256]{2,1,0:T(8,128)S(1)}, u32[]{:S(2)}, u32[]{:S(2)}) collective-permute-start(f32[1,16,256]{2,1,0:T(8,128)S(1)} %get-tuple-element.16), channel_id=1, source_target_pairs={{128,0},{256,128},{384,256},{512,384},{640,512},{768,640},{896,768... | collective-permute-start | bytes 49160 | tf_op jit(solution)/shard_map/ppermute | solution.py:21
  175.5 6.2 %collective-permute-start.33 = (f32[1,16,256]{2,1,0:T(8,128)S(1)}, f32[1,16,256]{2,1,0:T(8,128)S(1)}, u32[]{:S(2)}, u32[]{:S(2)}) collective-permute-start(f32[1,16,256]{2,1,0:T(8,128)S(1)} %get-tuple-element.15), channel_id=1, source_target_pairs={{0,128},{128,256},{256,384},{384,512},{512,640},{640,768},{768,896... | collective-permute-start | bytes 49160 | tf_op jit(solution)/shard_map/ppermute | solution.py:19
  183.7 6.5 %collective-permute-start.35 = (f32[10,1,256]{2,1,0:T(1,128)S(1)}, f32[10,1,256]{2,1,0:T(1,128)S(1)}, u32[]{:S(2)}, u32[]{:S(2)}) collective-permute-start(f32[10,1,256]{2,1,0:T(1,128)S(1)} %get-tuple-element.5), channel_id=1, source_target_pairs={{0,1},{1,2},{2,3},{3,4},{4,5},{5,6},{6,7},{7,8},{8,9},{9,10},{10,1... | collective-permute-start | bytes 30728 | tf_op jit(solution)/shard_map/ppermute | solution.py:19
  (14 other events, 90.6 us)
where the time goes:
time: 194 us; the launch traced here: 191 us
  starting transfers between devices  123 us (63%)
  waiting for transfers between devices  31.8 us (16%)
  local copies, waits for them, and re-layouts  22 us (11%)
  other arithmetic  13.5 us (7%)
    ppermute x18, starting transfers between devices, with_halo(): lax.ppermute(tail, axis, [(i, (i + 1) % count) for i in range(ends)])  65.8 us
    ppermute x18, starting transfers between devices, with_halo(): lax.ppermute(head, axis, [((i + 1) % count, i) for i in range(ends)])  57.4 us
    ppermute x18, waiting for transfers between devices, with_halo(): lax.ppermute(tail, axis, [(i, (i + 1) % count) for i in range(ends)])  29.6 us
    reshape x2, local copies, waits for them, and re-layouts, block_sum(): return field.reshape(nx // 2, 2, ny // 2, 2, nz // 2, 2).sum(axis=(1, 3, 5))  19.6 us
    reduce_sum x2, other arithmetic, block_sum(): return field.reshape(nx // 2, 2, ny // 2, 2, nz // 2, 2).sum(axis=(1, 3, 5))  8.04 us
  transfers between devices with their start and end apart: 36, of which 14 were waited for; matrix products, arithmetic and copies ran while one was open for 8% of the time, Pallas kernels for 0%

commit v1 on v0

v1 whole, which is shorter than its diff:
```python
import jax
import jax.numpy as jnp
from jax import lax
from jax.sharding import PartitionSpec as P
from jax.experimental import pallas as pl
from jax.experimental.pallas import tpu as pltpu

OMEGA = 0.8
KEEP = 1.0 - OMEGA
VM = pl.BlockSpec(memory_space=pltpu.VMEM)
F32 = jnp.float32
BX, BY, NZ = 8, 16, 256
CX, CY, CZ = 4, 8, 128


def call(kernel, outs, *args, scratch=(), hbm_out=False):
    make = jax.ShapeDtypeStruct if hbm_out else pltpu.VMEM
    return pl.pallas_call(
        kernel,
        out_shape=[make(s, F32) for s in outs],
        in_specs=[VM] * len(args),
        out_specs=[VM] * len(outs),
        scratch_shapes=[pltpu.VMEM(s, F32) for s in scratch],
        compiler_params=pltpu.CompilerParams(vmem_limit_bytes=8 * 2**20),
    )(*args)


def beside_z(v):
    lane = lax.broadcasted_iota(jnp.int32, v.shape, 1)
    last = v.shape[1] - 1
    below = jnp.where(lane == 0, 0.0, pltpu.roll(v, 1, 1))
    above = jnp.where(lane == last, 0.0, pltpu.roll(v, last, 1))
    return below + above


def shift_y(v, low, high):
    row = lax.broadcasted_iota(jnp.int32, v.shape, 0)
    last = v.shape[0] - 1
    below = jnp.where(row == 0, low, pltpu.roll(v, 1, 0))
    above = jnp.where(row == last, high, pltpu.roll(v, last, 0))
    return below, above


def beside_y(v, low, high):
    below, above = shift_y(v, low, high)
    return below + above


def slab(ref, k, rows=BY):
    return ref[k * rows : (k + 1) * rows, :]


def row(ref, k):
    return ref[k : k + 1, :]


def halved(n, m):
    a = lax.broadcasted_iota(jnp.int32, (n, m), 0)
    b = lax.broadcasted_iota(jnp.int32, (n, m), 1)
    return jnp.where((a // 2 == b) if n > m else (a == b // 2), 1.0, 0.0).astype(F32)


def diag_of(n):
    return 6.0 + 0.25 * n.astype(F32)


def pack_x_kernel(g, b, n, lo, hi):
    for out, layers in ((lo, (0, 1, 2)), (hi, (7, 6, 5))):
        for k in range(3):
            out[k * BY : (k + 1) * BY, :] = g[layers[k]]
        for k in range(2):
            out[(3 + k) * BY : (4 + k) * BY, :] = OMEGA / diag_of(n[layers[k]])
            out[(5 + k) * BY : (6 + k) * BY, :] = b[layers[k]]


class Wide:
    def __init__(self, g, b, n, left, right):
        self.g, self.b, self.n, self.left, self.right = g, b, n, left, right
        self.ws = {}

    def _side(self, x):
        return (self.left, -1 - x) if x < 0 else (self.right, x - BX)

    def guess(self, x):
        if 0 <= x < BX:
            return self.g[x]
        ref, k = self._side(x)
        return slab(ref, k)

    def w(self, x):
        if x not in self.ws:
            if 0 <= x < BX:
                self.ws[x] = OMEGA / diag_of(self.n[x])
            else:
                ref, k = self._side(x)
                self.ws[x] = slab(ref, 3 + k)
        return self.ws[x]

    def rhs(self, x):
        if 0 <= x < BX:
            return self.b[x]
        ref, k = self._side(x)
        return slab(ref, 5 + k)


Y_G, Y_P, Y_W, Y_Q = 0, 12, 22, 32
Y_ROWS = 40


def pack_y_kernel(g, b, n, left, right, lo, hi, f1z):
    a = Wide(g, b, n, left, right)
    for x in range(-2, 10):
        here = a.guess(x)
        f = KEEP * here + a.w(x) * (
            a.rhs(x) + a.guess(x - 1) + a.guess(x + 1) + beside_z(here) + beside_y(here, 0.0, 0.0)
        )
        f1z[(x + 2) * BY : (x + 3) * BY, :] = f
        for out, y, inner in ((lo, 0, 1), (hi, BY - 1, BY - 2)):
            k = Y_G + x + 2
            out[k : k + 1, :] = here[y : y + 1]
            if -1 <= x <= 8:
                k = Y_P + x + 1
                out[k : k + 1, :] = f[y : y + 1]
                k = Y_W + x + 1
                out[k : k + 1, :] = a.w(x)[y : y + 1]
            if 0 <= x <= 7:
                k = Y_Q + x
                out[k : k + 1, :] = a.w(x)[y : y + 1] * (a.rhs(x)[y : y + 1] + f[inner : inner + 1])


X2_ROWS = 3 * BY


def middle_kernel(g, b, n, left, right, f1z, low, high, f2, f2low, f2high, c1, wc, lo, hi, col, line, sums):
    a = Wide(g, b, n, left, right)
    rows = lax.broadcasted_iota(jnp.int32, (BY, NZ), 0)
    f1 = {}
    for x in range(-2, 10):
        k = Y_G + x + 2
        beyond = jnp.where(rows == 0, row(low, k), jnp.where(rows == BY - 1, row(high, k), 0.0))
        f1[x] = slab(f1z, x + 2) + a.w(x) * beyond
    for s, (side, y, out) in enumerate(((low, 0, f2low), (high, BY - 1, f2high))):
        for x in range(-1, 9):
            col[x + 1 : x + 2, :] = a.guess(x)[y : y + 1]
        line[s, 0:10, :] = side[Y_P : Y_P + 10, :] + side[Y_W : Y_W + 10, :] * col[0:10, :]
        for x in range(0, 8):
            col[x : x + 1, :] = f1[x][y : y + 1]
        mid = line[s, 1:9, :]
        out[...] = (
            KEEP * mid
            + side[Y_Q : Y_Q + 8, :]
            + side[Y_W + 1 : Y_W + 9, :]
            * (line[s, 0:8, :] + line[s, 2:10, :] + beside_z(mid) + col[0:8, :])
        )
    sec = {}
    for x in range(-1, 9):
        f = f1[x]
        sec[x] = KEEP * f + a.w(x) * (
            a.rhs(x)
            + f1[x - 1]
            + f1[x + 1]
            + beside_z(f)
            + beside_y(f, line[0, x + 1 : x + 2, :], line[1, x + 1 : x + 2, :])
        )
        f2[(x + 1) * BY : (x + 2) * BY, :] = sec[x]
    lo[2 * BY :, :] = sec[1]
    hi[2 * BY :, :] = sec[6]
    pairs, points = [], []
    for x in range(0, 8):
        f = sec[x]
        r = (
            a.rhs(x)
            - diag_of(n[x]) * f
            + sec[x - 1]
            + sec[x + 1]
            + beside_z(f)
            + beside_y(f, row(f2low, x), row(f2high, x))
        )
        if x % 2:
            pairs[-1] = pairs[-1] + r
            points[-1] = points[-1] + n[x].astype(F32)
        else:
            pairs.append(r)
            points.append(n[x].astype(F32))
    sums[...] = lax.dot_general(
        jnp.concatenate(pairs + points, axis=0),
        halved(NZ, CZ),
        (((1,), (0,)), ((), ())),
        precision=lax.Precision.HIGHEST,
        preferred_element_type=F32,
    )
    for x in range(CX):
        at = x * BY
        total = sums[pl.ds(at, CY, stride=2), :] + sums[pl.ds(at + 1, CY, stride=2), :]
        at = (CX + x) * BY
        count = sums[pl.ds(at, CY, stride=2), :] + sums[pl.ds(at + 1, CY, stride=2), :]
        weight = OMEGA / (6.0 + count / 8.0)
        first = weight * (0.5 * total)
        c1[x * CY : (x + 1) * CY, :] = first
        wc[x * CY : (x + 1) * CY, :] = weight
        for out, k in ((lo, x), (hi, CX - 1 - x)):
            out[k * CY : (k + 1) * CY, 0:CZ] = first
            out[k * CY : (k + 1) * CY, CZ:] = weight


class Coarse:
    def __init__(self, c1, wc, left, right):
        self.c1, self.wc, self.left, self.right = c1, wc, left, right

    def _get(self, x, own, lanes):
        if 0 <= x < CX:
            return slab(own, x, CY)
        ref, k = (self.left, -1 - x) if x < 0 else (self.right, x - CX)
        return ref[k * CY : (k + 1) * CY, lanes]

    def first(self, x):
        return self._get(x, self.c1, slice(0, CZ))

    def w(self, x):
        return self._get(x, self.wc, slice(CZ, 2 * CZ))


Z_C, Z_P, Z_W, Z_Q, Z_R, Z_V, Z_S, Z_K = 0, 10, 20, 30, 38, 44, 50, 66
Z_ROWS = 72


def pack_c_kernel(b, n, f2, c1, wc, left, right, lo, hi, c2z):
    a = Coarse(c1, wc, left, right)
    second = {}
    for x in range(-3, 7):
        c, w = a.first(x), a.w(x)
        second[x] = (1.0 + KEEP) * c + w * (
            a.first(x - 1) + a.first(x + 1) + beside_z(c) + beside_y(c, 0.0, 0.0)
        )
        c2z[(x + 3) * CY : (x + 4) * CY, :] = second[x]
        for out, y in ((lo, 0), (hi, CY - 1)):
            for base, v in ((Z_C, c), (Z_P, second[x]), (Z_W, w)):
                k = base + x + 3
                out[k : k + 1, :] = v[y : y + 1]
    for x in range(-2, 6):
        s, c, w = second[x], a.first(x), a.w(x)
        below, above = shift_y(s, 0.0, 0.0)
        inner = {0: above, 1: below}
        for side, (out, y, y2) in enumerate(((lo, 0, 1), (hi, CY - 1, CY - 2))):
            k = Z_Q + x + 2
            out[k : k + 1, :] = (c + w * inner[side])[y : y + 1]
        if -1 <= x <= 4:
            part = KEEP * s + c + w * (second[x - 1] + second[x + 1] + beside_z(s))
            for side, (out, y, y2) in enumerate(((lo, 0, 1), (hi, CY - 1, CY - 2))):
                k = Z_R + x + 1
                out[k : k + 1, :] = (part + w * inner[side])[y2 : y2 + 1]
                k = Z_V + x + 1
                out[k : k + 1, :] = w[y2 : y2 + 1]
    for out, y, inner in ((lo, 0, 1), (hi, BY - 1, BY - 2)):
        for x in range(BX):
            at = (x + 1) * BY
            w = OMEGA / diag_of(n[x][y : y + 1])
            v = w * (b[x][y : y + 1] + f2[at + inner : at + inner + 1, :])
            for half in range(2):
                k = Z_S + 2 * x + half
                out[k : k + 1, :] = v[:, half * CZ : (half + 1) * CZ]
        for j, x in enumerate((-1, 8)):
            at = (x + 1) * BY + y
            v = f2[at : at + 1, :]
            for half in range(2):
                k = Z_K + 2 * j + half
                out[k : k + 1, :] = v[:, half * CZ : (half + 1) * CZ]


def last_kernel(
    b, n, left, right, low, high, f2, f2low, f2high, c1, wc, cleft, cright, c2z, clow, chigh,
    out, col, line, line3, fine, corr, col2, s1, gline, g1line,
):
    a = Coarse(c1, wc, cleft, cright)
    wide = Wide(None, b, n, left, right)
    crow = lax.broadcasted_iota(jnp.int32, (CY, CZ), 0)
    c2 = {}
    for x in range(-3, 7):
        k = Z_C + x + 3
        beyond = jnp.where(crow == 0, row(clow, k), jnp.where(crow == CY - 1, row(chigh, k), 0.0))
        c2[x] = slab(c2z, x + 3, CY) + a.w(x) * beyond
    sides = ((clow, 0), (chigh, CY - 1))
    for s, (side, y) in enumerate(sides):
        for x in range(-3, 7):
            col[x + 3 : x + 4, :] = a.first(x)[y : y + 1]
        line[s, 0:10, :] = side[Z_P : Z_P + 10, :] + side[Z_W : Z_W + 10, :] * col[0:10, :]
        for x in range(-2, 6):
            col[x + 2 : x + 3, :] = c2[x][y : y + 1]
        mid = line[s, 1:9, :]
        line3[s, 0:8, :] = (
            KEEP * mid
            + side[Z_Q : Z_Q + 8, :]
            + side[Z_W + 1 : Z_W + 9, :]
            * (line[s, 0:8, :] + line[s, 2:10, :] + beside_z(mid) + col[0:8, :])
        )
    c3 = {}
    for x in range(-2, 6):
        c = c2[x]
        c3[x] = KEEP * c + a.first(x) + a.w(x) * (
            c2[x - 1]
            + c2[x + 1]
            + beside_z(c)
            + beside_y(c, line[0, x + 3 : x + 4, :], line[1, x + 3 : x + 4, :])
        )
    for x in range(-1, 5):
        c = c3[x]
        c4 = KEEP * c + a.first(x) + a.w(x) * (
            c3[x - 1]
            + c3[x + 1]
            + beside_z(c)
            + beside_y(c, line3[0, x + 2 : x + 3, :], line3[1, x + 2 : x + 3, :])
        )
        fine[pl.ds((x + 1) * BY, CY, stride=2), :] = c4
        fine[pl.ds((x + 1) * BY + 1, CY, stride=2), :] = c4
    for s, (side, y) in enumerate(sides):
        for x in range(-1, 5):
            col[x + 1 : x + 2, :] = c3[x][y : y + 1]
        mid = line3[s, 1:7, :]
        third = side[Z_R : Z_R + 6, :] + side[Z_V : Z_V + 6, :] * line[s, 2:8, :]
        fine[6 * BY + 8 * s : 6 * BY + 8 * s + 6, :] = (
            KEEP * mid
            + side[Z_C + 2 : Z_C + 8, :]
            + side[Z_W + 2 : Z_W + 8, :]
            * (line3[s, 0:6, :] + line3[s, 2:8, :] + beside_z(mid) + third + col[0:6, :])
        )
        fine[6 * BY + 8 * s + 6 : 6 * BY + 8 * s + 8, :] = jnp.zeros((2, CZ), F32)
    corr[...] = lax.dot_general(
        fine[...],
        halved(CZ, NZ),
        (((1,), (0,)), ((), ())),
        precision=lax.Precision.HIGHEST,
        preferred_element_type=F32,
    )
    g0 = {}
    for x in range(-2, 10):
        if x == -2:
            f = slab(cleft, 2)
        elif x == 9:
            f = slab(cright, 2)
        else:
            f = slab(f2, x + 1)
        g0[x] = f + slab(corr, (x + 2) // 2)
    for s, (cside, side, y, f2side) in enumerate(((clow, low, 0, f2low), (chigh, high, BY - 1, f2high))):
        base = 6 * BY + 8 * s
        for x in range(-1, 9):
            k = base + (x + 2) // 2
            col2[x + 1 : x + 2, :] = corr[k : k + 1, :]
        gline[s, 1:9, :] = f2side[...] + col2[1:9, :]
        for j, x in enumerate((-1, 8)):
            k = Z_K + 2 * j
            gline[s, x + 1 : x + 2, 0:CZ] = row(cside, k) + col2[x + 1 : x + 2, 0:CZ]
            gline[s, x + 1 : x + 2, CZ:] = row(cside, k + 1) + col2[x + 1 : x + 2, CZ:]
        for x in range(BX):
            k = Z_S + 2 * x
            s1[x : x + 1, 0:CZ] = row(cside, k)
            s1[x : x + 1, CZ:] = row(cside, k + 1)
        moved = col2[1:9, :]
        for x in range(BX):
            col2[x : x + 1, :] = g0[x][y : y + 1]
        mid = gline[s, 1:9, :]
        g1line[s, 0:8, :] = (
            KEEP * mid
            + s1[0:8, :]
            + side[Y_W + 1 : Y_W + 9, :]
            * (moved + gline[s, 0:8, :] + gline[s, 2:10, :] + beside_z(mid) + col2[0:8, :])
        )
    g1 = {}
    for x in range(-1, 9):
        f = g0[x]
        g1[x] = KEEP * f + wide.w(x) * (
            wide.rhs(x)
            + g0[x - 1]
            + g0[x + 1]
            + beside_z(f)
            + beside_y(f, gline[0, x + 1 : x + 2, :], gline[1, x + 1 : x + 2, :])
        )
    for x in range(BX):
        f = g1[x]
        out[x] = KEEP * f + wide.w(x) * (
            wide.rhs(x)
            + g1[x - 1]
            + g1[x + 1]
            + beside_z(f)
            + beside_y(f, g1line[0, x : x + 1, :], g1line[1, x : x + 1, :])
        )


def exchange(to_low, to_high, axis):
    n = lax.axis_size(axis)
    from_low = lax.ppermute(to_high, axis, [(i, i + 1) for i in range(n - 1)])
    from_high = lax.ppermute(to_low, axis, [(i + 1, i) for i in range(n - 1)])
    return from_low, from_high


def body(g, b, n):
    lo, hi = call(pack_x_kernel, [(7 * BY, NZ)] * 2, g, b, n)
    left, right = exchange(lo, hi, "group")
    lo, hi, f1z = call(pack_y_kernel, [(Y_ROWS, NZ)] * 2 + [(12 * BY, NZ)], g, b, n, left, right)
    low, high = exchange(lo, hi, "dev")
    f2, f2low, f2high, c1, wc, lo, hi = call(
        middle_kernel,
        [(10 * BY, NZ), (BX, NZ), (BX, NZ), (CX * CY, CZ), (CX * CY, CZ), (X2_ROWS, NZ), (X2_ROWS, NZ)],
        g, b, n, left, right, f1z, low, high,
        scratch=[(16, NZ), (2, 16, NZ), (8 * BY, CZ)],
    )
    cleft, cright = exchange(lo, hi, "group")
    lo, hi, c2z = call(
        pack_c_kernel, [(Z_ROWS, CZ)] * 2 + [(10 * CY, CZ)], b, n, f2, c1, wc, cleft, cright
    )
    clow, chigh = exchange(lo, hi, "dev")
    (out,) = call(
        last_kernel,
        [(BX, BY, NZ)],
        b, n, left, right, low, high, f2, f2low, f2high, c1, wc, cleft, cright, c2z, clow, chigh,
        scratch=[
            (16, CZ), (2, 16, CZ), (2, 8, CZ), (6 * BY + 16, CZ), (6 * BY + 16, NZ), (16, NZ), (8, NZ), (2, 16, NZ), (2, 8, NZ),
        ],
        hbm_out=True,
    )
    return out


def solution(mesh):
    s = P("group", "dev", None)
    return jax.shard_map(body, mesh=mesh, in_specs=(s, s, s), out_specs=s, check_vma=False)
```

time: 194 us -> 53.9 us (0.28); the launches traced: 191 us -> 53.5 us
  starting transfers between devices: 123 us -> 38.7 us
  waiting for transfers between devices: 31.8 us -> 9.75 us
  local copies, waits for them, and re-layouts: 22 us -> 2.72 us
  other arithmetic: 13.5 us -> 0 us
  Pallas kernels: 0 us -> 2.29 us
    ppermute x36 -> x8, starting transfers between devices: 123 us -> 38.7 us  [the longest x4 26.9 us: exchange(): from_high = lax.ppermute(to_low, axis, [(i + 1, i) for i in range(n - 1)])]
    ppermute x36 -> x8, waiting for transfers between devices: 31.8 us -> 9.75 us  [the longest x4 9.74 us: exchange(): from_high = lax.ppermute(to_low, axis, [(i + 1, i) for i in range(n - 1)])]
    reshape x4 -> x0, local copies, waits for them, and re-layouts: 20.2 us -> none  [the longest x2 19.6 us: block_sum(): return field.reshape(nx // 2, 2, ny // 2, 2, nz // 2, 2).sum(axis=(1, 3, 5))]
    reduce_sum x2 -> x0, other arithmetic: 8.04 us -> none  [block_sum(): return field.reshape(nx // 2, 2, ny // 2, 2, nz // 2, 2).sum(axis=(1, 3, 5))]
    add x8 -> x0, other arithmetic: 2.64 us -> none  [the longest x4 2.36 us: body(): field + 0.8 * (divergence - fine_apply(field, fine_diag)) / fine_diag]
    pallas_call x0 -> x5, Pallas kernels: none -> 2.29 us  [call(): pl.pallas_call(kernel, out_shape=[make(s, F32) for s in outs], in_specs=[...]
  transfers between devices with their start and end apart: 36 -> 8, of which waited for: 14 -> 4; matrix products, arithmetic and copies ran while one was open for 8% -> 0% of each run, Pallas kernels for 0% -> 0%
where the time goes in v1:
time: 53.9 us; the launch traced here: 53.5 us
  starting transfers between devices  38.7 us (72%)
  waiting for transfers between devices  9.75 us (18%)
  local copies, waits for them, and re-layouts  2.72 us (5%)
  Pallas kernels  2.29 us (4%)
    ppermute x4, starting transfers between devices, exchange(): from_high = lax.ppermute(to_low, axis, [(i + 1, i) for i in range(n - 1)])  26.9 us
    ppermute x4, starting transfers between devices, exchange(): from_low = lax.ppermute(to_high, axis, [(i, i + 1) for i in range(n - 1)])  11.8 us
    ppermute x4, waiting for transfers between devices, exchange(): from_high = lax.ppermute(to_low, axis, [(i + 1, i) for i in range(n - 1)])  9.74 us
    unnamed x10, local copies, waits for them, and re-layouts  2.72 us
    pallas_call x5, Pallas kernels, call(): pl.pallas_call(kernel, out_shape=[make(s, F32) for s in outs], in_specs=[...  2.29 us
  transfers between devices with their start and end apart: 8, of which 4 were waited for; matrix products, arithmetic and copies ran while one was open for 0% of the time, Pallas kernels for 0%

profile of v1, /device:TPU:25, one launch (start us, length us, event | category | flops | bytes accessed | tf_op | source)
XLA Modules:
  0.0 53.5 jit_solution(6908993496996804522)
XLA Ops:
  0.0 0.9 %copy-done = f32[8,16,256]{2,1,0:T(8,128)S(1)} copy-done((f32[8,16,256]{2,1,0:T(8,128)S(1)}, f32[8,16,256]{2,1,0:T(8,128)}, u32[]{:S(2)}) %copy-start) | copy-done | bytes 131096
  0.9 0.9 %copy-done.2 = s32[8,16,256]{2,1,0:T(8,128)S(1)} copy-done((s32[8,16,256]{2,1,0:T(8,128)S(1)}, s32[8,16,256]{2,1,0:T(8,128)}, u32[]{:S(2)}) %copy-start.2) | copy-done | bytes 131096
  1.8 0.9 %copy-done.4 = f32[8,16,256]{2,1,0:T(8,128)S(1)} copy-done((f32[8,16,256]{2,1,0:T(8,128)S(1)}, f32[8,16,256]{2,1,0:T(8,128)}, u32[]{:S(2)}) %copy-start.4) | copy-done | bytes 131096
  2.7 3.7 %collective-permute-start = (f32[112,256]{1,0:T(8,128)S(1)}, f32[112,256]{1,0:T(8,128)S(1)}, u32[]{:S(2)}, u32[]{:S(2)}) collective-permute-start(f32[112,256]{1,0:T(8,128)S(1)} %get-tuple-element.20), channel_id=1, source_target_pairs={{0,128},{128,256},{256,384},{384,512},{512,640},{640,768},{768,896... | collective-permute-start | bytes 344072 | tf_op jit(solution)/shard_map/ppermute | solution.py:390
  6.4 1.9 %collective-permute-start.1 = (f32[112,256]{1,0:T(8,128)S(1)}, f32[112,256]{1,0:T(8,128)S(1)}, u32[]{:S(2)}, u32[]{:S(2)}) collective-permute-start(f32[112,256]{1,0:T(8,128)S(1)} %get-tuple-element.21), channel_id=1, source_target_pairs={{128,0},{256,128},{384,256},{512,384},{640,512},{768,640},{896,768... | collective-permute-start | bytes 344072 | tf_op jit(solution)/shard_map/ppermute | solution.py:391
  8.4 0.0 collective-permute-done.left
  8.4 4.2 %collective-permute-done.1.right = f32[112,256]{1,0:T(8,128)S(1)} collective-permute-done((f32[112,256]{1,0:T(8,128)S(1)}, f32[112,256]{1,0:T(8,128)S(1)}, u32[]{:S(2)}, u32[]{:S(2)}) %collective-permute-start.1) | collective-permute-done | bytes 114720 | tf_op jit(solution)/shard_map/ppermute | solution.py:391
  12.5 0.2 shard_map.38
  12.8 3.5 %collective-permute-start.2 = (f32[40,256]{1,0:T(8,128)S(1)}, f32[40,256]{1,0:T(8,128)S(1)}, u32[]{:S(2)}, u32[]{:S(2)}) collective-permute-start(f32[40,256]{1,0:T(8,128)S(1)} %get-tuple-element.22), channel_id=1, source_target_pairs={{0,1},{1,2},{2,3},{3,4},{4,5},{5,6},{6,7},{7,8},{8,9},{9,10},{10,1... | collective-permute-start | bytes 122888 | tf_op jit(solution)/shard_map/ppermute | solution.py:390
  16.3 17.0 %collective-permute-start.3 = (f32[40,256]{1,0:T(8,128)S(1)}, f32[40,256]{1,0:T(8,128)S(1)}, u32[]{:S(2)}, u32[]{:S(2)}) collective-permute-start(f32[40,256]{1,0:T(8,128)S(1)} %get-tuple-element.23), channel_id=1, source_target_pairs={{1,0},{2,1},{3,2},{4,3},{5,4},{6,5},{7,6},{8,7},{9,8},{10,9},{11,1... | collective-permute-start | bytes 122888 | tf_op jit(solution)/shard_map/ppermute | solution.py:391
  33.3 0.0 collective-permute-done.2.low
  33.3 1.1 %collective-permute-done.3.high = f32[40,256]{1,0:T(8,128)S(1)} collective-permute-done((f32[40,256]{1,0:T(8,128)S(1)}, f32[40,256]{1,0:T(8,128)S(1)}, u32[]{:S(2)}, u32[]{:S(2)}) %collective-permute-start.3) | collective-permute-done | bytes 40992 | tf_op jit(solution)/shard_map/ppermute | solution.py:391
  34.4 0.6 %shard_map.39 = (f32[160,256]{1,0:T(8,128)S(1)}, f32[8,256]{1,0:T(8,128)S(1)}, f32[8,256]{1,0:T(8,128)S(1)}, f32[32,128]{1,0:T(8,128)S(1)}, f32[32,128]{1,0:T(8,...) custom-call(f32[8,16,256]{2,1,0:T(8,128)S(1)} %copy-done.4, f32[8,16,256]{2,1,0:T(8,128)S(1)} %copy-done, ...), custom_call_target="tpu_custom_call" | custom-call | tf_op jit(solution)/shard_map/pallas_call | solution.py:18
  35.0 2.7 %collective-permute-start.4 = (f32[48,256]{1,0:T(8,128)S(1)}, f32[48,256]{1,0:T(8,128)S(1)}, u32[]{:S(2)}, u32[]{:S(2)}) collective-permute-start(f32[48,256]{1,0:T(8,128)S(1)} %get-tuple-element.30), channel_id=1, source_target_pairs={{0,128},{128,256},{256,384},{384,512},{512,640},{640,768},{768,896... | collective-permute-start | bytes 147464 | tf_op jit(solution)/shard_map/ppermute | solution.py:390
  37.6 1.9 %collective-permute-start.5 = (f32[48,256]{1,0:T(8,128)S(1)}, f32[48,256]{1,0:T(8,128)S(1)}, u32[]{:S(2)}, u32[]{:S(2)}) collective-permute-start(f32[48,256]{1,0:T(8,128)S(1)} %get-tuple-element.31), channel_id=1, source_target_pairs={{128,0},{256,128},{384,256},{512,384},{640,512},{768,640},{896,768... | collective-permute-start | bytes 147464 | tf_op jit(solution)/shard_map/ppermute | solution.py:391
  39.6 0.0 collective-permute-done.4.left.cleft
  39.6 3.5 %collective-permute-done.5.right.cright = f32[48,256]{1,0:T(8,128)S(1)} collective-permute-done((f32[48,256]{1,0:T(8,128)S(1)}, f32[48,256]{1,0:T(8,128)S(1)}, u32[]{:S(2)}, u32[]{:S(2)}) %collective-permute-start.5) | collective-permute-done | bytes 49184 | tf_op jit(solution)/shard_map/ppermute | solution.py:391
  43.0 0.0 copy-done.1
  43.0 0.2 shard_map.40
  43.2 1.9 %collective-permute-start.6 = (f32[72,128]{1,0:T(8,128)S(1)}, f32[72,128]{1,0:T(8,128)S(1)}, u32[]{:S(2)}, u32[]{:S(2)}) collective-permute-start(f32[72,128]{1,0:T(8,128)S(1)} %get-tuple-element.33), channel_id=1, source_target_pairs={{0,1},{1,2},{2,3},{3,4},{4,5},{5,6},{6,7},{7,8},{8,9},{9,10},{10,1... | collective-permute-start | bytes 110600 | tf_op jit(solution)/shard_map/ppermute | solution.py:390
  45.1 6.1 %collective-permute-start.7 = (f32[72,128]{1,0:T(8,128)S(1)}, f32[72,128]{1,0:T(8,128)S(1)}, u32[]{:S(2)}, u32[]{:S(2)}) collective-permute-start(f32[72,128]{1,0:T(8,128)S(1)} %get-tuple-element.34), channel_id=1, source_target_pairs={{1,0},{2,1},{3,2},{4,3},{5,4},{6,5},{7,6},{8,7},{9,8},{10,9},{11,1... | collective-permute-start | bytes 110600 | tf_op jit(solution)/shard_map/ppermute | solution.py:391
  51.2 0.0 collective-permute-done.6.clow
  51.2 1.0 %collective-permute-done.7.chigh = f32[72,128]{1,0:T(8,128)S(1)} collective-permute-done((f32[72,128]{1,0:T(8,128)S(1)}, f32[72,128]{1,0:T(8,128)S(1)}, u32[]{:S(2)}, u32[]{:S(2)}) %collective-permute-start.7) | collective-permute-done | bytes 36896 | tf_op jit(solution)/shard_map/ppermute | solution.py:391
  52.2 1.3 %shard_map.41 = f32[8,16,256]{2,1,0:T(8,128)} custom-call(f32[8,16,256]{2,1,0:T(8,128)S(1)} %copy-done.1, s32[8,16,256]{2,1,0:T(8,128)S(1)} %copy-done.3, f32[112,256]{1,0:T(8,128)S(1)} %collective-permute-done.left, f32[112,256]{1,0:T(8,128)S(1)} %collective-permute-done.1.right, f32[40,256]{1,0:T(8,128)S(1)} %collective-permute-done.2.low, ...), custom_call_target="tpu_custom_call" | custom-call | tf_op jit(solution)/shard_map/pallas_call | solution.py:18
  (7 shorter events, 0.0 us)
Async XLA Ops:
  0.0 0.9 %copy-start = (f32[8,16,256]{2,1,0:T(8,128)S(1)}, f32[8,16,256]{2,1,0:T(8,128)}, u32[]{:S(2)}) copy-start(f32[8,16,256]{2,1,0:T(8,128)} %b.9) | copy-start | bytes 393220
  0.9 0.9 %copy-start.2 = (s32[8,16,256]{2,1,0:T(8,128)S(1)}, s32[8,16,256]{2,1,0:T(8,128)}, u32[]{:S(2)}) copy-start(s32[8,16,256]{2,1,0:T(8,128)} %n.9) | copy-start | bytes 393220
  1.8 0.9 %copy-start.4 = (f32[8,16,256]{2,1,0:T(8,128)S(1)}, f32[8,16,256]{2,1,0:T(8,128)}, u32[]{:S(2)}) copy-start(f32[8,16,256]{2,1,0:T(8,128)} %g.5) | copy-start | bytes 393220
  2.7 5.6 %collective-permute-start = (f32[112,256]{1,0:T(8,128)S(1)}, f32[112,256]{1,0:T(8,128)S(1)}, u32[]{:S(2)}, u32[]{:S(2)}) collective-permute-start(f32[112,256]{1,0:T(8,128)S(1)} %get-tuple-element.20), channel_id=1, source_target_pairs={{0,128},{128,256},{256,384},{384,512},{512,640},{640,768},{768,896... | collective-permute-start | bytes 344072 | tf_op jit(solution)/shard_map/ppermute | solution.py:390
  6.4 6.1 %collective-permute-start.1 = (f32[112,256]{1,0:T(8,128)S(1)}, f32[112,256]{1,0:T(8,128)S(1)}, u32[]{:S(2)}, u32[]{:S(2)}) collective-permute-start(f32[112,256]{1,0:T(8,128)S(1)} %get-tuple-element.21), channel_id=1, source_target_pairs={{128,0},{256,128},{384,256},{512,384},{640,512},{768,640},{896,768... | collective-permute-start | bytes 344072 | tf_op jit(solution)/shard_map/ppermute | solution.py:391
  12.8 20.5 %collective-permute-start.2 = (f32[40,256]{1,0:T(8,128)S(1)}, f32[40,256]{1,0:T(8,128)S(1)}, u32[]{:S(2)}, u32[]{:S(2)}) collective-permute-start(f32[40,256]{1,0:T(8,128)S(1)} %get-tuple-element.22), channel_id=1, source_target_pairs={{0,1},{1,2},{2,3},{3,4},{4,5},{5,6},{6,7},{7,8},{8,9},{9,10},{10,1... | collective-permute-start | bytes 122888 | tf_op jit(solution)/shard_map/ppermute | solution.py:390
  16.3 18.0 %collective-permute-start.3 = (f32[40,256]{1,0:T(8,128)S(1)}, f32[40,256]{1,0:T(8,128)S(1)}, u32[]{:S(2)}, u32[]{:S(2)}) collective-permute-start(f32[40,256]{1,0:T(8,128)S(1)} %get-tuple-element.23), channel_id=1, source_target_pairs={{1,0},{2,1},{3,2},{4,3},{5,4},{6,5},{7,6},{8,7},{9,8},{10,9},{11,1... | collective-permute-start | bytes 122888 | tf_op jit(solution)/shard_map/ppermute | solution.py:391
  34.4 8.7 %copy-start.1 = (f32[8,16,256]{2,1,0:T(8,128)S(1)}, f32[8,16,256]{2,1,0:T(8,128)}, u32[]{:S(2)}) copy-start(f32[8,16,256]{2,1,0:T(8,128)} %b.9) | copy-start | bytes 393220
  34.4 8.7 %copy-start.3 = (s32[8,16,256]{2,1,0:T(8,128)S(1)}, s32[8,16,256]{2,1,0:T(8,128)}, u32[]{:S(2)}) copy-start(s32[8,16,256]{2,1,0:T(8,128)} %n.9) | copy-start | bytes 393220
  35.0 4.6 %collective-permute-start.4 = (f32[48,256]{1,0:T(8,128)S(1)}, f32[48,256]{1,0:T(8,128)S(1)}, u32[]{:S(2)}, u32[]{:S(2)}) collective-permute-start(f32[48,256]{1,0:T(8,128)S(1)} %get-tuple-element.30), channel_id=1, source_target_pairs={{0,128},{128,256},{256,384},{384,512},{512,640},{640,768},{768,896... | collective-permute-start | bytes 147464 | tf_op jit(solution)/shard_map/ppermute | solution.py:390
  37.6 5.4 %collective-permute-start.5 = (f32[48,256]{1,0:T(8,128)S(1)}, f32[48,256]{1,0:T(8,128)S(1)}, u32[]{:S(2)}, u32[]{:S(2)}) collective-permute-start(f32[48,256]{1,0:T(8,128)S(1)} %get-tuple-element.31), channel_id=1, source_target_pairs={{128,0},{256,128},{384,256},{512,384},{640,512},{768,640},{896,768... | collective-permute-start | bytes 147464 | tf_op jit(solution)/shard_map/ppermute | solution.py:391
  43.2 8.0 %collective-permute-start.6 = (f32[72,128]{1,0:T(8,128)S(1)}, f32[72,128]{1,0:T(8,128)S(1)}, u32[]{:S(2)}, u32[]{:S(2)}) collective-permute-start(f32[72,128]{1,0:T(8,128)S(1)} %get-tuple-element.33), channel_id=1, source_target_pairs={{0,1},{1,2},{2,3},{3,4},{4,5},{5,6},{6,7},{7,8},{8,9},{9,10},{10,1... | collective-permute-start | bytes 110600 | tf_op jit(solution)/shard_map/ppermute | solution.py:390
  45.1 7.1 %collective-permute-start.7 = (f32[72,128]{1,0:T(8,128)S(1)}, f32[72,128]{1,0:T(8,128)S(1)}, u32[]{:S(2)}, u32[]{:S(2)}) collective-permute-start(f32[72,128]{1,0:T(8,128)S(1)} %get-tuple-element.34), channel_id=1, source_target_pairs={{1,0},{2,1},{3,2},{4,3},{5,4},{6,5},{7,6},{8,7},{9,8},{10,9},{11,1... | collective-permute-start | bytes 110600 | tf_op jit(solution)/shard_map/ppermute | solution.py:391

commit v2 on v1

--- a/solution.py
+++ b/solution.py
@@ -13,15 +13,15 @@
 CX, CY, CZ = 4, 8, 128
 
 
-def call(kernel, outs, *args, scratch=(), hbm_out=False):
+def call(kernel, outs, *args, scratch=(), hbm=0, hbm_out=False, vmem=8 * 2**20):
     make = jax.ShapeDtypeStruct if hbm_out else pltpu.VMEM
     return pl.pallas_call(
         kernel,
         out_shape=[make(s, F32) for s in outs],
-        in_specs=[VM] * len(args),
+        in_specs=[pl.BlockSpec(memory_space=pltpu.HBM)] * hbm + [VM] * (len(args) - hbm),
         out_specs=[VM] * len(outs),
-        scratch_shapes=[pltpu.VMEM(s, F32) for s in scratch],
-        compiler_params=pltpu.CompilerParams(vmem_limit_bytes=8 * 2**20),
+        scratch_shapes=[pltpu.VMEM(s, F32) if isinstance(s, tuple) else s for s in scratch],
+        compiler_params=pltpu.CompilerParams(vmem_limit_bytes=vmem),
     )(*args)
 
 
@@ -64,51 +64,75 @@
     return 6.0 + 0.25 * n.astype(F32)
 
 
-def pack_x_kernel(g, b, n, lo, hi):
-    for out, layers in ((lo, (0, 1, 2)), (hi, (7, 6, 5))):
+def place(x):
+    odd = lax.axis_index("group") % 2
+    return x + odd * (BX - 1 - 2 * x)
+
+
+def side_of_dev():
+    return lax.axis_index("dev") % 2
+
+
+def load_kernel(g_hbm, b_hbm, n_hbm, cross, chip, g, b, w, d, n, sems):
+    copies = [
+        pltpu.make_async_copy(src, dst, sems.at[k])
+        for k, (src, dst) in enumerate(((g_hbm, g), (b_hbm, b), (n_hbm, n)))
+    ]
+    for c in copies:
+        c.start()
+    for c in copies:
+        c.wait()
+    for x in range(BX):
+        diag = diag_of(n[x])
+        d[x] = diag
+        w[x] = OMEGA / diag
+    for out, layers in ((cross, (0, 1, 2)), (chip, (7, 6, 5))):
         for k in range(3):
-            out[k * BY : (k + 1) * BY, :] = g[layers[k]]
+            out[k * BY : (k + 1) * BY, :] = g[place(layers[k])]
         for k in range(2):
-            out[(3 + k) * BY : (4 + k) * BY, :] = OMEGA / diag_of(n[layers[k]])
-            out[(5 + k) * BY : (6 + k) * BY, :] = b[layers[k]]
+            out[(3 + k) * BY : (4 + k) * BY, :] = w[place(layers[k])]
+            out[(5 + k) * BY : (6 + k) * BY, :] = b[place(layers[k])]
 
 
 class Wide:
-    def __init__(self, g, b, n, left, right):
-        self.g, self.b, self.n, self.left, self.right = g, b, n, left, right
-        self.ws = {}
-
-    def _side(self, x):
-        return (self.left, -1 - x) if x < 0 else (self.right, x - BX)
+    def __init__(self, g, b, w, left, right):
+        self.own, self.left, self.right = (g, w, b), left, right
+
+    def _get(self, which, base, x):
+        if 0 <= x < BX:
+            return self.own[which][place(x)]
+        ref, k = (self.left, -1 - x) if x < 0 else (self.right, x - BX)
+        return slab(ref, base + k)
 
     def guess(self, x):
-        if 0 <= x < BX:
-            return self.g[x]
-        ref, k = self._side(x)
-        return slab(ref, k)
+        return self._get(0, 0, x)
 
     def w(self, x):
-        if x not in self.ws:
-            if 0 <= x < BX:
-                self.ws[x] = OMEGA / diag_of(self.n[x])
-            else:
-                ref, k = self._side(x)
-                self.ws[x] = slab(ref, 3 + k)
-        return self.ws[x]
+        return self._get(1, 3, x)
 
     def rhs(self, x):
-        if 0 <= x < BX:
-            return self.b[x]
-        ref, k = self._side(x)
-        return slab(ref, 5 + k)
+        return self._get(2, 5, x)
+
+
+def give(both, first, second):
+    p = side_of_dev()
+    first[...] = both[p]
+    second[...] = both[1 - p]
+
+
+def take(both, first, second):
+    p = side_of_dev()
+    both[p] = first[...]
+    both[1 - p] = second[...]
 
 
 Y_G, Y_P, Y_W, Y_Q = 0, 12, 22, 32
 Y_ROWS = 40
 
 
-def pack_y_kernel(g, b, n, left, right, lo, hi, f1z):
-    a = Wide(g, b, n, left, right)
+def pack_y_kernel(g, b, w, left, right, first, second, f1z, both):
+    a = Wide(g, b, w, left, right)
+    lo, hi = both.at[0], both.at[1]
     for x in range(-2, 10):
         here = a.guess(x)
         f = KEEP * here + a.w(x) * (
@@ -126,13 +150,18 @@
             if 0 <= x <= 7:
                 k = Y_Q + x
                 out[k : k + 1, :] = a.w(x)[y : y + 1] * (a.rhs(x)[y : y + 1] + f[inner : inner + 1])
+    give(both, first, second)
 
 
 X2_ROWS = 3 * BY
 
 
-def middle_kernel(g, b, n, left, right, f1z, low, high, f2, f2low, f2high, c1, wc, lo, hi, col, line, sums):
-    a = Wide(g, b, n, left, right)
+def middle_kernel(
+    g, b, w, d, left, right, f1z, first, second, f2, f2low, f2high, c1, wc, lo, hi, both, col, line, sums
+):
+    a = Wide(g, b, w, left, right)
+    take(both, first, second)
+    low, high = both.at[0], both.at[1]
     rows = lax.broadcasted_iota(jnp.int32, (BY, NZ), 0)
     f1 = {}
     for x in range(-2, 10):
@@ -170,7 +199,7 @@
         f = sec[x]
         r = (
             a.rhs(x)
-            - diag_of(n[x]) * f
+            - d[place(x)] * f
             + sec[x - 1]
             + sec[x + 1]
             + beside_z(f)
@@ -178,10 +207,10 @@
         )
         if x % 2:
             pairs[-1] = pairs[-1] + r
-            points[-1] = points[-1] + n[x].astype(F32)
+            points[-1] = points[-1] + d[place(x)]
         else:
             pairs.append(r)
-            points.append(n[x].astype(F32))
+            points.append(d[place(x)])
     sums[...] = lax.dot_general(
         jnp.concatenate(pairs + points, axis=0),
         halved(NZ, CZ),
@@ -193,8 +222,8 @@
         at = x * BY
         total = sums[pl.ds(at, CY, stride=2), :] + sums[pl.ds(at + 1, CY, stride=2), :]
         at = (CX + x) * BY
-        count = sums[pl.ds(at, CY, stride=2), :] + sums[pl.ds(at + 1, CY, stride=2), :]
-        weight = OMEGA / (6.0 + count / 8.0)
+        diags = sums[pl.ds(at, CY, stride=2), :] + sums[pl.ds(at + 1, CY, stride=2), :]
+        weight = OMEGA / (0.5 * diags - 18.0)
         first = weight * (0.5 * total)
         c1[x * CY : (x + 1) * CY, :] = first
         wc[x * CY : (x + 1) * CY, :] = weight
@@ -224,38 +253,39 @@
 Z_ROWS = 72
 
 
-def pack_c_kernel(b, n, f2, c1, wc, left, right, lo, hi, c2z):
+def pack_c_kernel(b, w, f2, c1, wc, left, right, one, two, c2z, both):
     a = Coarse(c1, wc, left, right)
+    lo, hi = both.at[0], both.at[1]
     second = {}
     for x in range(-3, 7):
-        c, w = a.first(x), a.w(x)
-        second[x] = (1.0 + KEEP) * c + w * (
+        c, cw = a.first(x), a.w(x)
+        second[x] = (1.0 + KEEP) * c + cw * (
             a.first(x - 1) + a.first(x + 1) + beside_z(c) + beside_y(c, 0.0, 0.0)
         )
         c2z[(x + 3) * CY : (x + 4) * CY, :] = second[x]
         for out, y in ((lo, 0), (hi, CY - 1)):
-            for base, v in ((Z_C, c), (Z_P, second[x]), (Z_W, w)):
+            for base, v in ((Z_C, c), (Z_P, second[x]), (Z_W, cw)):
                 k = base + x + 3
                 out[k : k + 1, :] = v[y : y + 1]
     for x in range(-2, 6):
-        s, c, w = second[x], a.first(x), a.w(x)
+        s, c, cw = second[x], a.first(x), a.w(x)
         below, above = shift_y(s, 0.0, 0.0)
         inner = {0: above, 1: below}
         for side, (out, y, y2) in enumerate(((lo, 0, 1), (hi, CY - 1, CY - 2))):
             k = Z_Q + x + 2
-            out[k : k + 1, :] = (c + w * inner[side])[y : y + 1]
+            out[k : k + 1, :] = (c + cw * inner[side])[y : y + 1]
         if -1 <= x <= 4:
-            part = KEEP * s + c + w * (second[x - 1] + second[x + 1] + beside_z(s))
+            part = KEEP * s + c + cw * (second[x - 1] + second[x + 1] + beside_z(s))
             for side, (out, y, y2) in enumerate(((lo, 0, 1), (hi, CY - 1, CY - 2))):
                 k = Z_R + x + 1
-                out[k : k + 1, :] = (part + w * inner[side])[y2 : y2 + 1]
+                out[k : k + 1, :] = (part + cw * inner[side])[y2 : y2 + 1]
                 k = Z_V + x + 1
-                out[k : k + 1, :] = w[y2 : y2 + 1]
+                out[k : k + 1, :] = cw[y2 : y2 + 1]
     for out, y, inner in ((lo, 0, 1), (hi, BY - 1, BY - 2)):
         for x in range(BX):
             at = (x + 1) * BY
-            w = OMEGA / diag_of(n[x][y : y + 1])
-            v = w * (b[x][y : y + 1] + f2[at + inner : at + inner + 1, :])
+            at_x = place(x)
+            v = w[at_x][y : y + 1] * (b[at_x][y : y + 1] + f2[at + inner : at + inner + 1, :])
             for half in range(2):
                 k = Z_S + 2 * x + half
                 out[k : k + 1, :] = v[:, half * CZ : (half + 1) * CZ]
@@ -265,14 +295,18 @@
             for half in range(2):
                 k = Z_K + 2 * j + half
                 out[k : k + 1, :] = v[:, half * CZ : (half + 1) * CZ]
+    give(both, one, two)
 
 
 def last_kernel(
-    b, n, left, right, low, high, f2, f2low, f2high, c1, wc, cleft, cright, c2z, clow, chigh,
-    out, col, line, line3, fine, corr, col2, s1, gline, g1line,
+    b, w, left, right, first, second, f2, f2low, f2high, c1, wc, cleft, cright, c2z, one, two,
+    out, both, cboth, col, line, line3, fine, corr, col2, s1, gline, g1line,
 ):
     a = Coarse(c1, wc, cleft, cright)
-    wide = Wide(None, b, n, left, right)
+    wide = Wide(None, b, w, left, right)
+    take(both, first, second)
+    take(cboth, one, two)
+    low, high, clow, chigh = both.at[0], both.at[1], cboth.at[0], cboth.at[1]
     crow = lax.broadcasted_iota(jnp.int32, (CY, CZ), 0)
     c2 = {}
     for x in range(-3, 7):
@@ -376,7 +410,7 @@
         )
     for x in range(BX):
         f = g1[x]
-        out[x] = KEEP * f + wide.w(x) * (
+        out[place(x)] = KEEP * f + wide.w(x) * (
             wide.rhs(x)
             + g1[x - 1]
             + g1[x + 1]
@@ -385,34 +419,53 @@
         )
 
 
-def exchange(to_low, to_high, axis):
-    n = lax.axis_size(axis)
-    from_low = lax.ppermute(to_high, axis, [(i, i + 1) for i in range(n - 1)])
-    from_high = lax.ppermute(to_low, axis, [(i + 1, i) for i in range(n - 1)])
-    return from_low, from_high
+def swap(v, axis, start):
+    pairs = [(i, i + 1) for i in range(start, lax.axis_size(axis) - 1, 2)]
+    return lax.ppermute(v, axis, pairs + [(j, i) for i, j in pairs])
+
+
+def exchange(first, second, axis):
+    return swap(first, axis, 1), swap(second, axis, 0)
 
 
 def body(g, b, n):
-    lo, hi = call(pack_x_kernel, [(7 * BY, NZ)] * 2, g, b, n)
-    left, right = exchange(lo, hi, "group")
-    lo, hi, f1z = call(pack_y_kernel, [(Y_ROWS, NZ)] * 2 + [(12 * BY, NZ)], g, b, n, left, right)
-    low, high = exchange(lo, hi, "dev")
-    f2, f2low, f2high, c1, wc, lo, hi = call(
+    block = (BX, BY, NZ)
+    cross, chip, g, b, w, d = call(
+        load_kernel,
+        [(7 * BY, NZ)] * 2 + [block] * 4,
+        g, b, n,
+        hbm=3,
+        vmem=None,
+        scratch=[pltpu.VMEM(block, jnp.int32), pltpu.SemaphoreType.DMA((3,))],
+    )
+    left, right = exchange(cross, chip, "group")
+    first, second, f1z = call(
+        pack_y_kernel,
+        [(Y_ROWS, NZ)] * 2 + [(12 * BY, NZ)],
+        g, b, w, left, right,
+        scratch=[(2, Y_ROWS, NZ)],
+    )
+    first, second = exchange(first, second, "dev")
+    f2, f2low, f2high, c1, wc, cross, chip = call(
         middle_kernel,
         [(10 * BY, NZ), (BX, NZ), (BX, NZ), (CX * CY, CZ), (CX * CY, CZ), (X2_ROWS, NZ), (X2_ROWS, NZ)],
-        g, b, n, left, right, f1z, low, high,
-        scratch=[(16, NZ), (2, 16, NZ), (8 * BY, CZ)],
-    )
-    cleft, cright = exchange(lo, hi, "group")
-    lo, hi, c2z = call(
-        pack_c_kernel, [(Z_ROWS, CZ)] * 2 + [(10 * CY, CZ)], b, n, f2, c1, wc, cleft, cright
-    )
-    clow, chigh = exchange(lo, hi, "dev")
+        g, b, w, d, left, right, f1z, first, second,
+        scratch=[(2, Y_ROWS, NZ), (16, NZ), (2, 16, NZ), (8 * BY, CZ)],
+    )
+    cleft, cright = exchange(cross, chip, "group")
+    one, two, c2z = call(
+        pack_c_kernel,
+        [(Z_ROWS, CZ)] * 2 + [(10 * CY, CZ)],
+        b, w, f2, c1, wc, cleft, cright,
+        scratch=[(2, Z_ROWS, CZ)],
+    )
+    one, two = exchange(one, two, "dev")
     (out,) = call(
         last_kernel,
-        [(BX, BY, NZ)],
-        b, n, left, right, low, high, f2, f2low, f2high, c1, wc, cleft, cright, c2z, clow, chigh,
+        [block],
+        b, w, left, right, first, second, f2, f2low, f2high, c1, wc, cleft, cright, c2z, one, two,
         scratch=[
+            (2, Y_ROWS, NZ), (2, Z_ROWS, CZ),
             (16, CZ), (2, 16, CZ), (2, 8, CZ), (6 * BY + 16, CZ), (6 * BY + 16, NZ), (16, NZ), (8, NZ), (2, 16, NZ), (2, 8, NZ),
         ],
         hbm_out=True,

time: 53.9 us -> 49.1 us (0.911)
  local copies, waits for them, and re-layouts: 2.72 us -> 0 us
  starting transfers between devices: 38.7 us -> 36.5 us
  waiting for transfers between devices: 9.75 us -> 8.36 us
  Pallas kernels: 2.29 us -> 3.35 us
    unnamed x10 -> x0, local copies, waits for them, and re-layouts: 2.72 us -> none
    ppermute x8, starting transfers between devices: 38.7 us -> 36.5 us  [swap(): return lax.ppermute(v, axis, pairs + [(j, i) for i, j in pairs])]
    ppermute x8, waiting for transfers between devices: 9.75 us -> 8.36 us  [swap(): return lax.ppermute(v, axis, pairs + [(j, i) for i, j in pairs])]
    pallas_call x5, Pallas kernels: 2.29 us -> 3.35 us  [call(): pl.pallas_call(kernel, out_shape=[make(s, F32) for s in outs], in_specs=[...]
  transfers between devices with their start and end apart: 8 -> 8, of which waited for: 4 -> 6; matrix products, arithmetic and copies ran while one was open for 0% -> 0% of each run, Pallas kernels for 0% -> 0%
where the time goes in v2:
time: 49.1 us; the launch traced here: 48.3 us
  starting transfers between devices  36.5 us (74%)
  waiting for transfers between devices  8.36 us (17%)
  Pallas kernels  3.35 us (7%)
    ppermute x8, starting transfers between devices, swap(): return lax.ppermute(v, axis, pairs + [(j, i) for i, j in pairs])  36.5 us
    ppermute x8, waiting for transfers between devices, swap(): return lax.ppermute(v, axis, pairs + [(j, i) for i, j in pairs])  8.36 us
    pallas_call x5, Pallas kernels, call(): pl.pallas_call(kernel, out_shape=[make(s, F32) for s in outs], in_specs=[...  3.35 us
  transfers between devices with their start and end apart: 8, of which 6 were waited for; matrix products, arithmetic and copies ran while one was open for 0% of the time, Pallas kernels for 0%

profile of v2, /device:TPU:25, one launch (start us, length us, event | category | flops | bytes accessed | tf_op | source)
XLA Modules:
  0.0 48.3 jit_solution(6119987471110882081)
XLA Ops:
  0.0 1.1 %shard_map.37 = (f32[112,256]{1,0:T(8,128)S(1)}, f32[112,256]{1,0:T(8,128)S(1)}, f32[8,16,256]{2,1,0:T(8,128)S(1)}, f32[8,16,256]{2,1,0:T(8,128)S(1)}, f32[8,16,...) custom-call(f32[8,16,256]{2,1,0:T(8,128)} %g_hbm.1, f32[8,16,256]{2,1,0:T(8,128)} %b_hbm.1, s32[8,16,256]{2,1,0:T(8,128)} %n_hbm.1), custom_call_target="tpu_custom_call" | custom-call | tf_op jit(solution)/shard_map/pallas_call | solution.py:18
  1.1 3.7 %collective-permute-start = (f32[112,256]{1,0:T(8,128)S(1)}, f32[112,256]{1,0:T(8,128)S(1)}, u32[]{:S(2)}, u32[]{:S(2)}) collective-permute-start(f32[112,256]{1,0:T(8,128)S(1)} %get-tuple-element.26), channel_id=1, source_target_pairs={{128,256},{384,512},{640,768},{256,128},{512,384},{768,640},{129,2... | collective-permute-start | bytes 344072 | tf_op jit(solution)/shard_map/ppermute | solution.py:424
  4.8 1.9 %collective-permute-start.1 = (f32[112,256]{1,0:T(8,128)S(1)}, f32[112,256]{1,0:T(8,128)S(1)}, u32[]{:S(2)}, u32[]{:S(2)}) collective-permute-start(f32[112,256]{1,0:T(8,128)S(1)} %get-tuple-element.27), channel_id=1, source_target_pairs={{0,128},{256,384},{512,640},{768,896},{128,0},{384,256},{640,512},... | collective-permute-start | bytes 344072 | tf_op jit(solution)/shard_map/ppermute | solution.py:424
  6.7 0.5 %collective-permute-done.left = f32[112,256]{1,0:T(8,128)S(1)} collective-permute-done((f32[112,256]{1,0:T(8,128)S(1)}, f32[112,256]{1,0:T(8,128)S(1)}, u32[]{:S(2)}, u32[]{:S(2)}) %collective-permute-start) | collective-permute-done | bytes 114720 | tf_op jit(solution)/shard_map/ppermute | solution.py:424
  7.3 0.8 %collective-permute-done.1.right = f32[112,256]{1,0:T(8,128)S(1)} collective-permute-done((f32[112,256]{1,0:T(8,128)S(1)}, f32[112,256]{1,0:T(8,128)S(1)}, u32[]{:S(2)}, u32[]{:S(2)}) %collective-permute-start.1) | collective-permute-done | bytes 114720 | tf_op jit(solution)/shard_map/ppermute | solution.py:424
  8.0 0.2 shard_map.38
  8.2 18.6 %collective-permute-start.2 = (f32[40,256]{1,0:T(8,128)S(1)}, f32[40,256]{1,0:T(8,128)S(1)}, u32[]{:S(2)}, u32[]{:S(2)}) collective-permute-start(f32[40,256]{1,0:T(8,128)S(1)} %get-tuple-element.29), channel_id=1, source_target_pairs={{1,2},{3,4},{5,6},{7,8},{9,10},{11,12},{13,14},{15,16},{17,18},{19... | collective-permute-start | bytes 122888 | tf_op jit(solution)/shard_map/ppermute | solution.py:424
  26.8 1.9 %collective-permute-start.3 = (f32[40,256]{1,0:T(8,128)S(1)}, f32[40,256]{1,0:T(8,128)S(1)}, u32[]{:S(2)}, u32[]{:S(2)}) collective-permute-start(f32[40,256]{1,0:T(8,128)S(1)} %get-tuple-element.30), channel_id=1, source_target_pairs={{0,1},{2,3},{4,5},{6,7},{8,9},{10,11},{12,13},{14,15},{16,17},{18,... | collective-permute-start | bytes 122888 | tf_op jit(solution)/shard_map/ppermute | solution.py:424
  28.7 0.0 collective-permute-done.2.first
  28.7 2.8 %collective-permute-done.3.second = f32[40,256]{1,0:T(8,128)S(1)} collective-permute-done((f32[40,256]{1,0:T(8,128)S(1)}, f32[40,256]{1,0:T(8,128)S(1)}, u32[]{:S(2)}, u32[]{:S(2)}) %collective-permute-start.3) | collective-permute-done | bytes 40992 | tf_op jit(solution)/shard_map/ppermute | solution.py:424
  31.6 0.6 %shard_map.39 = (f32[160,256]{1,0:T(8,128)S(1)}, f32[8,256]{1,0:T(8,128)S(1)}, f32[8,256]{1,0:T(8,128)S(1)}, f32[32,128]{1,0:T(8,128)S(1)}, f32[32,128]{1,0:T(8,...) custom-call(f32[8,16,256]{2,1,0:T(8,128)S(1)} %get-tuple-element.28.g, f32[8,16,256]{2,1,0:T(8,128)S(1)} %get-tuple-element.24.b, ...), custom_call_target="tpu_custom_call" | custom-call | tf_op jit(solution)/shard_map/pallas_call | solution.py:18
  32.1 4.6 %collective-permute-start.4 = (f32[48,256]{1,0:T(8,128)S(1)}, f32[48,256]{1,0:T(8,128)S(1)}, u32[]{:S(2)}, u32[]{:S(2)}) collective-permute-start(f32[48,256]{1,0:T(8,128)S(1)} %get-tuple-element.38), channel_id=1, source_target_pairs={{128,256},{384,512},{640,768},{256,128},{512,384},{768,640},{129,2... | collective-permute-start | bytes 147464 | tf_op jit(solution)/shard_map/ppermute | solution.py:424
  36.7 1.9 %collective-permute-start.5 = (f32[48,256]{1,0:T(8,128)S(1)}, f32[48,256]{1,0:T(8,128)S(1)}, u32[]{:S(2)}, u32[]{:S(2)}) collective-permute-start(f32[48,256]{1,0:T(8,128)S(1)} %get-tuple-element.39), channel_id=1, source_target_pairs={{0,128},{256,384},{512,640},{768,896},{128,0},{384,256},{640,512},... | collective-permute-start | bytes 147464 | tf_op jit(solution)/shard_map/ppermute | solution.py:424
  38.7 0.0 collective-permute-done.4.left.cleft
  38.7 1.2 %collective-permute-done.5.right.cright = f32[48,256]{1,0:T(8,128)S(1)} collective-permute-done((f32[48,256]{1,0:T(8,128)S(1)}, f32[48,256]{1,0:T(8,128)S(1)}, u32[]{:S(2)}, u32[]{:S(2)}) %collective-permute-start.5) | collective-permute-done | bytes 49184 | tf_op jit(solution)/shard_map/ppermute | solution.py:424
  39.9 0.2 shard_map.40
  40.0 1.9 %collective-permute-start.6 = (f32[72,128]{1,0:T(8,128)S(1)}, f32[72,128]{1,0:T(8,128)S(1)}, u32[]{:S(2)}, u32[]{:S(2)}) collective-permute-start(f32[72,128]{1,0:T(8,128)S(1)} %get-tuple-element.41), channel_id=1, source_target_pairs={{1,2},{3,4},{5,6},{7,8},{9,10},{11,12},{13,14},{15,16},{17,18},{19... | collective-permute-start | bytes 110600 | tf_op jit(solution)/shard_map/ppermute | solution.py:424
  42.0 1.9 %collective-permute-start.7 = (f32[72,128]{1,0:T(8,128)S(1)}, f32[72,128]{1,0:T(8,128)S(1)}, u32[]{:S(2)}, u32[]{:S(2)}) collective-permute-start(f32[72,128]{1,0:T(8,128)S(1)} %get-tuple-element.42), channel_id=1, source_target_pairs={{0,1},{2,3},{4,5},{6,7},{8,9},{10,11},{12,13},{14,15},{16,17},{18,... | collective-permute-start | bytes 110600 | tf_op jit(solution)/shard_map/ppermute | solution.py:424
  43.9 3.0 %collective-permute-done.6.one = f32[72,128]{1,0:T(8,128)S(1)} collective-permute-done((f32[72,128]{1,0:T(8,128)S(1)}, f32[72,128]{1,0:T(8,128)S(1)}, u32[]{:S(2)}, u32[]{:S(2)}) %collective-permute-start.6) | collective-permute-done | bytes 36896 | tf_op jit(solution)/shard_map/ppermute | solution.py:424
  46.8 0.1 collective-permute-done.7.two
  47.0 1.3 %shard_map.41 = f32[8,16,256]{2,1,0:T(8,128)} custom-call(f32[8,16,256]{2,1,0:T(8,128)S(1)} %get-tuple-element.24.b, f32[8,16,256]{2,1,0:T(8,128)S(1)} %get-tuple-element.25.w, f32[112,256]{1,0:T(8,128)S(1)} %collective-permute-done.left, f32[112,256]{1,0:T(8,128)S(1)} %collective-permute-done.1.right, f32[40,256]{1,0:T(8,128)S(1)} %collective-permute-done.2.first, ...), custom_call_target="tpu_custom_call" | custom-call | tf_op jit(solution)/shard_map/pallas_call | solution.py:18
Async XLA Ops:
  1.1 6.1 %collective-permute-start = (f32[112,256]{1,0:T(8,128)S(1)}, f32[112,256]{1,0:T(8,128)S(1)}, u32[]{:S(2)}, u32[]{:S(2)}) collective-permute-start(f32[112,256]{1,0:T(8,128)S(1)} %get-tuple-element.26), channel_id=1, source_target_pairs={{128,256},{384,512},{640,768},{256,128},{512,384},{768,640},{129,2... | collective-permute-start | bytes 344072 | tf_op jit(solution)/shard_map/ppermute | solution.py:424
  4.8 3.2 %collective-permute-start.1 = (f32[112,256]{1,0:T(8,128)S(1)}, f32[112,256]{1,0:T(8,128)S(1)}, u32[]{:S(2)}, u32[]{:S(2)}) collective-permute-start(f32[112,256]{1,0:T(8,128)S(1)} %get-tuple-element.27), channel_id=1, source_target_pairs={{0,128},{256,384},{512,640},{768,896},{128,0},{384,256},{640,512},... | collective-permute-start | bytes 344072 | tf_op jit(solution)/shard_map/ppermute | solution.py:424
  8.2 20.5 %collective-permute-start.2 = (f32[40,256]{1,0:T(8,128)S(1)}, f32[40,256]{1,0:T(8,128)S(1)}, u32[]{:S(2)}, u32[]{:S(2)}) collective-permute-start(f32[40,256]{1,0:T(8,128)S(1)} %get-tuple-element.29), channel_id=1, source_target_pairs={{1,2},{3,4},{5,6},{7,8},{9,10},{11,12},{13,14},{15,16},{17,18},{19... | collective-permute-start | bytes 122888 | tf_op jit(solution)/shard_map/ppermute | solution.py:424
  26.8 4.7 %collective-permute-start.3 = (f32[40,256]{1,0:T(8,128)S(1)}, f32[40,256]{1,0:T(8,128)S(1)}, u32[]{:S(2)}, u32[]{:S(2)}) collective-permute-start(f32[40,256]{1,0:T(8,128)S(1)} %get-tuple-element.30), channel_id=1, source_target_pairs={{0,1},{2,3},{4,5},{6,7},{8,9},{10,11},{12,13},{14,15},{16,17},{18,... | collective-permute-start | bytes 122888 | tf_op jit(solution)/shard_map/ppermute | solution.py:424
  32.1 6.5 %collective-permute-start.4 = (f32[48,256]{1,0:T(8,128)S(1)}, f32[48,256]{1,0:T(8,128)S(1)}, u32[]{:S(2)}, u32[]{:S(2)}) collective-permute-start(f32[48,256]{1,0:T(8,128)S(1)} %get-tuple-element.38), channel_id=1, source_target_pairs={{128,256},{384,512},{640,768},{256,128},{512,384},{768,640},{129,2... | collective-permute-start | bytes 147464 | tf_op jit(solution)/shard_map/ppermute | solution.py:424
  36.7 3.1 %collective-permute-start.5 = (f32[48,256]{1,0:T(8,128)S(1)}, f32[48,256]{1,0:T(8,128)S(1)}, u32[]{:S(2)}, u32[]{:S(2)}) collective-permute-start(f32[48,256]{1,0:T(8,128)S(1)} %get-tuple-element.39), channel_id=1, source_target_pairs={{0,128},{256,384},{512,640},{768,896},{128,0},{384,256},{640,512},... | collective-permute-start | bytes 147464 | tf_op jit(solution)/shard_map/ppermute | solution.py:424
  40.0 6.8 %collective-permute-start.6 = (f32[72,128]{1,0:T(8,128)S(1)}, f32[72,128]{1,0:T(8,128)S(1)}, u32[]{:S(2)}, u32[]{:S(2)}) collective-permute-start(f32[72,128]{1,0:T(8,128)S(1)} %get-tuple-element.41), channel_id=1, source_target_pairs={{1,2},{3,4},{5,6},{7,8},{9,10},{11,12},{13,14},{15,16},{17,18},{19... | collective-permute-start | bytes 110600 | tf_op jit(solution)/shard_map/ppermute | solution.py:424
  42.0 5.0 %collective-permute-start.7 = (f32[72,128]{1,0:T(8,128)S(1)}, f32[72,128]{1,0:T(8,128)S(1)}, u32[]{:S(2)}, u32[]{:S(2)}) collective-permute-start(f32[72,128]{1,0:T(8,128)S(1)} %get-tuple-element.42), channel_id=1, source_target_pairs={{0,1},{2,3},{4,5},{6,7},{8,9},{10,11},{12,13},{14,15},{16,17},{18,... | collective-permute-start | bytes 110600 | tf_op jit(solution)/shard_map/ppermute | solution.py:424

commit v3 on v2

--- a/solution.py
+++ b/solution.py
@@ -67,6 +67,10 @@
 def place(x):
     odd = lax.axis_index("group") % 2
     return x + odd * (BX - 1 - 2 * x)
+
+
+def partner(ref):
+    return ref.at[1 - lax.axis_index("group") % 2]
 
 
 def side_of_dev():
@@ -96,7 +100,7 @@
 
 class Wide:
     def __init__(self, g, b, w, left, right):
-        self.own, self.left, self.right = (g, w, b), left, right
+        self.own, self.left, self.right = (g, w, b), left, partner(right)
 
     def _get(self, which, base, x):
         if 0 <= x < BX:
@@ -123,7 +127,7 @@
 def take(both, first, second):
     p = side_of_dev()
     both[p] = first[...]
-    both[1 - p] = second[...]
+    both[1 - p] = second[1 - p]
 
 
 Y_G, Y_P, Y_W, Y_Q = 0, 12, 22, 32
@@ -234,7 +238,7 @@
 
 class Coarse:
     def __init__(self, c1, wc, left, right):
-        self.c1, self.wc, self.left, self.right = c1, wc, left, right
+        self.c1, self.wc, self.left, self.right = c1, wc, left, partner(right)
 
     def _get(self, x, own, lanes):
         if 0 <= x < CX:
@@ -370,7 +374,7 @@
         if x == -2:
             f = slab(cleft, 2)
         elif x == 9:
-            f = slab(cright, 2)
+            f = slab(a.right, 2)
         else:
             f = slab(f2, x + 1)
         g0[x] = f + slab(corr, (x + 2) // 2)
@@ -425,7 +429,8 @@
 
 
 def exchange(first, second, axis):
-    return swap(first, axis, 1), swap(second, axis, 0)
+    groups = [[i, i + 1] for i in range(0, lax.axis_size(axis), 2)]
+    return swap(first, axis, 1), lax.all_gather(second, axis, axis_index_groups=groups)
 
 
 def body(g, b, n):

time: 49.1 us -> 46.6 us (0.949)
  the two profiles are of different devices: /device:TPU:25 before, /device:TPU:28 now
where the time goes in v3:
time: 46.6 us; the launch traced here: 46.4 us
  starting transfers between devices  26 us (56%)
  blocking collectives  15.1 us (32%)
  Pallas kernels  3.37 us (7%)
  waiting for transfers between devices  1.93 us (4%)
    ppermute x4, starting transfers between devices, swap(): return lax.ppermute(v, axis, pairs + [(j, i) for i, j in pairs])  26 us
    all_gather x4, blocking collectives, exchange(): lax.all_gather(second, axis, axis_index_groups=groups)  15.1 us
    pallas_call x5, Pallas kernels, call(): pl.pallas_call(kernel, out_shape=[make(s, F32) for s in outs], in_specs=[...  3.37 us
    ppermute x4, waiting for transfers between devices, swap(): return lax.ppermute(v, axis, pairs + [(j, i) for i, j in pairs])  1.93 us
  transfers between devices with their start and end apart: 4, of which 2 were waited for; matrix products, arithmetic and copies ran while one was open for 0% of the time, Pallas kernels for 0%

profile of v3, /device:TPU:28, one launch (start us, length us, event | category | flops | bytes accessed | tf_op | source)
XLA Modules:
  0.0 46.4 jit_solution(10604431095621030270)
XLA Ops:
  0.0 1.1 %shard_map.37 = (f32[112,256]{1,0:T(8,128)S(1)}, f32[112,256]{1,0:T(8,128)S(1)}, f32[8,16,256]{2,1,0:T(8,128)S(1)}, f32[8,16,256]{2,1,0:T(8,128)S(1)}, f32[8,16,...) custom-call(f32[8,16,256]{2,1,0:T(8,128)} %g_hbm.1, f32[8,16,256]{2,1,0:T(8,128)} %b_hbm.1, s32[8,16,256]{2,1,0:T(8,128)} %n_hbm.1), custom_call_target="tpu_custom_call" | custom-call | tf_op jit(solution)/shard_map/pallas_call | solution.py:18
  1.1 1.9 %collective-permute-start = (f32[112,256]{1,0:T(8,128)S(1)}, f32[112,256]{1,0:T(8,128)S(1)}, u32[]{:S(2)}, u32[]{:S(2)}) collective-permute-start(f32[112,256]{1,0:T(8,128)S(1)} %get-tuple-element.26), channel_id=1, source_target_pairs={{128,256},{384,512},{640,768},{256,128},{512,384},{768,640},{129,2... | collective-permute-start | bytes 344072 | tf_op jit(solution)/shard_map/ppermute | solution.py:428
  3.0 2.9 %all-gather = f32[224,256]{1,0:T(8,128)S(1)} all-gather(f32[112,256]{1,0:T(8,128)S(1)} %get-tuple-element.27), channel_id=2, replica_groups={{0,128},{256,384},{512,640},{768,896},{1,129},{257,385},{513,641},{769,..., dimensions={0}, use_global_device_ids=true | all-gather | bytes 344064 | tf_op jit(solution)/shard_map/all_gather | solution.py:433
  5.9 1.3 %collective-permute-done.left = f32[112,256]{1,0:T(8,128)S(1)} collective-permute-done((f32[112,256]{1,0:T(8,128)S(1)}, f32[112,256]{1,0:T(8,128)S(1)}, u32[]{:S(2)}, u32[]{:S(2)}) %collective-permute-start) | collective-permute-done | bytes 114720 | tf_op jit(solution)/shard_map/ppermute | solution.py:428
  7.2 0.2 shard_map.38
  7.4 18.9 %collective-permute-start.1 = (f32[40,256]{1,0:T(8,128)S(1)}, f32[40,256]{1,0:T(8,128)S(1)}, u32[]{:S(2)}, u32[]{:S(2)}) collective-permute-start(f32[40,256]{1,0:T(8,128)S(1)} %get-tuple-element.29), channel_id=1, source_target_pairs={{1,2},{3,4},{5,6},{7,8},{9,10},{11,12},{13,14},{15,16},{17,18},{19... | collective-permute-start | bytes 122888 | tf_op jit(solution)/shard_map/ppermute | solution.py:428
  26.3 4.7 %all-gather.1 = f32[80,256]{1,0:T(8,128)S(1)} all-gather(f32[40,256]{1,0:T(8,128)S(1)} %get-tuple-element.30), channel_id=3, replica_groups={{0,1},{2,3},{4,5},{6,7},{8,9},{10,11},{12,13},{14,15},{16,17},{18,19},{..., dimensions={0}, use_global_device_ids=true | all-gather | bytes 122880 | tf_op jit(solution)/shard_map/all_gather | solution.py:433
  31.0 0.0 collective-permute-done.1.first
  31.0 0.6 %shard_map.39 = (f32[160,256]{1,0:T(8,128)S(1)}, f32[8,256]{1,0:T(8,128)S(1)}, f32[8,256]{1,0:T(8,128)S(1)}, f32[32,128]{1,0:T(8,128)S(1)}, f32[32,128]{1,0:T(8,...) custom-call(f32[8,16,256]{2,1,0:T(8,128)S(1)} %get-tuple-element.28.g, f32[8,16,256]{2,1,0:T(8,128)S(1)} %get-tuple-element.24.b, ...), custom_call_target="tpu_custom_call" | custom-call | tf_op jit(solution)/shard_map/pallas_call | solution.py:18
  31.6 1.9 %collective-permute-start.2 = (f32[48,256]{1,0:T(8,128)S(1)}, f32[48,256]{1,0:T(8,128)S(1)}, u32[]{:S(2)}, u32[]{:S(2)}) collective-permute-start(f32[48,256]{1,0:T(8,128)S(1)} %get-tuple-element.38), channel_id=1, source_target_pairs={{128,256},{384,512},{640,768},{256,128},{512,384},{768,640},{129,2... | collective-permute-start | bytes 147464 | tf_op jit(solution)/shard_map/ppermute | solution.py:428
  33.5 2.8 %all-gather.2 = f32[96,256]{1,0:T(8,128)S(1)} all-gather(f32[48,256]{1,0:T(8,128)S(1)} %get-tuple-element.39), channel_id=4, replica_groups={{0,128},{256,384},{512,640},{768,896},{1,129},{257,385},{513,641},{769,..., dimensions={0}, use_global_device_ids=true | all-gather | bytes 147456 | tf_op jit(solution)/shard_map/all_gather | solution.py:433
  36.3 0.7 %collective-permute-done.2.left.cleft = f32[48,256]{1,0:T(8,128)S(1)} collective-permute-done((f32[48,256]{1,0:T(8,128)S(1)}, f32[48,256]{1,0:T(8,128)S(1)}, u32[]{:S(2)}, u32[]{:S(2)}) %collective-permute-start.2) | collective-permute-done | bytes 49184 | tf_op jit(solution)/shard_map/ppermute | solution.py:428
  37.0 0.2 shard_map.40
  37.1 3.3 %collective-permute-start.3 = (f32[72,128]{1,0:T(8,128)S(1)}, f32[72,128]{1,0:T(8,128)S(1)}, u32[]{:S(2)}, u32[]{:S(2)}) collective-permute-start(f32[72,128]{1,0:T(8,128)S(1)} %get-tuple-element.41), channel_id=1, source_target_pairs={{1,2},{3,4},{5,6},{7,8},{9,10},{11,12},{13,14},{15,16},{17,18},{19... | collective-permute-start | bytes 110600 | tf_op jit(solution)/shard_map/ppermute | solution.py:428
  40.5 4.6 %all-gather.3 = f32[144,128]{1,0:T(8,128)S(1)} all-gather(f32[72,128]{1,0:T(8,128)S(1)} %get-tuple-element.42), channel_id=5, replica_groups={{0,1},{2,3},{4,5},{6,7},{8,9},{10,11},{12,13},{14,15},{16,17},{18,19},{..., dimensions={0}, use_global_device_ids=true | all-gather | bytes 110592 | tf_op jit(solution)/shard_map/all_gather | solution.py:433
  45.1 0.0 collective-permute-done.3.one
  45.1 1.3 %shard_map.41 = f32[8,16,256]{2,1,0:T(8,128)} custom-call(f32[8,16,256]{2,1,0:T(8,128)S(1)} %get-tuple-element.24.b, f32[8,16,256]{2,1,0:T(8,128)S(1)} %get-tuple-element.25.w, f32[112,256]{1,0:T(8,128)S(1)} %collective-permute-done.left, f32[2,112,256]{2,1,0:T(8,128)S(1)} %bitcast.6, f32[40,256]{1,0:T(8,128)S(1)} %collective-permute-done.1.first, ...), custom_call_target="tpu_custom_call" | custom-call | tf_op jit(solution)/shard_map/pallas_call | solution.py:18
Async XLA Ops:
  1.1 6.1 %collective-permute-start = (f32[112,256]{1,0:T(8,128)S(1)}, f32[112,256]{1,0:T(8,128)S(1)}, u32[]{:S(2)}, u32[]{:S(2)}) collective-permute-start(f32[112,256]{1,0:T(8,128)S(1)} %get-tuple-element.26), channel_id=1, source_target_pairs={{128,256},{384,512},{640,768},{256,128},{512,384},{768,640},{129,2... | collective-permute-start | bytes 344072 | tf_op jit(solution)/shard_map/ppermute | solution.py:428
  7.4 23.5 %collective-permute-start.1 = (f32[40,256]{1,0:T(8,128)S(1)}, f32[40,256]{1,0:T(8,128)S(1)}, u32[]{:S(2)}, u32[]{:S(2)}) collective-permute-start(f32[40,256]{1,0:T(8,128)S(1)} %get-tuple-element.29), channel_id=1, source_target_pairs={{1,2},{3,4},{5,6},{7,8},{9,10},{11,12},{13,14},{15,16},{17,18},{19... | collective-permute-start | bytes 122888 | tf_op jit(solution)/shard_map/ppermute | solution.py:428
  31.6 5.4 %collective-permute-start.2 = (f32[48,256]{1,0:T(8,128)S(1)}, f32[48,256]{1,0:T(8,128)S(1)}, u32[]{:S(2)}, u32[]{:S(2)}) collective-permute-start(f32[48,256]{1,0:T(8,128)S(1)} %get-tuple-element.38), channel_id=1, source_target_pairs={{128,256},{384,512},{640,768},{256,128},{512,384},{768,640},{129,2... | collective-permute-start | bytes 147464 | tf_op jit(solution)/shard_map/ppermute | solution.py:428
  37.1 8.0 %collective-permute-start.3 = (f32[72,128]{1,0:T(8,128)S(1)}, f32[72,128]{1,0:T(8,128)S(1)}, u32[]{:S(2)}, u32[]{:S(2)}) collective-permute-start(f32[72,128]{1,0:T(8,128)S(1)} %get-tuple-element.41), channel_id=1, source_target_pairs={{1,2},{3,4},{5,6},{7,8},{9,10},{11,12},{13,14},{15,16},{17,18},{19... | collective-permute-start | bytes 110600 | tf_op jit(solution)/shard_map/ppermute | solution.py:428

commit v4 on v3

--- a/solution.py
+++ b/solution.py
@@ -118,16 +118,18 @@
         return self._get(2, 5, x)
 
 
-def give(both, first, second):
+def give(both, even, odd):
     p = side_of_dev()
-    first[...] = both[p]
-    second[...] = both[1 - p]
-
-
-def take(both, first, second):
+    even[...] = both[1 - p]
+    odd[...] = both[p]
+
+
+def take(both, even, odd):
     p = side_of_dev()
-    both[p] = first[...]
-    both[1 - p] = second[1 - p]
+    at = lax.axis_index("dev")
+    at_end = (at == 0) | (at == lax.axis_size("dev") - 1)
+    both[1 - p] = even[...]
+    both[p] = jnp.where(at_end, 0.0, odd[p])
 
 
 Y_G, Y_P, Y_W, Y_Q = 0, 12, 22, 32
@@ -428,9 +430,15 @@
     return lax.ppermute(v, axis, pairs + [(j, i) for i, j in pairs])
 
 
-def exchange(first, second, axis):
-    groups = [[i, i + 1] for i in range(0, lax.axis_size(axis), 2)]
-    return swap(first, axis, 1), lax.all_gather(second, axis, axis_index_groups=groups)
+def exchange_group(cross, chip):
+    groups = [[i, i + 1] for i in range(0, lax.axis_size("group"), 2)]
+    return swap(cross, "group", 1), lax.all_gather(chip, "group", axis_index_groups=groups)
+
+
+def exchange_dev(even, odd):
+    n = lax.axis_size("dev")
+    groups = [[i, (i + 1) % n] for i in range(1, n, 2)]
+    return swap(even, "dev", 0), lax.all_gather(odd, "dev", axis_index_groups=groups)
 
 
 def body(g, b, n):
@@ -443,28 +451,28 @@
         vmem=None,
         scratch=[pltpu.VMEM(block, jnp.int32), pltpu.SemaphoreType.DMA((3,))],
     )
-    left, right = exchange(cross, chip, "group")
+    left, right = exchange_group(cross, chip)
     first, second, f1z = call(
         pack_y_kernel,
         [(Y_ROWS, NZ)] * 2 + [(12 * BY, NZ)],
         g, b, w, left, right,
         scratch=[(2, Y_ROWS, NZ)],
     )
-    first, second = exchange(first, second, "dev")
+    first, second = exchange_dev(first, second)
     f2, f2low, f2high, c1, wc, cross, chip = call(
         middle_kernel,
         [(10 * BY, NZ), (BX, NZ), (BX, NZ), (CX * CY, CZ), (CX * CY, CZ), (X2_ROWS, NZ), (X2_ROWS, NZ)],
         g, b, w, d, left, right, f1z, first, second,
         scratch=[(2, Y_ROWS, NZ), (16, NZ), (2, 16, NZ), (8 * BY, CZ)],
     )
-    cleft, cright = exchange(cross, chip, "group")
+    cleft, cright = exchange_group(cross, chip)
     one, two, c2z = call(
         pack_c_kernel,
         [(Z_ROWS, CZ)] * 2 + [(10 * CY, CZ)],
         b, w, f2, c1, wc, cleft, cright,
         scratch=[(2, Z_ROWS, CZ)],
     )
-    one, two = exchange(one, two, "dev")
+    one, two = exchange_dev(one, two)
     (out,) = call(
         last_kernel,
         [block],

time: 46.6 us -> 50.3 us (1.079)
  the two profiles are of different devices: /device:TPU:28 before, /device:TPU:1 now
where the time goes in v4:
time: 50.3 us; the launch traced here: 50 us
  blocking collectives  34.1 us (68%)
  starting transfers between devices  12.5 us (25%)
  Pallas kernels  3.37 us (7%)
    all_gather x2, blocking collectives, exchange_dev(): lax.all_gather(odd, 'dev', axis_index_groups=groups)  20.3 us
    all_gather x2, blocking collectives, exchange_group(): lax.all_gather(chip, 'group', axis_index_groups=groups)  13.8 us
    ppermute x4, starting transfers between devices, swap(): return lax.ppermute(v, axis, pairs + [(j, i) for i, j in pairs])  12.5 us
    pallas_call x5, Pallas kernels, call(): pl.pallas_call(kernel, out_shape=[make(s, F32) for s in outs], in_specs=[...  3.37 us
  transfers between devices with their start and end apart: 4, of which 0 were waited for; matrix products, arithmetic and copies ran while one was open for 0% of the time, Pallas kernels for 0%

profile of v4, /device:TPU:1, one launch (start us, length us, event | category | flops | bytes accessed | tf_op | source)
XLA Modules:
  0.0 50.0 jit_solution(13391363695864929180)
XLA Ops:
  0.0 1.1 %shard_map.37 = (f32[112,256]{1,0:T(8,128)S(1)}, f32[112,256]{1,0:T(8,128)S(1)}, f32[8,16,256]{2,1,0:T(8,128)S(1)}, f32[8,16,256]{2,1,0:T(8,128)S(1)}, f32[8,16,...) custom-call(f32[8,16,256]{2,1,0:T(8,128)} %g_hbm.1, f32[8,16,256]{2,1,0:T(8,128)} %b_hbm.1, s32[8,16,256]{2,1,0:T(8,128)} %n_hbm.1), custom_call_target="tpu_custom_call" | custom-call | tf_op jit(solution)/shard_map/pallas_call | solution.py:18
  1.1 4.5 %collective-permute-start = (f32[112,256]{1,0:T(8,128)S(1)}, f32[112,256]{1,0:T(8,128)S(1)}, u32[]{:S(2)}, u32[]{:S(2)}) collective-permute-start(f32[112,256]{1,0:T(8,128)S(1)} %get-tuple-element.26), channel_id=1, source_target_pairs={{128,256},{384,512},{640,768},{256,128},{512,384},{768,640},{129,2... | collective-permute-start | bytes 344072 | tf_op jit(solution)/shard_map/ppermute | solution.py:430
  5.6 11.9 %all-gather = f32[224,256]{1,0:T(8,128)S(1)} all-gather(f32[112,256]{1,0:T(8,128)S(1)} %get-tuple-element.27), channel_id=2, replica_groups={{0,128},{256,384},{512,640},{768,896},{1,129},{257,385},{513,641},{769,..., dimensions={0}, use_global_device_ids=true | all-gather | bytes 344064 | tf_op jit(solution)/shard_map/all_gather | solution.py:435
  17.6 0.0 collective-permute-done.left
  17.6 0.2 shard_map.38
  17.8 1.9 %collective-permute-start.1 = (f32[40,256]{1,0:T(8,128)S(1)}, f32[40,256]{1,0:T(8,128)S(1)}, u32[]{:S(2)}, u32[]{:S(2)}) collective-permute-start(f32[40,256]{1,0:T(8,128)S(1)} %get-tuple-element.29), channel_id=1, source_target_pairs={{0,1},{2,3},{4,5},{6,7},{8,9},{10,11},{12,13},{14,15},{16,17},{18,... | collective-permute-start | bytes 122888 | tf_op jit(solution)/shard_map/ppermute | solution.py:430
  19.7 12.8 %all-gather.1 = f32[80,256]{1,0:T(8,128)S(1)} all-gather(f32[40,256]{1,0:T(8,128)S(1)} %get-tuple-element.30), channel_id=3, replica_groups={{1,2},{3,4},{5,6},{7,8},{9,10},{11,12},{13,14},{15,16},{17,18},{19,20},..., dimensions={0}, use_global_device_ids=true | all-gather | bytes 122880 | tf_op jit(solution)/shard_map/all_gather | solution.py:441
  32.5 0.0 collective-permute-done.1.first
  32.5 0.6 %shard_map.39 = (f32[160,256]{1,0:T(8,128)S(1)}, f32[8,256]{1,0:T(8,128)S(1)}, f32[8,256]{1,0:T(8,128)S(1)}, f32[32,128]{1,0:T(8,128)S(1)}, f32[32,128]{1,0:T(8,...) custom-call(f32[8,16,256]{2,1,0:T(8,128)S(1)} %get-tuple-element.28.g, f32[8,16,256]{2,1,0:T(8,128)S(1)} %get-tuple-element.24.b, ...), custom_call_target="tpu_custom_call" | custom-call | tf_op jit(solution)/shard_map/pallas_call | solution.py:18
  33.1 4.2 %collective-permute-start.2 = (f32[48,256]{1,0:T(8,128)S(1)}, f32[48,256]{1,0:T(8,128)S(1)}, u32[]{:S(2)}, u32[]{:S(2)}) collective-permute-start(f32[48,256]{1,0:T(8,128)S(1)} %get-tuple-element.38), channel_id=1, source_target_pairs={{128,256},{384,512},{640,768},{256,128},{512,384},{768,640},{129,2... | collective-permute-start | bytes 147464 | tf_op jit(solution)/shard_map/ppermute | solution.py:430
  37.3 1.9 %all-gather.2 = f32[96,256]{1,0:T(8,128)S(1)} all-gather(f32[48,256]{1,0:T(8,128)S(1)} %get-tuple-element.39), channel_id=4, replica_groups={{0,128},{256,384},{512,640},{768,896},{1,129},{257,385},{513,641},{769,..., dimensions={0}, use_global_device_ids=true | all-gather | bytes 147456 | tf_op jit(solution)/shard_map/all_gather | solution.py:435
  39.2 0.0 collective-permute-done.2.left.cleft
  39.2 0.2 shard_map.40
  39.4 1.9 %collective-permute-start.3 = (f32[72,128]{1,0:T(8,128)S(1)}, f32[72,128]{1,0:T(8,128)S(1)}, u32[]{:S(2)}, u32[]{:S(2)}) collective-permute-start(f32[72,128]{1,0:T(8,128)S(1)} %get-tuple-element.41), channel_id=1, source_target_pairs={{0,1},{2,3},{4,5},{6,7},{8,9},{10,11},{12,13},{14,15},{16,17},{18,... | collective-permute-start | bytes 110600 | tf_op jit(solution)/shard_map/ppermute | solution.py:430
  41.3 7.4 %all-gather.3 = f32[144,128]{1,0:T(8,128)S(1)} all-gather(f32[72,128]{1,0:T(8,128)S(1)} %get-tuple-element.42), channel_id=5, replica_groups={{1,2},{3,4},{5,6},{7,8},{9,10},{11,12},{13,14},{15,16},{17,18},{19,20},..., dimensions={0}, use_global_device_ids=true | all-gather | bytes 110592 | tf_op jit(solution)/shard_map/all_gather | solution.py:441
  48.7 0.0 collective-permute-done.3.one
  48.7 1.3 %shard_map.41 = f32[8,16,256]{2,1,0:T(8,128)} custom-call(f32[8,16,256]{2,1,0:T(8,128)S(1)} %get-tuple-element.24.b, f32[8,16,256]{2,1,0:T(8,128)S(1)} %get-tuple-element.25.w, f32[112,256]{1,0:T(8,128)S(1)} %collective-permute-done.left, f32[2,112,256]{2,1,0:T(8,128)S(1)} %bitcast.6, f32[40,256]{1,0:T(8,128)S(1)} %collective-permute-done.1.first, ...), custom_call_target="tpu_custom_call" | custom-call | tf_op jit(solution)/shard_map/pallas_call | solution.py:18
Async XLA Ops:
  1.1 16.4 %collective-permute-start = (f32[112,256]{1,0:T(8,128)S(1)}, f32[112,256]{1,0:T(8,128)S(1)}, u32[]{:S(2)}, u32[]{:S(2)}) collective-permute-start(f32[112,256]{1,0:T(8,128)S(1)} %get-tuple-element.26), channel_id=1, source_target_pairs={{128,256},{384,512},{640,768},{256,128},{512,384},{768,640},{129,2... | collective-permute-start | bytes 344072 | tf_op jit(solution)/shard_map/ppermute | solution.py:430
  17.8 14.8 %collective-permute-start.1 = (f32[40,256]{1,0:T(8,128)S(1)}, f32[40,256]{1,0:T(8,128)S(1)}, u32[]{:S(2)}, u32[]{:S(2)}) collective-permute-start(f32[40,256]{1,0:T(8,128)S(1)} %get-tuple-element.29), channel_id=1, source_target_pairs={{0,1},{2,3},{4,5},{6,7},{8,9},{10,11},{12,13},{14,15},{16,17},{18,... | collective-permute-start | bytes 122888 | tf_op jit(solution)/shard_map/ppermute | solution.py:430
  33.1 6.1 %collective-permute-start.2 = (f32[48,256]{1,0:T(8,128)S(1)}, f32[48,256]{1,0:T(8,128)S(1)}, u32[]{:S(2)}, u32[]{:S(2)}) collective-permute-start(f32[48,256]{1,0:T(8,128)S(1)} %get-tuple-element.38), channel_id=1, source_target_pairs={{128,256},{384,512},{640,768},{256,128},{512,384},{768,640},{129,2... | collective-permute-start | bytes 147464 | tf_op jit(solution)/shard_map/ppermute | solution.py:430
  39.4 9.3 %collective-permute-start.3 = (f32[72,128]{1,0:T(8,128)S(1)}, f32[72,128]{1,0:T(8,128)S(1)}, u32[]{:S(2)}, u32[]{:S(2)}) collective-permute-start(f32[72,128]{1,0:T(8,128)S(1)} %get-tuple-element.41), channel_id=1, source_target_pairs={{0,1},{2,3},{4,5},{6,7},{8,9},{10,11},{12,13},{14,15},{16,17},{18,... | collective-permute-start | bytes 110600 | tf_op jit(solution)/shard_map/ppermute | solution.py:430

commit v5 on v3

--- a/solution.py
+++ b/solution.py
@@ -11,9 +11,10 @@
 F32 = jnp.float32
 BX, BY, NZ = 8, 16, 256
 CX, CY, CZ = 4, 8, 128
-
-
-def call(kernel, outs, *args, scratch=(), hbm=0, hbm_out=False, vmem=8 * 2**20):
+RUN = 32
+
+
+def call(kernel, outs, *args, scratch=(), hbm=0, hbm_out=False, vmem=8 * 2**20, cost=None):
     make = jax.ShapeDtypeStruct if hbm_out else pltpu.VMEM
     return pl.pallas_call(
         kernel,
@@ -22,6 +23,7 @@
         out_specs=[VM] * len(outs),
         scratch_shapes=[pltpu.VMEM(s, F32) if isinstance(s, tuple) else s for s in scratch],
         compiler_params=pltpu.CompilerParams(vmem_limit_bytes=vmem),
+        cost_estimate=cost,
     )(*args)
 
 
@@ -60,6 +62,19 @@
     return jnp.where((a // 2 == b) if n > m else (a == b // 2), 1.0, 0.0).astype(F32)
 
 
+def lanes(v, index):
+    return jnp.take_along_axis(v, index, axis=1)
+
+
+def pair_z(v):
+    lane = lax.broadcasted_iota(jnp.int32, (v.shape[0], CZ), 1)
+    low, high = v[:, :CZ], v[:, CZ:]
+    low = low + pltpu.roll(low, CZ - 1, 1)
+    high = high + pltpu.roll(high, CZ - 1, 1)
+    index = (2 * lane) % CZ
+    return jnp.where(lane < CZ // 2, lanes(low, index), lanes(high, index))
+
+
 def diag_of(n):
     return 6.0 + 0.25 * n.astype(F32)
 
@@ -77,7 +92,12 @@
     return lax.axis_index("dev") % 2
 
 
-def load_kernel(g_hbm, b_hbm, n_hbm, cross, chip, g, b, w, d, n, sems):
+Y_G, Y_P, Y_W, Y_Q, Y_G2, Y_W2 = 0, 8, 16, 24, 32, 34
+Y_ROWS = 40
+X_ROWS = 7 * BY
+
+
+def load_kernel(g_hbm, b_hbm, n_hbm, cross, cross2, chip, even, even2, odd, f1z, g, b, w, d, n, both, sems):
     copies = [
         pltpu.make_async_copy(src, dst, sems.at[k])
         for k, (src, dst) in enumerate(((g_hbm, g), (b_hbm, b), (n_hbm, n)))
@@ -96,95 +116,118 @@
         for k in range(2):
             out[(3 + k) * BY : (4 + k) * BY, :] = w[place(layers[k])]
             out[(5 + k) * BY : (6 + k) * BY, :] = b[place(layers[k])]
+    zero = jnp.zeros((BY, NZ), F32)
+    for x in range(BX):
+        at = place(x)
+        here, wx, bx = g[at], w[at], b[at]
+        before = g[place(x - 1)] if x else zero
+        after = g[place(x + 1)] if x < BX - 1 else zero
+        f = KEEP * here + wx * (bx + before + after + beside_z(here) + beside_y(here, 0.0, 0.0))
+        f1z[x * BY : (x + 1) * BY, :] = f
+        for s, (y, inner) in enumerate(((0, 1), (BY - 1, BY - 2))):
+            rows = [
+                (Y_G + x, here[y : y + 1]),
+                (Y_P + x, f[y : y + 1]),
+                (Y_W + x, wx[y : y + 1]),
+                (Y_Q + x, wx[y : y + 1] * (bx[y : y + 1] + f[inner : inner + 1])),
+            ]
+            if x in (0, 7):
+                rows += [(Y_G2 + x // 7, here[inner : inner + 1]), (Y_W2 + x // 7, wx[inner : inner + 1])]
+            for k, v in rows:
+                both[s, k : k + 1, :] = v
+    p = side_of_dev()
+    cross2[...] = cross[...]
+    even[...] = both[1 - p]
+    even2[...] = both[1 - p]
+    odd[...] = both[p]
 
 
 class Wide:
     def __init__(self, g, b, w, left, right):
         self.own, self.left, self.right = (g, w, b), left, partner(right)
 
-    def _get(self, which, base, x):
+    def _get(self, which, base, x, y):
         if 0 <= x < BX:
-            return self.own[which][place(x)]
+            v = self.own[which]
+            return v[place(x)] if y is None else v[place(x), y : y + 1, :]
         ref, k = (self.left, -1 - x) if x < 0 else (self.right, x - BX)
-        return slab(ref, base + k)
-
-    def guess(self, x):
-        return self._get(0, 0, x)
-
-    def w(self, x):
-        return self._get(1, 3, x)
-
-    def rhs(self, x):
-        return self._get(2, 5, x)
-
-
-def give(both, first, second):
+        return slab(ref, base + k) if y is None else row(ref, (base + k) * BY + y)
+
+    def guess(self, x, y=None):
+        return self._get(0, 0, x, y)
+
+    def w(self, x, y=None):
+        return self._get(1, 3, x, y)
+
+    def rhs(self, x, y=None):
+        return self._get(2, 5, x, y)
+
+
+def take(both, even, odd):
     p = side_of_dev()
-    first[...] = both[p]
-    second[...] = both[1 - p]
-
-
-def take(both, first, second):
+    both[1 - p] = even
+    both[p] = odd
+
+
+def gather_kernel(cross, even, odd, left, both):
+    left[...] = cross[...]
+    take(both, even[...], odd[...])
+
+
+X2_D = 3 * BY
+X2_ROWS = X2_D + 16
+
+
+def diagonal_rows(edge):
+    at, inner = (0, 1) if edge == 0 else (7, 6)
+    return (Y_G + at, Y_G2 + edge, Y_G + inner, Y_P + at, Y_W + at, Y_W2 + edge, Y_W + inner)
+
+
+def middle_kernel(
+    g, b, w, d, left1, cross2, chip, f1z, both1, even2,
+    f2, f2low, f2high, c1, wc, left, both, lo, hi, col, line, sums,
+):
+    left[...] = left1[...] + cross2[...]
+    a = Wide(g, b, w, left, chip)
     p = side_of_dev()
-    both[p] = first[...]
-    both[1 - p] = second[1 - p]
-
-
-Y_G, Y_P, Y_W, Y_Q = 0, 12, 22, 32
-Y_ROWS = 40
-
-
-def pack_y_kernel(g, b, w, left, right, first, second, f1z, both):
-    a = Wide(g, b, w, left, right)
-    lo, hi = both.at[0], both.at[1]
-    for x in range(-2, 10):
-        here = a.guess(x)
-        f = KEEP * here + a.w(x) * (
-            a.rhs(x) + a.guess(x - 1) + a.guess(x + 1) + beside_z(here) + beside_y(here, 0.0, 0.0)
-        )
-        f1z[(x + 2) * BY : (x + 3) * BY, :] = f
-        for out, y, inner in ((lo, 0, 1), (hi, BY - 1, BY - 2)):
-            k = Y_G + x + 2
-            out[k : k + 1, :] = here[y : y + 1]
-            if -1 <= x <= 8:
-                k = Y_P + x + 1
-                out[k : k + 1, :] = f[y : y + 1]
-                k = Y_W + x + 1
-                out[k : k + 1, :] = a.w(x)[y : y + 1]
-            if 0 <= x <= 7:
-                k = Y_Q + x
-                out[k : k + 1, :] = a.w(x)[y : y + 1] * (a.rhs(x)[y : y + 1] + f[inner : inner + 1])
-    give(both, first, second)
-
-
-X2_ROWS = 3 * BY
-
-
-def middle_kernel(
-    g, b, w, d, left, right, f1z, first, second, f2, f2low, f2high, c1, wc, lo, hi, both, col, line, sums
-):
-    a = Wide(g, b, w, left, right)
-    take(both, first, second)
+    both[p] = both1[p]
+    both[1 - p] = both1[1 - p] + even2[...]
     low, high = both.at[0], both.at[1]
     rows = lax.broadcasted_iota(jnp.int32, (BY, NZ), 0)
     f1 = {}
     for x in range(-2, 10):
-        k = Y_G + x + 2
-        beyond = jnp.where(rows == 0, row(low, k), jnp.where(rows == BY - 1, row(high, k), 0.0))
-        f1[x] = slab(f1z, x + 2) + a.w(x) * beyond
+        if 0 <= x < BX:
+            k = Y_G + x
+            beyond = jnp.where(rows == 0, row(low, k), jnp.where(rows == BY - 1, row(high, k), 0.0))
+            if x == 0:
+                beyond = beyond + a.guess(-1)
+            if x == BX - 1:
+                beyond = beyond + a.guess(BX)
+            f1[x] = slab(f1z, x) + a.w(x) * beyond
+        else:
+            here = a.guess(x)
+            f1[x] = KEEP * here + a.w(x) * (
+                a.rhs(x) + a.guess(x - 1) + a.guess(x + 1) + beside_z(here) + beside_y(here, 0.0, 0.0)
+            )
     for s, (side, y, out) in enumerate(((low, 0, f2low), (high, BY - 1, f2high))):
-        for x in range(-1, 9):
-            col[x + 1 : x + 2, :] = a.guess(x)[y : y + 1]
-        line[s, 0:10, :] = side[Y_P : Y_P + 10, :] + side[Y_W : Y_W + 10, :] * col[0:10, :]
-        for x in range(0, 8):
+        for x in range(BX):
+            col[x : x + 1, :] = a.guess(x, y)
+        line[s, 0:16, :] = jnp.zeros((16, NZ), F32)
+        line[s, 1:9, :] = side[Y_P : Y_P + 8, :] + side[Y_W : Y_W + 8, :] * col[0:8, :]
+        for x in range(BX):
             col[x : x + 1, :] = f1[x][y : y + 1]
         mid = line[s, 1:9, :]
         out[...] = (
             KEEP * mid
             + side[Y_Q : Y_Q + 8, :]
-            + side[Y_W + 1 : Y_W + 9, :]
-            * (line[s, 0:8, :] + line[s, 2:10, :] + beside_z(mid) + col[0:8, :])
-        )
+            + side[Y_W : Y_W + 8, :] * (line[s, 0:8, :] + line[s, 2:10, :] + beside_z(mid) + col[0:8, :])
+        )
+        for edge, pack in enumerate((lo, hi)):
+            for k, r in enumerate(diagonal_rows(edge)):
+                at = X2_D + 7 * s + k
+                pack[at : at + 1, :] = row(side, r)
+    for pack in (lo, hi):
+        pack[X2_D + 14 :, :] = jnp.zeros((2, NZ), F32)
     sec = {}
     for x in range(-1, 9):
         f = f1[x]
@@ -196,8 +239,8 @@
             + beside_y(f, line[0, x + 1 : x + 2, :], line[1, x + 1 : x + 2, :])
         )
         f2[(x + 1) * BY : (x + 2) * BY, :] = sec[x]
-    lo[2 * BY :, :] = sec[1]
-    hi[2 * BY :, :] = sec[6]
+    lo[2 * BY : X2_D, :] = sec[1]
+    hi[2 * BY : X2_D, :] = sec[6]
     pairs, points = [], []
     for x in range(0, 8):
         f = sec[x]
@@ -237,29 +280,88 @@
 
 
 class Coarse:
-    def __init__(self, c1, wc, left, right):
-        self.c1, self.wc, self.left, self.right = c1, wc, left, partner(right)
-
-    def _get(self, x, own, lanes):
+    def __init__(self, c1x, wc, left, right):
+        self.c1x, self.wc, self.left, self.right = c1x, wc, left, right
+
+    def first(self, x):
+        return slab(self.c1x, x + CX, CY)
+
+    def w(self, x):
         if 0 <= x < CX:
-            return slab(own, x, CY)
+            return slab(self.wc, x, CY)
         ref, k = (self.left, -1 - x) if x < 0 else (self.right, x - CX)
-        return ref[k * CY : (k + 1) * CY, lanes]
-
-    def first(self, x):
-        return self._get(x, self.c1, slice(0, CZ))
-
-    def w(self, x):
-        return self._get(x, self.wc, slice(CZ, 2 * CZ))
+        return ref[k * CY : (k + 1) * CY, CZ:]
+
+
+def corner_terms(a, low, high, relays, put):
+    for e, (xe, xi, xn, xm) in enumerate(((0, 1, -1, -2), (7, 6, 8, 9))):
+        for s, (side, y, yi) in enumerate(((low, 0, 1), (high, BY - 1, BY - 2))):
+            own = [row(side, r) for r in diagonal_rows(e)]
+            far = [row(relays[e], X2_D + 7 * s + k) for k in range(7)]
+            corner, beside = a.guess(xe, y), a.guess(xn, y)
+            w_corner, w_beside = a.w(xe, y), a.w(xn, y)
+            put(2 * e + s, far[:5] + [beside + own[0], w_beside, a.w(xm, y), a.w(xn, yi), own[4], own[5], own[6], w_corner])
+            put(4 + 2 * e + s, own[:5] + [corner + far[0], w_corner, a.w(xi, y), a.w(xe, yi), far[4], far[5], far[6], w_beside])
+
+
+def corner_sums(t):
+    g1, g2, g3, part, wd, near, wx, wx2, wxs, wy, wy2, wys, wq = (t[k] for k in range(13))
+    dq = jnp.where(wq > 0.0, OMEGA / jnp.where(wq > 0.0, wq, 1.0), 0.0)
+    by_y = wy * g1
+    by_x = wx * g1
+    diagonal = part + wd * near
+    at_q = wq * (by_x + by_y)
+    at_y = KEEP * by_y + wy * (beside_z(by_y) + diagonal + wy2 * g2)
+    at_x = KEEP * by_x + wx * (beside_z(by_x) + diagonal + wx2 * g3)
+    at_ys = wys * by_y
+    at_xs = wxs * by_x
+    total = at_y + at_x + beside_z(at_q) - dq * at_q + 2.0 * at_q + at_ys + at_xs
+    return at_q, at_y, at_x, at_ys, at_xs, 0.5 * pair_z(total)
 
 
 Z_C, Z_P, Z_W, Z_Q, Z_R, Z_V, Z_S, Z_K = 0, 10, 20, 30, 38, 44, 50, 66
 Z_ROWS = 72
 
 
-def pack_c_kernel(b, w, f2, c1, wc, left, right, one, two, c2z, both):
-    a = Coarse(c1, wc, left, right)
-    lo, hi = both.at[0], both.at[1]
+def pack_c_kernel(
+    g, b, w, left, chip, both, f2in, f2lowin, f2highin, c1, wc, cleft, cchip,
+    even, even2, odd, f2, f2low, f2high, c1x, c2z, table, terms, rows, sides,
+):
+    fine = Wide(g, b, w, left, chip)
+    cright = partner(cchip)
+
+    def put(i, values):
+        for k, v in enumerate(values):
+            table[k, i : i + 1, :] = v
+
+    corner_terms(fine, both.at[0], both.at[1], (cleft, cright), put)
+    *parts, share = corner_sums(table)
+    for k, v in enumerate(parts):
+        terms[k] = v
+    rows[...] = share
+    a = Coarse(c1x, wc, cleft, cright)
+    for x in range(CX):
+        c1x[(x + CX) * CY : (x + CX + 1) * CY, :] = slab(c1, x, CY)
+        c1x[(CX - 1 - x) * CY : (CX - x) * CY, :] = cleft[x * CY : (x + 1) * CY, 0:CZ]
+        c1x[(x + 2 * CX) * CY : (x + 2 * CX + 1) * CY, :] = cright[x * CY : (x + 1) * CY, 0:CZ]
+    f2[...] = f2in[...]
+    f2low[...] = f2lowin[...]
+    f2high[...] = f2highin[...]
+
+    def add(ref, k, v):
+        ref[k : k + 1, :] = ref[k : k + 1, :] + v
+
+    for e, (xe, xi, xn, cxe, cxn) in enumerate(((0, 1, -1, 0, -1), (7, 6, 8, 3, 4))):
+        for s, (side, y, yi, cy) in enumerate(((f2low, 0, 1, 0), (f2high, BY - 1, BY - 2, CY - 1))):
+            i = 2 * e + s
+            add(f2, (xe + 1) * BY + y, terms[0, i : i + 1, :])
+            add(side, xe, terms[1, i : i + 1, :])
+            add(f2, (xn + 1) * BY + y, terms[2, i : i + 1, :])
+            add(side, xi, terms[3, i : i + 1, :])
+            add(f2, (xn + 1) * BY + yi, terms[4, i : i + 1, :])
+            add(c1x, (cxe + CX) * CY + cy, a.w(cxe)[cy : cy + 1] * rows[i : i + 1, :])
+            add(c1x, (cxn + CX) * CY + cy, a.w(cxn)[cy : cy + 1] * rows[i + 4 : i + 5, :])
+    lo, hi = sides.at[0], sides.at[1]
     second = {}
     for x in range(-3, 7):
         c, cw = a.first(x), a.w(x)
@@ -288,8 +390,7 @@
     for out, y, inner in ((lo, 0, 1), (hi, BY - 1, BY - 2)):
         for x in range(BX):
             at = (x + 1) * BY
-            at_x = place(x)
-            v = w[at_x][y : y + 1] * (b[at_x][y : y + 1] + f2[at + inner : at + inner + 1, :])
+            v = fine.w(x, y) * (fine.rhs(x, y) + row(f2, at + inner))
             for half in range(2):
                 k = Z_S + 2 * x + half
                 out[k : k + 1, :] = v[:, half * CZ : (half + 1) * CZ]
@@ -299,17 +400,19 @@
             for half in range(2):
                 k = Z_K + 2 * j + half
                 out[k : k + 1, :] = v[:, half * CZ : (half + 1) * CZ]
-    give(both, one, two)
+    p = side_of_dev()
+    even[...] = sides[1 - p]
+    even2[...] = sides[1 - p]
+    odd[...] = sides[p]
 
 
 def last_kernel(
-    b, w, left, right, first, second, f2, f2low, f2high, c1, wc, cleft, cright, c2z, one, two,
-    out, both, cboth, col, line, line3, fine, corr, col2, s1, gline, g1line,
+    g, b, w, left, chip, both, f2, f2low, f2high, c1x, wc, cleft, cchip, c2z, even1, odd, even2,
+    out, cboth, col, line, line3, fine, corr, col2, s1, gline, g1line,
 ):
-    a = Coarse(c1, wc, cleft, cright)
-    wide = Wide(None, b, w, left, right)
-    take(both, first, second)
-    take(cboth, one, two)
+    wide = Wide(g, b, w, left, chip)
+    a = Coarse(c1x, wc, cleft, partner(cchip))
+    take(cboth, even1[...] + even2[...], odd[...])
     low, high, clow, chigh = both.at[0], both.at[1], cboth.at[0], cboth.at[1]
     crow = lax.broadcasted_iota(jnp.int32, (CY, CZ), 0)
     c2 = {}
@@ -399,7 +502,7 @@
         g1line[s, 0:8, :] = (
             KEEP * mid
             + s1[0:8, :]
-            + side[Y_W + 1 : Y_W + 9, :]
+            + side[Y_W : Y_W + 8, :]
             * (moved + gline[s, 0:8, :] + gline[s, 2:10, :] + beside_z(mid) + col2[0:8, :])
         )
     g1 = {}
@@ -423,54 +526,80 @@
         )
 
 
-def swap(v, axis, start):
-    pairs = [(i, i + 1) for i in range(start, lax.axis_size(axis) - 1, 2)]
-    return lax.ppermute(v, axis, pairs + [(j, i) for i, j in pairs])
-
-
-def exchange(first, second, axis):
-    groups = [[i, i + 1] for i in range(0, lax.axis_size(axis), 2)]
-    return swap(first, axis, 1), lax.all_gather(second, axis, axis_index_groups=groups)
+def swap(v, pairs):
+    n = lax.axis_size("dev")
+    links = [(i * n + j, k * n + l) for (i, j), (k, l) in pairs]
+    return lax.ppermute(v, ("group", "dev"), links + [(j, i) for i, j in links])
+
+
+def share_chip(v):
+    groups = [[i, i + 1] for i in range(0, lax.axis_size("group"), 2)]
+    return lax.all_gather(v, "group", axis_index_groups=groups)
+
+
+def cross_pairs(keep):
+    devs = [d for d in range(lax.axis_size("dev")) if keep(d)]
+    return [((i, d), (i + 1, d)) for i in range(1, lax.axis_size("group") - 1, 2) for d in devs]
+
+
+def dev_pairs(start, keep):
+    devs = [d for d in range(start, lax.axis_size("dev") - 1, 2) if keep(d)]
+    return [((i, d), (i, d + 1)) for i in range(lax.axis_size("group")) for d in devs]
+
+
+def is_end(d):
+    return d % RUN == RUN - 1
+
+
+def before_end(d):
+    return d % RUN == RUN - 2
 
 
 def body(g, b, n):
     block = (BX, BY, NZ)
-    cross, chip, g, b, w, d = call(
+    cross, cross2, chip, even, even2, odd, f1z, g, b, w, d = call(
         load_kernel,
-        [(7 * BY, NZ)] * 2 + [block] * 4,
+        [(X_ROWS, NZ)] * 3 + [(Y_ROWS, NZ)] * 3 + [(BX * BY, NZ)] + [block] * 4,
         g, b, n,
         hbm=3,
         vmem=None,
-        scratch=[pltpu.VMEM(block, jnp.int32), pltpu.SemaphoreType.DMA((3,))],
+        scratch=[pltpu.VMEM(block, jnp.int32), (2, Y_ROWS, NZ), pltpu.SemaphoreType.DMA((3,))],
     )
-    left, right = exchange(cross, chip, "group")
-    first, second, f1z = call(
-        pack_y_kernel,
-        [(Y_ROWS, NZ)] * 2 + [(12 * BY, NZ)],
-        g, b, w, left, right,
-        scratch=[(2, Y_ROWS, NZ)],
+    cross1 = swap(cross, cross_pairs(lambda d: not is_end(d)))
+    even1 = swap(even, dev_pairs(0, lambda d: not before_end(d)))
+    odd = swap(odd, dev_pairs(1, lambda d: True))
+    cross2 = swap(cross2, cross_pairs(is_end))
+    even2 = swap(even2, dev_pairs(0, before_end))
+    chip = share_chip(chip)
+    left, both = call(
+        gather_kernel,
+        [(X_ROWS, NZ), (2, Y_ROWS, NZ)],
+        cross1, even1, odd,
+        cost=pl.CostEstimate(flops=2**34, bytes_accessed=2**28, transcendentals=0),
     )
-    first, second = exchange(first, second, "dev")
-    f2, f2low, f2high, c1, wc, cross, chip = call(
+    f2, f2low, f2high, c1, wc, left, both, cross, near = call(
         middle_kernel,
-        [(10 * BY, NZ), (BX, NZ), (BX, NZ), (CX * CY, CZ), (CX * CY, CZ), (X2_ROWS, NZ), (X2_ROWS, NZ)],
-        g, b, w, d, left, right, f1z, first, second,
-        scratch=[(2, Y_ROWS, NZ), (16, NZ), (2, 16, NZ), (8 * BY, CZ)],
+        [(10 * BY, NZ), (BX, NZ), (BX, NZ), (CX * CY, CZ), (CX * CY, CZ), (X_ROWS, NZ), (2, Y_ROWS, NZ)] + [(X2_ROWS, NZ)] * 2,
+        g, b, w, d, left, cross2, chip, f1z, both, even2,
+        scratch=[(16, NZ), (2, 16, NZ), (8 * BY, CZ)],
     )
-    cleft, cright = exchange(cross, chip, "group")
-    one, two, c2z = call(
+    cleft = swap(cross, cross_pairs(lambda d: True))
+    cchip = share_chip(near)
+    even, even2, odd, f2, f2low, f2high, c1x, c2z = call(
         pack_c_kernel,
-        [(Z_ROWS, CZ)] * 2 + [(10 * CY, CZ)],
-        b, w, f2, c1, wc, cleft, cright,
-        scratch=[(2, Z_ROWS, CZ)],
+        [(Z_ROWS, CZ)] * 3 + [(10 * BY, NZ), (BX, NZ), (BX, NZ), (3 * CX * CY, CZ), (10 * CY, CZ)],
+        g, b, w, left, chip, both, f2, f2low, f2high, c1, wc, cleft, cchip,
+        scratch=[(13, 8, NZ), (5, 8, NZ), (8, CZ), (2, Z_ROWS, CZ)],
     )
-    one, two = exchange(one, two, "dev")
+    even1 = swap(even, dev_pairs(0, lambda d: not before_end(d)))
+    odd = swap(odd, dev_pairs(1, lambda d: True))
+    even2 = swap(even2, dev_pairs(0, before_end))
     (out,) = call(
         last_kernel,
         [block],
-        b, w, left, right, first, second, f2, f2low, f2high, c1, wc, cleft, cright, c2z, one, two,
+        g, b, w, left, chip, both, f2, f2low, f2high, c1x, wc, cleft, cchip, c2z, even1, odd, even2,
         scratch=[
-            (2, Y_ROWS, NZ), (2, Z_ROWS, CZ),
+            (2, Z_ROWS, CZ),
             (16, CZ), (2, 16, CZ), (2, 8, CZ), (6 * BY + 16, CZ), (6 * BY + 16, NZ), (16, NZ), (8, NZ), (2, 16, NZ), (2, 8, NZ),
         ],
         hbm_out=True,

time: 46.6 us -> 48.4 us (1.039)
  the two profiles are of different devices: /device:TPU:28 before, /device:TPU:25 now
where the time goes in v5:
time: 48.4 us; the launch traced here: 47.6 us
  starting transfers between devices  38.3 us (79%)
  blocking collectives  4.46 us (9%)
  Pallas kernels  3.7 us (8%)
  waiting for transfers between devices  0.98 us (2%)
    ppermute x9, starting transfers between devices, swap(): return lax.ppermute(v, ('group', 'dev'), links + [(j, i) for i, j in links])  38.3 us
    all_gather x2, blocking collectives, share_chip(): return lax.all_gather(v, 'group', axis_index_groups=groups)  4.46 us
    pallas_call x5, Pallas kernels, call(): pl.pallas_call(kernel, out_shape=[make(s, F32) for s in outs], in_specs=[...  3.7 us
    ppermute x9, waiting for transfers between devices, swap(): return lax.ppermute(v, ('group', 'dev'), links + [(j, i) for i, j in links])  0.98 us
  transfers between devices with their start and end apart: 9, of which 2 were waited for; matrix products, arithmetic and copies ran while one was open for 0% of the time, Pallas kernels for 0%

profile of v5, /device:TPU:25, one launch (start us, length us, event | category | flops | bytes accessed | tf_op | source)
XLA Modules:
  0.0 47.6 jit_solution(8650795259124566583)
XLA Ops:
  0.0 1.3 %shard_map.37 = (f32[112,256]{1,0:T(8,128)S(1)}, f32[112,256]{1,0:T(8,128)S(1)}, f32[112,256]{1,0:T(8,128)S(1)}, f32[40,256]{1,0:T(8,128)S(1)}, f32[40,256]{1,0:...) custom-call(f32[8,16,256]{2,1,0:T(8,128)} %g_hbm.1, ...), custom_call_target="tpu_custom_call" | custom-call | tf_op jit(solution)/shard_map/pallas_call | solution.py:19
  1.3 3.7 %collective-permute-start = (f32[112,256]{1,0:T(8,128)S(1)}, f32[112,256]{1,0:T(8,128)S(1)}, u32[]{:S(2)}, u32[]{:S(2)}) collective-permute-start(f32[112,256]{1,0:T(8,128)S(1)} %get-tuple-element.39), channel_id=1, source_target_pairs={{128,256},{129,257},{130,258},{131,259},{132,260},{133,261},{134,2... | collective-permute-start | bytes 344072 | tf_op jit(solution)/shard_map/ppermute | solution.py:532
  5.0 3.5 %collective-permute-start.1 = (f32[40,256]{1,0:T(8,128)S(1)}, f32[40,256]{1,0:T(8,128)S(1)}, u32[]{:S(2)}, u32[]{:S(2)}) collective-permute-start(f32[40,256]{1,0:T(8,128)S(1)} %get-tuple-element.40), channel_id=1, source_target_pairs={{0,1},{2,3},{4,5},{6,7},{8,9},{10,11},{12,13},{14,15},{16,17},{18,... | collective-permute-start | bytes 122888 | tf_op jit(solution)/shard_map/ppermute | solution.py:532
  8.5 12.7 %collective-permute-start.2 = (f32[40,256]{1,0:T(8,128)S(1)}, f32[40,256]{1,0:T(8,128)S(1)}, u32[]{:S(2)}, u32[]{:S(2)}) collective-permute-start(f32[40,256]{1,0:T(8,128)S(1)} %get-tuple-element.41), channel_id=1, source_target_pairs={{1,2},{3,4},{5,6},{7,8},{9,10},{11,12},{13,14},{15,16},{17,18},{19... | collective-permute-start | bytes 122888 | tf_op jit(solution)/shard_map/ppermute | solution.py:532
  21.2 0.7 %collective-permute-start.4 = (f32[40,256]{1,0:T(8,128)S(1)}, f32[40,256]{1,0:T(8,128)S(1)}, u32[]{:S(2)}, u32[]{:S(2)}) collective-permute-start(f32[40,256]{1,0:T(8,128)S(1)} %get-tuple-element.47), channel_id=1, source_target_pairs={{30,31},{62,63},{94,95},{126,127},{158,159},{190,191},{222,223},{2... | collective-permute-start | bytes 122888 | tf_op jit(solution)/shard_map/ppermute | solution.py:532
  21.9 0.7 %collective-permute-start.3 = (f32[112,256]{1,0:T(8,128)S(1)}, f32[112,256]{1,0:T(8,128)S(1)}, u32[]{:S(2)}, u32[]{:S(2)}) collective-permute-start(f32[112,256]{1,0:T(8,128)S(1)} %get-tuple-element.43), channel_id=1, source_target_pairs={{159,287},{191,319},{223,351},{255,383},{415,543},{447,575},{479,6... | collective-permute-start | bytes 344072 | tf_op jit(solution)/shard_map/ppermute | solution.py:532
  22.6 2.6 %all-gather = f32[224,256]{1,0:T(8,128)S(1)} all-gather(f32[112,256]{1,0:T(8,128)S(1)} %get-tuple-element.44), channel_id=2, replica_groups={{0,128},{256,384},{512,640},{768,896},{1,129},{257,385},{513,641},{769,..., dimensions={0}, use_global_device_ids=true | all-gather | bytes 344064 | tf_op jit(solution)/shard_map/all_gather | solution.py:537
  25.1 0.0 collective-permute-done.1.even
  25.1 0.0 collective-permute-done.2.odd
  25.1 0.0 collective-permute-done.cross
  25.2 0.0 collective-permute-done.4.even2
  25.2 0.0 collective-permute-done.3.cross2
  25.2 0.6 %shard_map.39 = (f32[160,256]{1,0:T(8,128)S(1)}, f32[8,256]{1,0:T(8,128)S(1)}, f32[8,256]{1,0:T(8,128)S(1)}, f32[32,128]{1,0:T(8,128)S(1)}, f32[32,128]{1,0:T(8,...) custom-call(f32[8,16,256]{2,1,0:T(8,128)S(1)} %get-tuple-element.35., ...), custom_call_target="tpu_custom_call" | custom-call | tf_op jit(solution)/shard_map/pallas_call | solution.py:19
  25.8 3.4 %collective-permute-start.5 = (f32[64,256]{1,0:T(8,128)S(1)}, f32[64,256]{1,0:T(8,128)S(1)}, u32[]{:S(2)}, u32[]{:S(2)}) collective-permute-start(f32[64,256]{1,0:T(8,128)S(1)} %get-tuple-element.55), channel_id=1, source_target_pairs={{128,256},{129,257},{130,258},{131,259},{132,260},{133,261},{134,2... | collective-permute-start | bytes 196616 | tf_op jit(solution)/shard_map/ppermute | solution.py:532
  29.2 1.9 %all-gather.1 = f32[128,256]{1,0:T(8,128)S(1)} all-gather(f32[64,256]{1,0:T(8,128)S(1)} %get-tuple-element.56), channel_id=3, replica_groups={{0,128},{256,384},{512,640},{768,896},{1,129},{257,385},{513,641},{769,..., dimensions={0}, use_global_device_ids=true | all-gather | bytes 196608 | tf_op jit(solution)/shard_map/all_gather | solution.py:537
  31.1 0.3 collective-permute-done.5.cleft
  31.4 0.4 shard_map.40
  31.9 1.9 %collective-permute-start.6 = (f32[72,128]{1,0:T(8,128)S(1)}, f32[72,128]{1,0:T(8,128)S(1)}, u32[]{:S(2)}, u32[]{:S(2)}) collective-permute-start(f32[72,128]{1,0:T(8,128)S(1)} %get-tuple-element.62), channel_id=1, source_target_pairs={{0,1},{2,3},{4,5},{6,7},{8,9},{10,11},{12,13},{14,15},{16,17},{18,... | collective-permute-start | bytes 110600 | tf_op jit(solution)/shard_map/ppermute | solution.py:532
  33.8 11.1 %collective-permute-start.7 = (f32[72,128]{1,0:T(8,128)S(1)}, f32[72,128]{1,0:T(8,128)S(1)}, u32[]{:S(2)}, u32[]{:S(2)}) collective-permute-start(f32[72,128]{1,0:T(8,128)S(1)} %get-tuple-element.63), channel_id=1, source_target_pairs={{1,2},{3,4},{5,6},{7,8},{9,10},{11,12},{13,14},{15,16},{17,18},{19... | collective-permute-start | bytes 110600 | tf_op jit(solution)/shard_map/ppermute | solution.py:532
  44.9 0.7 %collective-permute-start.8 = (f32[72,128]{1,0:T(8,128)S(1)}, f32[72,128]{1,0:T(8,128)S(1)}, u32[]{:S(2)}, u32[]{:S(2)}) collective-permute-start(f32[72,128]{1,0:T(8,128)S(1)} %get-tuple-element.64), channel_id=1, source_target_pairs={{30,31},{62,63},{94,95},{126,127},{158,159},{190,191},{222,223},{2... | collective-permute-start | bytes 110600 | tf_op jit(solution)/shard_map/ppermute | solution.py:532
  45.6 0.0 collective-permute-done.6.even1
  45.6 0.7 %collective-permute-done.7.odd = f32[72,128]{1,0:T(8,128)S(1)} collective-permute-done((f32[72,128]{1,0:T(8,128)S(1)}, f32[72,128]{1,0:T(8,128)S(1)}, u32[]{:S(2)}, u32[]{:S(2)}) %collective-permute-start.7) | collective-permute-done | bytes 36896 | tf_op jit(solution)/shard_map/ppermute | solution.py:532
  46.3 0.0 collective-permute-done.8.even2
  46.3 1.3 %shard_map.41 = f32[8,16,256]{2,1,0:T(8,128)} custom-call(f32[8,16,256]{2,1,0:T(8,128)S(1)} %get-tuple-element.35.g, f32[8,16,256]{2,1,0:T(8,128)S(1)} %get-tuple-element.36.b, f32[8,16,256]{2,1,0:T(8,128)S(1)} %get-tuple-element.37.w, f32[112,256]{1,0:T(8,128)S(1)} %get-tuple-element.48.left, f32[2,112,256]{2,1,0:T(8,128)S(1)} %bitcast.4, ...), custom_call_target="tpu_custom_call" | custom-call | tf_op jit(solution)/shard_map/pallas_call | solution.py:19
  (1 shorter events, 0.0 us)
Async XLA Ops:
  1.3 23.9 %collective-permute-start = (f32[112,256]{1,0:T(8,128)S(1)}, f32[112,256]{1,0:T(8,128)S(1)}, u32[]{:S(2)}, u32[]{:S(2)}) collective-permute-start(f32[112,256]{1,0:T(8,128)S(1)} %get-tuple-element.39), channel_id=1, source_target_pairs={{128,256},{129,257},{130,258},{131,259},{132,260},{133,261},{134,2... | collective-permute-start | bytes 344072 | tf_op jit(solution)/shard_map/ppermute | solution.py:532
  5.0 20.2 %collective-permute-start.1 = (f32[40,256]{1,0:T(8,128)S(1)}, f32[40,256]{1,0:T(8,128)S(1)}, u32[]{:S(2)}, u32[]{:S(2)}) collective-permute-start(f32[40,256]{1,0:T(8,128)S(1)} %get-tuple-element.40), channel_id=1, source_target_pairs={{0,1},{2,3},{4,5},{6,7},{8,9},{10,11},{12,13},{14,15},{16,17},{18,... | collective-permute-start | bytes 122888 | tf_op jit(solution)/shard_map/ppermute | solution.py:532
  8.5 16.6 %collective-permute-start.2 = (f32[40,256]{1,0:T(8,128)S(1)}, f32[40,256]{1,0:T(8,128)S(1)}, u32[]{:S(2)}, u32[]{:S(2)}) collective-permute-start(f32[40,256]{1,0:T(8,128)S(1)} %get-tuple-element.41), channel_id=1, source_target_pairs={{1,2},{3,4},{5,6},{7,8},{9,10},{11,12},{13,14},{15,16},{17,18},{19... | collective-permute-start | bytes 122888 | tf_op jit(solution)/shard_map/ppermute | solution.py:532
  21.2 4.0 %collective-permute-start.4 = (f32[40,256]{1,0:T(8,128)S(1)}, f32[40,256]{1,0:T(8,128)S(1)}, u32[]{:S(2)}, u32[]{:S(2)}) collective-permute-start(f32[40,256]{1,0:T(8,128)S(1)} %get-tuple-element.47), channel_id=1, source_target_pairs={{30,31},{62,63},{94,95},{126,127},{158,159},{190,191},{222,223},{2... | collective-permute-start | bytes 122888 | tf_op jit(solution)/shard_map/ppermute | solution.py:532
  21.9 3.3 %collective-permute-start.3 = (f32[112,256]{1,0:T(8,128)S(1)}, f32[112,256]{1,0:T(8,128)S(1)}, u32[]{:S(2)}, u32[]{:S(2)}) collective-permute-start(f32[112,256]{1,0:T(8,128)S(1)} %get-tuple-element.43), channel_id=1, source_target_pairs={{159,287},{191,319},{223,351},{255,383},{415,543},{447,575},{479,6... | collective-permute-start | bytes 344072 | tf_op jit(solution)/shard_map/ppermute | solution.py:532
  25.8 5.6 %collective-permute-start.5 = (f32[64,256]{1,0:T(8,128)S(1)}, f32[64,256]{1,0:T(8,128)S(1)}, u32[]{:S(2)}, u32[]{:S(2)}) collective-permute-start(f32[64,256]{1,0:T(8,128)S(1)} %get-tuple-element.55), channel_id=1, source_target_pairs={{128,256},{129,257},{130,258},{131,259},{132,260},{133,261},{134,2... | collective-permute-start | bytes 196616 | tf_op jit(solution)/shard_map/ppermute | solution.py:532
  31.9 13.7 %collective-permute-start.6 = (f32[72,128]{1,0:T(8,128)S(1)}, f32[72,128]{1,0:T(8,128)S(1)}, u32[]{:S(2)}, u32[]{:S(2)}) collective-permute-start(f32[72,128]{1,0:T(8,128)S(1)} %get-tuple-element.62), channel_id=1, source_target_pairs={{0,1},{2,3},{4,5},{6,7},{8,9},{10,11},{12,13},{14,15},{16,17},{18,... | collective-permute-start | bytes 110600 | tf_op jit(solution)/shard_map/ppermute | solution.py:532
  33.8 12.5 %collective-permute-start.7 = (f32[72,128]{1,0:T(8,128)S(1)}, f32[72,128]{1,0:T(8,128)S(1)}, u32[]{:S(2)}, u32[]{:S(2)}) collective-permute-start(f32[72,128]{1,0:T(8,128)S(1)} %get-tuple-element.63), channel_id=1, source_target_pairs={{1,2},{3,4},{5,6},{7,8},{9,10},{11,12},{13,14},{15,16},{17,18},{19... | collective-permute-start | bytes 110600 | tf_op jit(solution)/shard_map/ppermute | solution.py:532
  44.9 1.3 %collective-permute-start.8 = (f32[72,128]{1,0:T(8,128)S(1)}, f32[72,128]{1,0:T(8,128)S(1)}, u32[]{:S(2)}, u32[]{:S(2)}) collective-permute-start(f32[72,128]{1,0:T(8,128)S(1)} %get-tuple-element.64), channel_id=1, source_target_pairs={{30,31},{62,63},{94,95},{126,127},{158,159},{190,191},{222,223},{2... | collective-permute-start | bytes 110600 | tf_op jit(solution)/shard_map/ppermute | solution.py:532

commit v6 on v5

--- a/solution.py
+++ b/solution.py
@@ -88,6 +88,11 @@
     return ref.at[1 - lax.axis_index("group") % 2]
 
 
+def inner_pair():
+    at = lax.axis_index("dev") % RUN
+    return (at == RUN - 3) | (at == RUN - 2)
+
+
 def side_of_dev():
     return lax.axis_index("dev") % 2
 
@@ -97,7 +102,9 @@
 X_ROWS = 7 * BY
 
 
-def load_kernel(g_hbm, b_hbm, n_hbm, cross, cross2, chip, even, even2, odd, f1z, g, b, w, d, n, both, sems):
+def load_kernel(
+    g_hbm, b_hbm, n_hbm, cross, mixed, chip, even, even2, odd, f1z, g, b, w, d, n, both, sems
+):
     copies = [
         pltpu.make_async_copy(src, dst, sems.at[k])
         for k, (src, dst) in enumerate(((g_hbm, g), (b_hbm, b), (n_hbm, n)))
@@ -136,10 +143,14 @@
             for k, v in rows:
                 both[s, k : k + 1, :] = v
     p = side_of_dev()
-    cross2[...] = cross[...]
     even[...] = both[1 - p]
     even2[...] = both[1 - p]
     odd[...] = both[p]
+    mixed[...] = cross[...]
+
+    @pl.when(inner_pair())
+    def _():
+        mixed[0:Y_ROWS, :] = both[p]
 
 
 class Wide:
@@ -184,13 +195,14 @@
 
 
 def middle_kernel(
-    g, b, w, d, left1, cross2, chip, f1z, both1, even2,
+    g, b, w, d, left1, mixed, chip, f1z, both1, even2,
     f2, f2low, f2high, c1, wc, left, both, lo, hi, col, line, sums,
 ):
-    left[...] = left1[...] + cross2[...]
+    inner = inner_pair()
+    left[...] = left1[...] + jnp.where(inner, 0.0, mixed[...])
     a = Wide(g, b, w, left, chip)
     p = side_of_dev()
-    both[p] = both1[p]
+    both[p] = both1[p] + jnp.where(inner, mixed[0:Y_ROWS, :], 0.0)
     both[1 - p] = both1[1 - p] + even2[...]
     low, high = both.at[0], both.at[1]
     rows = lax.broadcasted_iota(jnp.int32, (BY, NZ), 0)
@@ -557,7 +569,7 @@
 
 def body(g, b, n):
     block = (BX, BY, NZ)
-    cross, cross2, chip, even, even2, odd, f1z, g, b, w, d = call(
+    cross, mixed, chip, even, even2, odd, f1z, g, b, w, d = call(
         load_kernel,
         [(X_ROWS, NZ)] * 3 + [(Y_ROWS, NZ)] * 3 + [(BX * BY, NZ)] + [block] * 4,
         g, b, n,
@@ -567,20 +579,20 @@
     )
     cross1 = swap(cross, cross_pairs(lambda d: not is_end(d)))
     even1 = swap(even, dev_pairs(0, lambda d: not before_end(d)))
-    odd = swap(odd, dev_pairs(1, lambda d: True))
-    cross2 = swap(cross2, cross_pairs(is_end))
+    odd1 = swap(odd, dev_pairs(1, lambda d: not before_end(d + 1)))
     even2 = swap(even2, dev_pairs(0, before_end))
+    mixed = swap(mixed, dev_pairs(1, lambda d: before_end(d + 1)) + cross_pairs(is_end))
     chip = share_chip(chip)
     left, both = call(
         gather_kernel,
         [(X_ROWS, NZ), (2, Y_ROWS, NZ)],
-        cross1, even1, odd,
+        cross1, even1, odd1,
         cost=pl.CostEstimate(flops=2**34, bytes_accessed=2**28, transcendentals=0),
     )
     f2, f2low, f2high, c1, wc, left, both, cross, near = call(
         middle_kernel,
         [(10 * BY, NZ), (BX, NZ), (BX, NZ), (CX * CY, CZ), (CX * CY, CZ), (X_ROWS, NZ), (2, Y_ROWS, NZ)] + [(X2_ROWS, NZ)] * 2,
-        g, b, w, d, left, cross2, chip, f1z, both, even2,
+        g, b, w, d, left, mixed, chip, f1z, both, even2,
         scratch=[(16, NZ), (2, 16, NZ), (8 * BY, CZ)],
     )
     cleft = swap(cross, cross_pairs(lambda d: True))

time: 48.4 us -> 44 us (0.909)
  starting transfers between devices: 38.3 us -> 34.4 us
    ppermute x9, starting transfers between devices: 38.3 us -> 34.4 us  [swap(): return lax.ppermute(v, ('group', 'dev'), links + [(j, i) for i, j in links])]
where the time goes in v6:
time: 44 us; the launch traced here: 43.7 us
  starting transfers between devices  34.4 us (78%)
  blocking collectives  4.46 us (10%)
  Pallas kernels  3.71 us (8%)
  waiting for transfers between devices  0.98 us (2%)
    ppermute x9, starting transfers between devices, swap(): return lax.ppermute(v, ('group', 'dev'), links + [(j, i) for i, j in links])  34.4 us
    all_gather x2, blocking collectives, share_chip(): return lax.all_gather(v, 'group', axis_index_groups=groups)  4.46 us
    pallas_call x5, Pallas kernels, call(): pl.pallas_call(kernel, out_shape=[make(s, F32) for s in outs], in_specs=[...  3.71 us
    ppermute x9, waiting for transfers between devices, swap(): return lax.ppermute(v, ('group', 'dev'), links + [(j, i) for i, j in links])  0.98 us
  transfers between devices with their start and end apart: 9, of which 2 were waited for; matrix products, arithmetic and copies ran while one was open for 0% of the time, Pallas kernels for 0%

profile of v6, /device:TPU:25, one launch (start us, length us, event | category | flops | bytes accessed | tf_op | source)
XLA Modules:
  0.0 43.7 jit_solution(17946842080366876519)
XLA Ops:
  0.0 1.3 %shard_map.37 = (f32[112,256]{1,0:T(8,128)S(1)}, f32[112,256]{1,0:T(8,128)S(1)}, f32[112,256]{1,0:T(8,128)S(1)}, f32[40,256]{1,0:T(8,128)S(1)}, f32[40,256]{1,0:...) custom-call(f32[8,16,256]{2,1,0:T(8,128)} %g_hbm.1, ...), custom_call_target="tpu_custom_call" | custom-call | tf_op jit(solution)/shard_map/pallas_call | solution.py:19
  1.3 3.7 %collective-permute-start = (f32[112,256]{1,0:T(8,128)S(1)}, f32[112,256]{1,0:T(8,128)S(1)}, u32[]{:S(2)}, u32[]{:S(2)}) collective-permute-start(f32[112,256]{1,0:T(8,128)S(1)} %get-tuple-element.39), channel_id=1, source_target_pairs={{128,256},{129,257},{130,258},{131,259},{132,260},{133,261},{134,2... | collective-permute-start | bytes 344072 | tf_op jit(solution)/shard_map/ppermute | solution.py:544
  5.0 3.5 %collective-permute-start.1 = (f32[40,256]{1,0:T(8,128)S(1)}, f32[40,256]{1,0:T(8,128)S(1)}, u32[]{:S(2)}, u32[]{:S(2)}) collective-permute-start(f32[40,256]{1,0:T(8,128)S(1)} %get-tuple-element.40), channel_id=1, source_target_pairs={{0,1},{2,3},{4,5},{6,7},{8,9},{10,11},{12,13},{14,15},{16,17},{18,... | collective-permute-start | bytes 122888 | tf_op jit(solution)/shard_map/ppermute | solution.py:544
  8.5 12.7 %collective-permute-start.2 = (f32[40,256]{1,0:T(8,128)S(1)}, f32[40,256]{1,0:T(8,128)S(1)}, u32[]{:S(2)}, u32[]{:S(2)}) collective-permute-start(f32[40,256]{1,0:T(8,128)S(1)} %get-tuple-element.41), channel_id=1, source_target_pairs={{1,2},{3,4},{5,6},{7,8},{9,10},{11,12},{13,14},{15,16},{17,18},{19... | collective-permute-start | bytes 122888 | tf_op jit(solution)/shard_map/ppermute | solution.py:544
  21.2 0.7 %collective-permute-start.4 = (f32[40,256]{1,0:T(8,128)S(1)}, f32[40,256]{1,0:T(8,128)S(1)}, u32[]{:S(2)}, u32[]{:S(2)}) collective-permute-start(f32[40,256]{1,0:T(8,128)S(1)} %get-tuple-element.47), channel_id=1, source_target_pairs={{30,31},{62,63},{94,95},{126,127},{158,159},{190,191},{222,223},{2... | collective-permute-start | bytes 122888 | tf_op jit(solution)/shard_map/ppermute | solution.py:544
  21.9 0.7 %collective-permute-start.3 = (f32[112,256]{1,0:T(8,128)S(1)}, f32[112,256]{1,0:T(8,128)S(1)}, u32[]{:S(2)}, u32[]{:S(2)}) collective-permute-start(f32[112,256]{1,0:T(8,128)S(1)} %get-tuple-element.43), channel_id=1, source_target_pairs={{29,30},{61,62},{93,94},{125,126},{157,158},{189,190},{221,222},{2... | collective-permute-start | bytes 344072 | tf_op jit(solution)/shard_map/ppermute | solution.py:544
  22.6 2.6 %all-gather = f32[224,256]{1,0:T(8,128)S(1)} all-gather(f32[112,256]{1,0:T(8,128)S(1)} %get-tuple-element.44), channel_id=2, replica_groups={{0,128},{256,384},{512,640},{768,896},{1,129},{257,385},{513,641},{769,..., dimensions={0}, use_global_device_ids=true | all-gather | bytes 344064 | tf_op jit(solution)/shard_map/all_gather | solution.py:549
  25.1 0.0 collective-permute-done.1.even
  25.1 0.0 collective-permute-done.2.odd
  25.1 0.0 collective-permute-done.cross
  25.2 0.0 collective-permute-done.4.even2
  25.2 0.0 collective-permute-done.3.mixed
  25.2 0.7 %shard_map.39 = (f32[160,256]{1,0:T(8,128)S(1)}, f32[8,256]{1,0:T(8,128)S(1)}, f32[8,256]{1,0:T(8,128)S(1)}, f32[32,128]{1,0:T(8,128)S(1)}, f32[32,128]{1,0:T(8,...) custom-call(f32[8,16,256]{2,1,0:T(8,128)S(1)} %get-tuple-element.35., ...), custom_call_target="tpu_custom_call" | custom-call | tf_op jit(solution)/shard_map/pallas_call | solution.py:19
  25.8 3.4 %collective-permute-start.5 = (f32[64,256]{1,0:T(8,128)S(1)}, f32[64,256]{1,0:T(8,128)S(1)}, u32[]{:S(2)}, u32[]{:S(2)}) collective-permute-start(f32[64,256]{1,0:T(8,128)S(1)} %get-tuple-element.55), channel_id=1, source_target_pairs={{128,256},{129,257},{130,258},{131,259},{132,260},{133,261},{134,2... | collective-permute-start | bytes 196616 | tf_op jit(solution)/shard_map/ppermute | solution.py:544
  29.2 1.9 %all-gather.1 = f32[128,256]{1,0:T(8,128)S(1)} all-gather(f32[64,256]{1,0:T(8,128)S(1)} %get-tuple-element.56), channel_id=3, replica_groups={{0,128},{256,384},{512,640},{768,896},{1,129},{257,385},{513,641},{769,..., dimensions={0}, use_global_device_ids=true | all-gather | bytes 196608 | tf_op jit(solution)/shard_map/all_gather | solution.py:549
  31.1 0.3 collective-permute-done.5.cleft
  31.4 0.4 %shard_map.40 = (f32[72,128]{1,0:T(8,128)S(1)}, f32[72,128]{1,0:T(8,128)S(1)}, f32[72,128]{1,0:T(8,128)S(1)}, f32[160,256]{1,0:T(8,128)S(1)}, f32[8,256]{1,0:T(8...) custom-call(f32[8,16,256]{2,1,0:T(8,128)S(1)} %get-tuple-element.35.g, ...), custom_call_target="tpu_custom_call" | custom-call | tf_op jit(solution)/shard_map/pallas_call | solution.py:19
  31.9 1.9 %collective-permute-start.6 = (f32[72,128]{1,0:T(8,128)S(1)}, f32[72,128]{1,0:T(8,128)S(1)}, u32[]{:S(2)}, u32[]{:S(2)}) collective-permute-start(f32[72,128]{1,0:T(8,128)S(1)} %get-tuple-element.62), channel_id=1, source_target_pairs={{0,1},{2,3},{4,5},{6,7},{8,9},{10,11},{12,13},{14,15},{16,17},{18,... | collective-permute-start | bytes 110600 | tf_op jit(solution)/shard_map/ppermute | solution.py:544
  33.8 7.2 %collective-permute-start.7 = (f32[72,128]{1,0:T(8,128)S(1)}, f32[72,128]{1,0:T(8,128)S(1)}, u32[]{:S(2)}, u32[]{:S(2)}) collective-permute-start(f32[72,128]{1,0:T(8,128)S(1)} %get-tuple-element.63), channel_id=1, source_target_pairs={{1,2},{3,4},{5,6},{7,8},{9,10},{11,12},{13,14},{15,16},{17,18},{19... | collective-permute-start | bytes 110600 | tf_op jit(solution)/shard_map/ppermute | solution.py:544
  41.0 0.7 %collective-permute-start.8 = (f32[72,128]{1,0:T(8,128)S(1)}, f32[72,128]{1,0:T(8,128)S(1)}, u32[]{:S(2)}, u32[]{:S(2)}) collective-permute-start(f32[72,128]{1,0:T(8,128)S(1)} %get-tuple-element.64), channel_id=1, source_target_pairs={{30,31},{62,63},{94,95},{126,127},{158,159},{190,191},{222,223},{2... | collective-permute-start | bytes 110600 | tf_op jit(solution)/shard_map/ppermute | solution.py:544
  41.7 0.0 collective-permute-done.6.even1
  41.7 0.7 %collective-permute-done.7.odd = f32[72,128]{1,0:T(8,128)S(1)} collective-permute-done((f32[72,128]{1,0:T(8,128)S(1)}, f32[72,128]{1,0:T(8,128)S(1)}, u32[]{:S(2)}, u32[]{:S(2)}) %collective-permute-start.7) | collective-permute-done | bytes 36896 | tf_op jit(solution)/shard_map/ppermute | solution.py:544
  42.3 0.0 collective-permute-done.8.even2
  42.3 1.3 %shard_map.41 = f32[8,16,256]{2,1,0:T(8,128)} custom-call(f32[8,16,256]{2,1,0:T(8,128)S(1)} %get-tuple-element.35.g, f32[8,16,256]{2,1,0:T(8,128)S(1)} %get-tuple-element.36.b, f32[8,16,256]{2,1,0:T(8,128)S(1)} %get-tuple-element.37.w, f32[112,256]{1,0:T(8,128)S(1)} %get-tuple-element.48.left, f32[2,112,256]{2,1,0:T(8,128)S(1)} %bitcast.4, ...), custom_call_target="tpu_custom_call" | custom-call | tf_op jit(solution)/shard_map/pallas_call | solution.py:19
  (1 shorter events, 0.0 us)
Async XLA Ops:
  1.3 23.9 %collective-permute-start = (f32[112,256]{1,0:T(8,128)S(1)}, f32[112,256]{1,0:T(8,128)S(1)}, u32[]{:S(2)}, u32[]{:S(2)}) collective-permute-start(f32[112,256]{1,0:T(8,128)S(1)} %get-tuple-element.39), channel_id=1, source_target_pairs={{128,256},{129,257},{130,258},{131,259},{132,260},{133,261},{134,2... | collective-permute-start | bytes 344072 | tf_op jit(solution)/shard_map/ppermute | solution.py:544
  5.0 20.2 %collective-permute-start.1 = (f32[40,256]{1,0:T(8,128)S(1)}, f32[40,256]{1,0:T(8,128)S(1)}, u32[]{:S(2)}, u32[]{:S(2)}) collective-permute-start(f32[40,256]{1,0:T(8,128)S(1)} %get-tuple-element.40), channel_id=1, source_target_pairs={{0,1},{2,3},{4,5},{6,7},{8,9},{10,11},{12,13},{14,15},{16,17},{18,... | collective-permute-start | bytes 122888 | tf_op jit(solution)/shard_map/ppermute | solution.py:544
  8.5 16.6 %collective-permute-start.2 = (f32[40,256]{1,0:T(8,128)S(1)}, f32[40,256]{1,0:T(8,128)S(1)}, u32[]{:S(2)}, u32[]{:S(2)}) collective-permute-start(f32[40,256]{1,0:T(8,128)S(1)} %get-tuple-element.41), channel_id=1, source_target_pairs={{1,2},{3,4},{5,6},{7,8},{9,10},{11,12},{13,14},{15,16},{17,18},{19... | collective-permute-start | bytes 122888 | tf_op jit(solution)/shard_map/ppermute | solution.py:544
  21.2 4.0 %collective-permute-start.4 = (f32[40,256]{1,0:T(8,128)S(1)}, f32[40,256]{1,0:T(8,128)S(1)}, u32[]{:S(2)}, u32[]{:S(2)}) collective-permute-start(f32[40,256]{1,0:T(8,128)S(1)} %get-tuple-element.47), channel_id=1, source_target_pairs={{30,31},{62,63},{94,95},{126,127},{158,159},{190,191},{222,223},{2... | collective-permute-start | bytes 122888 | tf_op jit(solution)/shard_map/ppermute | solution.py:544
  21.9 3.3 %collective-permute-start.3 = (f32[112,256]{1,0:T(8,128)S(1)}, f32[112,256]{1,0:T(8,128)S(1)}, u32[]{:S(2)}, u32[]{:S(2)}) collective-permute-start(f32[112,256]{1,0:T(8,128)S(1)} %get-tuple-element.43), channel_id=1, source_target_pairs={{29,30},{61,62},{93,94},{125,126},{157,158},{189,190},{221,222},{2... | collective-permute-start | bytes 344072 | tf_op jit(solution)/shard_map/ppermute | solution.py:544
  25.8 5.6 %collective-permute-start.5 = (f32[64,256]{1,0:T(8,128)S(1)}, f32[64,256]{1,0:T(8,128)S(1)}, u32[]{:S(2)}, u32[]{:S(2)}) collective-permute-start(f32[64,256]{1,0:T(8,128)S(1)} %get-tuple-element.55), channel_id=1, source_target_pairs={{128,256},{129,257},{130,258},{131,259},{132,260},{133,261},{134,2... | collective-permute-start | bytes 196616 | tf_op jit(solution)/shard_map/ppermute | solution.py:544
  31.9 9.8 %collective-permute-start.6 = (f32[72,128]{1,0:T(8,128)S(1)}, f32[72,128]{1,0:T(8,128)S(1)}, u32[]{:S(2)}, u32[]{:S(2)}) collective-permute-start(f32[72,128]{1,0:T(8,128)S(1)} %get-tuple-element.62), channel_id=1, source_target_pairs={{0,1},{2,3},{4,5},{6,7},{8,9},{10,11},{12,13},{14,15},{16,17},{18,... | collective-permute-start | bytes 110600 | tf_op jit(solution)/shard_map/ppermute | solution.py:544
  33.8 8.5 %collective-permute-start.7 = (f32[72,128]{1,0:T(8,128)S(1)}, f32[72,128]{1,0:T(8,128)S(1)}, u32[]{:S(2)}, u32[]{:S(2)}) collective-permute-start(f32[72,128]{1,0:T(8,128)S(1)} %get-tuple-element.63), channel_id=1, source_target_pairs={{1,2},{3,4},{5,6},{7,8},{9,10},{11,12},{13,14},{15,16},{17,18},{19... | collective-permute-start | bytes 110600 | tf_op jit(solution)/shard_map/ppermute | solution.py:544
  41.0 1.3 %collective-permute-start.8 = (f32[72,128]{1,0:T(8,128)S(1)}, f32[72,128]{1,0:T(8,128)S(1)}, u32[]{:S(2)}, u32[]{:S(2)}) collective-permute-start(f32[72,128]{1,0:T(8,128)S(1)} %get-tuple-element.64), channel_id=1, source_target_pairs={{30,31},{62,63},{94,95},{126,127},{158,159},{190,191},{222,223},{2... | collective-permute-start | bytes 110600 | tf_op jit(solution)/shard_map/ppermute | solution.py:544

commit v7 on v5

--- a/solution.py
+++ b/solution.py
@@ -97,7 +97,9 @@
 X_ROWS = 7 * BY
 
 
-def load_kernel(g_hbm, b_hbm, n_hbm, cross, cross2, chip, even, even2, odd, f1z, g, b, w, d, n, both, sems):
+def load_kernel(
+    g_hbm, b_hbm, n_hbm, cross, cross2, chip, even, odd, f1z, g, b, w, d, n, both, sems
+):
     copies = [
         pltpu.make_async_copy(src, dst, sems.at[k])
         for k, (src, dst) in enumerate(((g_hbm, g), (b_hbm, b), (n_hbm, n)))
@@ -136,10 +138,9 @@
             for k, v in rows:
                 both[s, k : k + 1, :] = v
     p = side_of_dev()
+    even[...] = both[1 - p]
+    odd[...] = both[p]
     cross2[...] = cross[...]
-    even[...] = both[1 - p]
-    even2[...] = both[1 - p]
-    odd[...] = both[p]
 
 
 class Wide:
@@ -169,6 +170,12 @@
     both[p] = odd
 
 
+def again_kernel(even, odd, chip, met, even2, odd2, chip2):
+    chip2[...] = chip[...]
+    even2[...] = even[...]
+    odd2[...] = odd[...]
+
+
 def gather_kernel(cross, even, odd, left, both):
     left[...] = cross[...]
     take(both, even[...], odd[...])
@@ -184,13 +191,13 @@
 
 
 def middle_kernel(
-    g, b, w, d, left1, cross2, chip, f1z, both1, even2,
+    g, b, w, d, left1, cross2, chip, f1z, both1, even2, odd2,
     f2, f2low, f2high, c1, wc, left, both, lo, hi, col, line, sums,
 ):
     left[...] = left1[...] + cross2[...]
     a = Wide(g, b, w, left, chip)
     p = side_of_dev()
-    both[p] = both1[p]
+    both[p] = both1[p] + odd2[...]
     both[1 - p] = both1[1 - p] + even2[...]
     low, high = both.at[0], both.at[1]
     rows = lax.broadcasted_iota(jnp.int32, (BY, NZ), 0)
@@ -557,9 +564,9 @@
 
 def body(g, b, n):
     block = (BX, BY, NZ)
-    cross, cross2, chip, even, even2, odd, f1z, g, b, w, d = call(
+    cross, cross2, chip, even, odd, f1z, g, b, w, d = call(
         load_kernel,
-        [(X_ROWS, NZ)] * 3 + [(Y_ROWS, NZ)] * 3 + [(BX * BY, NZ)] + [block] * 4,
+        [(X_ROWS, NZ)] * 3 + [(Y_ROWS, NZ)] * 2 + [(BX * BY, NZ)] + [block] * 4,
         g, b, n,
         hbm=3,
         vmem=None,
@@ -567,20 +574,22 @@
     )
     cross1 = swap(cross, cross_pairs(lambda d: not is_end(d)))
     even1 = swap(even, dev_pairs(0, lambda d: not before_end(d)))
-    odd = swap(odd, dev_pairs(1, lambda d: True))
+    odd1 = swap(odd, dev_pairs(1, lambda d: not before_end(d + 1)))
     cross2 = swap(cross2, cross_pairs(is_end))
+    even2, odd2, chip = call(again_kernel, [(Y_ROWS, NZ)] * 2 + [(X_ROWS, NZ)], even, odd, chip, even1)
     even2 = swap(even2, dev_pairs(0, before_end))
+    odd2 = swap(odd2, dev_pairs(1, lambda d: before_end(d + 1)))
     chip = share_chip(chip)
     left, both = call(
         gather_kernel,
         [(X_ROWS, NZ), (2, Y_ROWS, NZ)],
-        cross1, even1, odd,
-        cost=pl.CostEstimate(flops=2**34, bytes_accessed=2**28, transcendentals=0),
+        cross1, even1, odd1,
+        cost=pl.CostEstimate(flops=2**34, bytes_accessed=0, transcendentals=0),
     )
     f2, f2low, f2high, c1, wc, left, both, cross, near = call(
         middle_kernel,
         [(10 * BY, NZ), (BX, NZ), (BX, NZ), (CX * CY, CZ), (CX * CY, CZ), (X_ROWS, NZ), (2, Y_ROWS, NZ)] + [(X2_ROWS, NZ)] * 2,
-        g, b, w, d, left, cross2, chip, f1z, both, even2,
+        g, b, w, d, left, cross2, chip, f1z, both, even2, odd2,
         scratch=[(16, NZ), (2, 16, NZ), (8 * BY, CZ)],
     )
     cleft = swap(cross, cross_pairs(lambda d: True))

time: 48.4 us -> 43.7 us (0.903)
  starting transfers between devices: 38.3 us -> 32.3 us
  waiting for transfers between devices: 0.98 us -> 2.38 us
    ppermute x9 -> x10, starting transfers between devices: 38.3 us -> 32.3 us  [swap(): return lax.ppermute(v, ('group', 'dev'), links + [(j, i) for i, j in links])]
    ppermute x9 -> x10, waiting for transfers between devices: 0.98 us -> 2.38 us  [swap(): return lax.ppermute(v, ('group', 'dev'), links + [(j, i) for i, j in links])]
    pallas_call x5 -> x6, Pallas kernels: 3.7 us -> 3.68 us  [call(): pl.pallas_call(kernel, out_shape=[make(s, F32) for s in outs], in_specs=[...]
  transfers between devices with their start and end apart: 9 -> 10, of which waited for: 2 -> 2; matrix products, arithmetic and copies ran while one was open for 0% -> 0% of each run, Pallas kernels for 0% -> 0%
where the time goes in v7:
time: 43.7 us; the launch traced here: 43 us
  starting transfers between devices  32.3 us (74%)
  blocking collectives  4.46 us (10%)
  Pallas kernels  3.68 us (8%)
  waiting for transfers between devices  2.38 us (5%)
    ppermute x10, starting transfers between devices, swap(): return lax.ppermute(v, ('group', 'dev'), links + [(j, i) for i, j in links])  32.3 us
    all_gather x2, blocking collectives, share_chip(): return lax.all_gather(v, 'group', axis_index_groups=groups)  4.46 us
    pallas_call x6, Pallas kernels, call(): pl.pallas_call(kernel, out_shape=[make(s, F32) for s in outs], in_specs=[...  3.68 us
    ppermute x10, waiting for transfers between devices, swap(): return lax.ppermute(v, ('group', 'dev'), links + [(j, i) for i, j in links])  2.38 us
  transfers between devices with their start and end apart: 10, of which 2 were waited for; matrix products, arithmetic and copies ran while one was open for 0% of the time, Pallas kernels for 0%

profile of v7, /device:TPU:25, one launch (start us, length us, event | category | flops | bytes accessed | tf_op | source)
XLA Modules:
  0.0 43.0 jit_solution(5201778745788599598)
XLA Ops:
  0.0 1.3 %shard_map.37 = (f32[112,256]{1,0:T(8,128)S(1)}, f32[112,256]{1,0:T(8,128)S(1)}, f32[112,256]{1,0:T(8,128)S(1)}, f32[40,256]{1,0:T(8,128)S(1)}, f32[40,256]{1,0:...) custom-call(f32[8,16,256]{2,1,0:T(8,128)} %g_hbm.1, ...), custom_call_target="tpu_custom_call" | custom-call | tf_op jit(solution)/shard_map/pallas_call | solution.py:19
  1.3 3.7 %collective-permute-start = (f32[112,256]{1,0:T(8,128)S(1)}, f32[112,256]{1,0:T(8,128)S(1)}, u32[]{:S(2)}, u32[]{:S(2)}) collective-permute-start(f32[112,256]{1,0:T(8,128)S(1)} %get-tuple-element.41), channel_id=1, source_target_pairs={{128,256},{129,257},{130,258},{131,259},{132,260},{133,261},{134,2... | collective-permute-start | bytes 344072 | tf_op jit(solution)/shard_map/ppermute | solution.py:539
  4.9 3.5 %collective-permute-start.1 = (f32[40,256]{1,0:T(8,128)S(1)}, f32[40,256]{1,0:T(8,128)S(1)}, u32[]{:S(2)}, u32[]{:S(2)}) collective-permute-start(f32[40,256]{1,0:T(8,128)S(1)} %get-tuple-element.42.even), channel_id=1, source_target_pairs={{0,1},{2,3},{4,5},{6,7},{8,9},{10,11},{12,13},{14,15},{16,17},{18,... | collective-permute-start | bytes 122888 | tf_op jit(solution)/shard_map/ppermute | solution.py:539
  8.5 12.7 %collective-permute-start.2 = (f32[40,256]{1,0:T(8,128)S(1)}, f32[40,256]{1,0:T(8,128)S(1)}, u32[]{:S(2)}, u32[]{:S(2)}) collective-permute-start(f32[40,256]{1,0:T(8,128)S(1)} %get-tuple-element.43.odd), channel_id=1, source_target_pairs={{1,2},{3,4},{5,6},{7,8},{9,10},{11,12},{13,14},{15,16},{17,18},{19... | collective-permute-start | bytes 122888 | tf_op jit(solution)/shard_map/ppermute | solution.py:539
  21.2 0.7 %collective-permute-start.3 = (f32[112,256]{1,0:T(8,128)S(1)}, f32[112,256]{1,0:T(8,128)S(1)}, u32[]{:S(2)}, u32[]{:S(2)}) collective-permute-start(f32[112,256]{1,0:T(8,128)S(1)} %get-tuple-element.45), channel_id=1, source_target_pairs={{159,287},{191,319},{223,351},{255,383},{415,543},{447,575},{479,6... | collective-permute-start | bytes 344072 | tf_op jit(solution)/shard_map/ppermute | solution.py:539
  21.9 0.0 collective-permute-done.1.even.met
  21.9 0.7 %collective-permute-start.4 = (f32[40,256]{1,0:T(8,128)S(1)}, f32[40,256]{1,0:T(8,128)S(1)}, u32[]{:S(2)}, u32[]{:S(2)}) collective-permute-start(f32[40,256]{1,0:T(8,128)S(1)} %get-tuple-element.50), channel_id=1, source_target_pairs={{30,31},{62,63},{94,95},{126,127},{158,159},{190,191},{222,223},{2... | collective-permute-start | bytes 122888 | tf_op jit(solution)/shard_map/ppermute | solution.py:539
  22.6 0.7 %collective-permute-start.5 = (f32[40,256]{1,0:T(8,128)S(1)}, f32[40,256]{1,0:T(8,128)S(1)}, u32[]{:S(2)}, u32[]{:S(2)}) collective-permute-start(f32[40,256]{1,0:T(8,128)S(1)} %get-tuple-element.51), channel_id=1, source_target_pairs={{29,30},{61,62},{93,94},{125,126},{157,158},{189,190},{221,222},{2... | collective-permute-start | bytes 122888 | tf_op jit(solution)/shard_map/ppermute | solution.py:539
  23.3 2.6 %all-gather = f32[224,256]{1,0:T(8,128)S(1)} all-gather(f32[112,256]{1,0:T(8,128)S(1)} %get-tuple-element.47), channel_id=2, replica_groups={{0,128},{256,384},{512,640},{768,896},{1,129},{257,385},{513,641},{769,..., dimensions={0}, use_global_device_ids=true | all-gather | bytes 344064 | tf_op jit(solution)/shard_map/all_gather | solution.py:544
  25.8 0.0 collective-permute-done.2.odd
  25.8 0.0 collective-permute-done.cross
  25.8 0.0 collective-permute-done.4.even2
  25.9 0.0 collective-permute-done.3.cross2
  25.9 0.6 %shard_map.40 = (f32[160,256]{1,0:T(8,128)S(1)}, f32[8,256]{1,0:T(8,128)S(1)}, f32[8,256]{1,0:T(8,128)S(1)}, f32[32,128]{1,0:T(8,128)S(1)}, f32[32,128]{1,0:T(8,...) custom-call(f32[8,16,256]{2,1,0:T(8,128)S(1)} %get-tuple-element.37., ...), custom_call_target="tpu_custom_call" | custom-call | tf_op jit(solution)/shard_map/pallas_call | solution.py:19
  26.5 3.4 %collective-permute-start.6 = (f32[64,256]{1,0:T(8,128)S(1)}, f32[64,256]{1,0:T(8,128)S(1)}, u32[]{:S(2)}, u32[]{:S(2)}) collective-permute-start(f32[64,256]{1,0:T(8,128)S(1)} %get-tuple-element.59), channel_id=1, source_target_pairs={{128,256},{129,257},{130,258},{131,259},{132,260},{133,261},{134,2... | collective-permute-start | bytes 196616 | tf_op jit(solution)/shard_map/ppermute | solution.py:539
  29.9 1.9 %all-gather.1 = f32[128,256]{1,0:T(8,128)S(1)} all-gather(f32[64,256]{1,0:T(8,128)S(1)} %get-tuple-element.60), channel_id=3, replica_groups={{0,128},{256,384},{512,640},{768,896},{1,129},{257,385},{513,641},{769,..., dimensions={0}, use_global_device_ids=true | all-gather | bytes 196608 | tf_op jit(solution)/shard_map/all_gather | solution.py:544
  31.8 0.3 collective-permute-done.6.cleft
  32.1 0.4 %shard_map.41 = (f32[72,128]{1,0:T(8,128)S(1)}, f32[72,128]{1,0:T(8,128)S(1)}, f32[72,128]{1,0:T(8,128)S(1)}, f32[160,256]{1,0:T(8,128)S(1)}, f32[8,256]{1,0:T(8...) custom-call(f32[8,16,256]{2,1,0:T(8,128)S(1)} %get-tuple-element.37.g, ...), custom_call_target="tpu_custom_call" | custom-call | tf_op jit(solution)/shard_map/pallas_call | solution.py:19
  32.6 1.9 %collective-permute-start.7 = (f32[72,128]{1,0:T(8,128)S(1)}, f32[72,128]{1,0:T(8,128)S(1)}, u32[]{:S(2)}, u32[]{:S(2)}) collective-permute-start(f32[72,128]{1,0:T(8,128)S(1)} %get-tuple-element.66), channel_id=1, source_target_pairs={{0,1},{2,3},{4,5},{6,7},{8,9},{10,11},{12,13},{14,15},{16,17},{18,... | collective-permute-start | bytes 110600 | tf_op jit(solution)/shard_map/ppermute | solution.py:539
  34.5 4.5 %collective-permute-start.8 = (f32[72,128]{1,0:T(8,128)S(1)}, f32[72,128]{1,0:T(8,128)S(1)}, u32[]{:S(2)}, u32[]{:S(2)}) collective-permute-start(f32[72,128]{1,0:T(8,128)S(1)} %get-tuple-element.67), channel_id=1, source_target_pairs={{1,2},{3,4},{5,6},{7,8},{9,10},{11,12},{13,14},{15,16},{17,18},{19... | collective-permute-start | bytes 110600 | tf_op jit(solution)/shard_map/ppermute | solution.py:539
  38.9 0.7 %collective-permute-start.9 = (f32[72,128]{1,0:T(8,128)S(1)}, f32[72,128]{1,0:T(8,128)S(1)}, u32[]{:S(2)}, u32[]{:S(2)}) collective-permute-start(f32[72,128]{1,0:T(8,128)S(1)} %get-tuple-element.68), channel_id=1, source_target_pairs={{30,31},{62,63},{94,95},{126,127},{158,159},{190,191},{222,223},{2... | collective-permute-start | bytes 110600 | tf_op jit(solution)/shard_map/ppermute | solution.py:539
  39.6 2.0 %collective-permute-done.8.odd = f32[72,128]{1,0:T(8,128)S(1)} collective-permute-done((f32[72,128]{1,0:T(8,128)S(1)}, f32[72,128]{1,0:T(8,128)S(1)}, u32[]{:S(2)}, u32[]{:S(2)}) %collective-permute-start.8) | collective-permute-done | bytes 36896 | tf_op jit(solution)/shard_map/ppermute | solution.py:539
  41.7 0.0 collective-permute-done.9.even2
  41.7 1.3 %shard_map.42 = f32[8,16,256]{2,1,0:T(8,128)} custom-call(f32[8,16,256]{2,1,0:T(8,128)S(1)} %get-tuple-element.37.g, f32[8,16,256]{2,1,0:T(8,128)S(1)} %get-tuple-element.38.b, f32[8,16,256]{2,1,0:T(8,128)S(1)} %get-tuple-element.39.w, f32[112,256]{1,0:T(8,128)S(1)} %get-tuple-element.52.left, f32[2,112,256]{2,1,0:T(8,128)S(1)} %bitcast.4, ...), custom_call_target="tpu_custom_call" | custom-call | tf_op jit(solution)/shard_map/pallas_call | solution.py:19
  (4 shorter events, 0.0 us)
Async XLA Ops:
  1.3 24.6 %collective-permute-start = (f32[112,256]{1,0:T(8,128)S(1)}, f32[112,256]{1,0:T(8,128)S(1)}, u32[]{:S(2)}, u32[]{:S(2)}) collective-permute-start(f32[112,256]{1,0:T(8,128)S(1)} %get-tuple-element.41), channel_id=1, source_target_pairs={{128,256},{129,257},{130,258},{131,259},{132,260},{133,261},{134,2... | collective-permute-start | bytes 344072 | tf_op jit(solution)/shard_map/ppermute | solution.py:539
  4.9 16.9 %collective-permute-start.1 = (f32[40,256]{1,0:T(8,128)S(1)}, f32[40,256]{1,0:T(8,128)S(1)}, u32[]{:S(2)}, u32[]{:S(2)}) collective-permute-start(f32[40,256]{1,0:T(8,128)S(1)} %get-tuple-element.42.even), channel_id=1, source_target_pairs={{0,1},{2,3},{4,5},{6,7},{8,9},{10,11},{12,13},{14,15},{16,17},{18,... | collective-permute-start | bytes 122888 | tf_op jit(solution)/shard_map/ppermute | solution.py:539
  8.5 17.3 %collective-permute-start.2 = (f32[40,256]{1,0:T(8,128)S(1)}, f32[40,256]{1,0:T(8,128)S(1)}, u32[]{:S(2)}, u32[]{:S(2)}) collective-permute-start(f32[40,256]{1,0:T(8,128)S(1)} %get-tuple-element.43.odd), channel_id=1, source_target_pairs={{1,2},{3,4},{5,6},{7,8},{9,10},{11,12},{13,14},{15,16},{17,18},{19... | collective-permute-start | bytes 122888 | tf_op jit(solution)/shard_map/ppermute | solution.py:539
  21.2 4.7 %collective-permute-start.3 = (f32[112,256]{1,0:T(8,128)S(1)}, f32[112,256]{1,0:T(8,128)S(1)}, u32[]{:S(2)}, u32[]{:S(2)}) collective-permute-start(f32[112,256]{1,0:T(8,128)S(1)} %get-tuple-element.45), channel_id=1, source_target_pairs={{159,287},{191,319},{223,351},{255,383},{415,543},{447,575},{479,6... | collective-permute-start | bytes 344072 | tf_op jit(solution)/shard_map/ppermute | solution.py:539
  21.9 3.9 %collective-permute-start.4 = (f32[40,256]{1,0:T(8,128)S(1)}, f32[40,256]{1,0:T(8,128)S(1)}, u32[]{:S(2)}, u32[]{:S(2)}) collective-permute-start(f32[40,256]{1,0:T(8,128)S(1)} %get-tuple-element.50), channel_id=1, source_target_pairs={{30,31},{62,63},{94,95},{126,127},{158,159},{190,191},{222,223},{2... | collective-permute-start | bytes 122888 | tf_op jit(solution)/shard_map/ppermute | solution.py:539
  22.6 3.3 %collective-permute-start.5 = (f32[40,256]{1,0:T(8,128)S(1)}, f32[40,256]{1,0:T(8,128)S(1)}, u32[]{:S(2)}, u32[]{:S(2)}) collective-permute-start(f32[40,256]{1,0:T(8,128)S(1)} %get-tuple-element.51), channel_id=1, source_target_pairs={{29,30},{61,62},{93,94},{125,126},{157,158},{189,190},{221,222},{2... | collective-permute-start | bytes 122888 | tf_op jit(solution)/shard_map/ppermute | solution.py:539
  26.5 5.6 %collective-permute-start.6 = (f32[64,256]{1,0:T(8,128)S(1)}, f32[64,256]{1,0:T(8,128)S(1)}, u32[]{:S(2)}, u32[]{:S(2)}) collective-permute-start(f32[64,256]{1,0:T(8,128)S(1)} %get-tuple-element.59), channel_id=1, source_target_pairs={{128,256},{129,257},{130,258},{131,259},{132,260},{133,261},{134,2... | collective-permute-start | bytes 196616 | tf_op jit(solution)/shard_map/ppermute | solution.py:539
  32.6 7.1 %collective-permute-start.7 = (f32[72,128]{1,0:T(8,128)S(1)}, f32[72,128]{1,0:T(8,128)S(1)}, u32[]{:S(2)}, u32[]{:S(2)}) collective-permute-start(f32[72,128]{1,0:T(8,128)S(1)} %get-tuple-element.66), channel_id=1, source_target_pairs={{0,1},{2,3},{4,5},{6,7},{8,9},{10,11},{12,13},{14,15},{16,17},{18,... | collective-permute-start | bytes 110600 | tf_op jit(solution)/shard_map/ppermute | solution.py:539
  34.5 7.2 %collective-permute-start.8 = (f32[72,128]{1,0:T(8,128)S(1)}, f32[72,128]{1,0:T(8,128)S(1)}, u32[]{:S(2)}, u32[]{:S(2)}) collective-permute-start(f32[72,128]{1,0:T(8,128)S(1)} %get-tuple-element.67), channel_id=1, source_target_pairs={{1,2},{3,4},{5,6},{7,8},{9,10},{11,12},{13,14},{15,16},{17,18},{19... | collective-permute-start | bytes 110600 | tf_op jit(solution)/shard_map/ppermute | solution.py:539
  38.9 2.7 %collective-permute-start.9 = (f32[72,128]{1,0:T(8,128)S(1)}, f32[72,128]{1,0:T(8,128)S(1)}, u32[]{:S(2)}, u32[]{:S(2)}) collective-permute-start(f32[72,128]{1,0:T(8,128)S(1)} %get-tuple-element.68), channel_id=1, source_target_pairs={{30,31},{62,63},{94,95},{126,127},{158,159},{190,191},{222,223},{2... | collective-permute-start | bytes 110600 | tf_op jit(solution)/shard_map/ppermute | solution.py:539

commit v8 on v7

--- a/solution.py
+++ b/solution.py
@@ -52,29 +52,36 @@
     return ref[k * rows : (k + 1) * rows, :]
 
 
+def by_row(n, rows):
+    total = 0.0
+    for k, v in rows.items():
+        at = lax.broadcasted_iota(jnp.int32, (n, v.shape[1]), 0)
+        total = jnp.where(at == k, v, total)
+    return total
+
+
 def row(ref, k):
     return ref[k : k + 1, :]
 
 
-def halved(n, m):
-    a = lax.broadcasted_iota(jnp.int32, (n, m), 0)
-    b = lax.broadcasted_iota(jnp.int32, (n, m), 1)
-    return jnp.where((a // 2 == b) if n > m else (a == b // 2), 1.0, 0.0).astype(F32)
-
-
 def lanes(v, index):
     return jnp.take_along_axis(v, index, axis=1)
 
 
-def pair_z(v):
-    lane = lax.broadcasted_iota(jnp.int32, (v.shape[0], CZ), 1)
-    low, high = v[:, :CZ], v[:, CZ:]
+def pair_z(low, high):
+    lane = lax.broadcasted_iota(jnp.int32, low.shape, 1)
     low = low + pltpu.roll(low, CZ - 1, 1)
     high = high + pltpu.roll(high, CZ - 1, 1)
     index = (2 * lane) % CZ
     return jnp.where(lane < CZ // 2, lanes(low, index), lanes(high, index))
 
 
+def spread_z(v, out):
+    half = lax.broadcasted_iota(jnp.int32, v.shape, 1) // 2
+    out[:, :CZ] = lanes(v, half)
+    out[:, CZ:] = lanes(v, half + CZ // 2)
+
+
 def diag_of(n):
     return 6.0 + 0.25 * n.astype(F32)
 
@@ -98,7 +105,7 @@
 
 
 def load_kernel(
-    g_hbm, b_hbm, n_hbm, cross, cross2, chip, even, odd, f1z, g, b, w, d, n, both, sems
+    g_hbm, b_hbm, n_hbm, cross, chip, even, odd, f1z, g, b, w, d, n, both, sems
 ):
     copies = [
         pltpu.make_async_copy(src, dst, sems.at[k])
@@ -140,7 +147,6 @@
     p = side_of_dev()
     even[...] = both[1 - p]
     odd[...] = both[p]
-    cross2[...] = cross[...]
 
 
 class Wide:
@@ -170,10 +176,11 @@
     both[p] = odd
 
 
-def again_kernel(even, odd, chip, met, even2, odd2, chip2):
+def again_kernel(cross, even, odd, chip, met, cross2, even2, odd2, chip2):
+    even2[...] = even[...]
+    cross2[...] = cross[...]
+    odd2[...] = odd[...]
     chip2[...] = chip[...]
-    even2[...] = even[...]
-    odd2[...] = odd[...]
 
 
 def gather_kernel(cross, even, odd, left, both):
@@ -248,7 +255,6 @@
         f2[(x + 1) * BY : (x + 2) * BY, :] = sec[x]
     lo[2 * BY : X2_D, :] = sec[1]
     hi[2 * BY : X2_D, :] = sec[6]
-    pairs, points = [], []
     for x in range(0, 8):
         f = sec[x]
         r = (
@@ -260,30 +266,27 @@
             + beside_y(f, row(f2low, x), row(f2high, x))
         )
         if x % 2:
-            pairs[-1] = pairs[-1] + r
-            points[-1] = points[-1] + d[place(x)]
+            pairs = pairs + r
+            points = points + d[place(x)]
+            at = (x // 2) * BY
+            for half in range(2):
+                sums[half, at : at + BY, :] = pairs[:, half * CZ : (half + 1) * CZ]
+                sums[2 + half, at : at + BY, :] = points[:, half * CZ : (half + 1) * CZ]
         else:
-            pairs.append(r)
-            points.append(d[place(x)])
-    sums[...] = lax.dot_general(
-        jnp.concatenate(pairs + points, axis=0),
-        halved(NZ, CZ),
-        (((1,), (0,)), ((), ())),
-        precision=lax.Precision.HIGHEST,
-        preferred_element_type=F32,
-    )
+            pairs, points = r, d[place(x)]
+    doubled = [
+        sums[k, pl.ds(0, CX * CY, stride=2), :] + sums[k, pl.ds(1, CX * CY, stride=2), :] for k in range(4)
+    ]
+    total = pair_z(doubled[0], doubled[1])
+    diags = pair_z(doubled[2], doubled[3])
+    weight = OMEGA / (0.5 * diags - 18.0)
+    first = weight * (0.5 * total)
+    c1[...] = first
+    wc[...] = weight
     for x in range(CX):
-        at = x * BY
-        total = sums[pl.ds(at, CY, stride=2), :] + sums[pl.ds(at + 1, CY, stride=2), :]
-        at = (CX + x) * BY
-        diags = sums[pl.ds(at, CY, stride=2), :] + sums[pl.ds(at + 1, CY, stride=2), :]
-        weight = OMEGA / (0.5 * diags - 18.0)
-        first = weight * (0.5 * total)
-        c1[x * CY : (x + 1) * CY, :] = first
-        wc[x * CY : (x + 1) * CY, :] = weight
         for out, k in ((lo, x), (hi, CX - 1 - x)):
-            out[k * CY : (k + 1) * CY, 0:CZ] = first
-            out[k * CY : (k + 1) * CY, CZ:] = weight
+            out[k * CY : (k + 1) * CY, 0:CZ] = first[x * CY : (x + 1) * CY]
+            out[k * CY : (k + 1) * CY, CZ:] = weight[x * CY : (x + 1) * CY]
 
 
 class Coarse:
@@ -323,7 +326,7 @@
     at_ys = wys * by_y
     at_xs = wxs * by_x
     total = at_y + at_x + beside_z(at_q) - dq * at_q + 2.0 * at_q + at_ys + at_xs
-    return at_q, at_y, at_x, at_ys, at_xs, 0.5 * pair_z(total)
+    return at_q, at_y, at_x, at_ys, at_xs, 0.5 * pair_z(total[:, :CZ], total[:, CZ:])
 
 
 Z_C, Z_P, Z_W, Z_Q, Z_R, Z_V, Z_S, Z_K = 0, 10, 20, 30, 38, 44, 50, 66
@@ -347,27 +350,28 @@
         terms[k] = v
     rows[...] = share
     a = Coarse(c1x, wc, cleft, cright)
-    for x in range(CX):
-        c1x[(x + CX) * CY : (x + CX + 1) * CY, :] = slab(c1, x, CY)
+    for x in range(1, CX):
         c1x[(CX - 1 - x) * CY : (CX - x) * CY, :] = cleft[x * CY : (x + 1) * CY, 0:CZ]
         c1x[(x + 2 * CX) * CY : (x + 2 * CX + 1) * CY, :] = cright[x * CY : (x + 1) * CY, 0:CZ]
-    f2[...] = f2in[...]
-    f2low[...] = f2lowin[...]
-    f2high[...] = f2highin[...]
-
-    def add(ref, k, v):
-        ref[k : k + 1, :] = ref[k : k + 1, :] + v
-
-    for e, (xe, xi, xn, cxe, cxn) in enumerate(((0, 1, -1, 0, -1), (7, 6, 8, 3, 4))):
-        for s, (side, y, yi, cy) in enumerate(((f2low, 0, 1, 0), (f2high, BY - 1, BY - 2, CY - 1))):
-            i = 2 * e + s
-            add(f2, (xe + 1) * BY + y, terms[0, i : i + 1, :])
-            add(side, xe, terms[1, i : i + 1, :])
-            add(f2, (xn + 1) * BY + y, terms[2, i : i + 1, :])
-            add(side, xi, terms[3, i : i + 1, :])
-            add(f2, (xn + 1) * BY + yi, terms[4, i : i + 1, :])
-            add(c1x, (cxe + CX) * CY + cy, a.w(cxe)[cy : cy + 1] * rows[i : i + 1, :])
-            add(c1x, (cxn + CX) * CY + cy, a.w(cxn)[cy : cy + 1] * rows[i + 4 : i + 5, :])
+    for x in range(1, CX - 1):
+        c1x[(x + CX) * CY : (x + CX + 1) * CY, :] = slab(c1, x, CY)
+    term = lambda k, e, s: terms[k, 2 * e + s : 2 * e + s + 1, :]
+    for e, (xe, xn, cxe, cxn) in enumerate(((0, -1, 0, -1), (7, 8, 3, 4))):
+        at = (xe + 1) * BY
+        f2[at : at + BY, :] = f2in[at : at + BY, :] + by_row(BY, {0: term(0, e, 0), BY - 1: term(0, e, 1)})
+        at = (xn + 1) * BY
+        f2[at : at + BY, :] = f2in[at : at + BY, :] + by_row(
+            BY, {0: term(2, e, 0), 1: term(4, e, 0), BY - 2: term(4, e, 1), BY - 1: term(2, e, 1)}
+        )
+        for i, cx in ((2 * e, cxe), (2 * e + 4, cxn)):
+            at = (cx + CX) * CY
+            given = slab(c1, cx, CY) if 0 <= cx < CX else (cleft if cx < 0 else cright)[0:CY, 0:CZ]
+            c1x[at : at + CY, :] = given + a.w(cx) * by_row(CY, {0: row(rows, i), CY - 1: row(rows, i + 1)})
+    f2[2 * BY : 8 * BY, :] = f2in[2 * BY : 8 * BY, :]
+    for s, (side, sidein) in enumerate(((f2low, f2lowin), (f2high, f2highin))):
+        side[...] = sidein[...] + by_row(
+            BX, {0: term(1, 0, s), 1: term(3, 0, s), BX - 2: term(3, 1, s), BX - 1: term(1, 1, s)}
+        )
     lo, hi = sides.at[0], sides.at[1]
     second = {}
     for x in range(-3, 7):
@@ -472,13 +476,7 @@
             * (line3[s, 0:6, :] + line3[s, 2:8, :] + beside_z(mid) + third + col[0:6, :])
         )
         fine[6 * BY + 8 * s + 6 : 6 * BY + 8 * s + 8, :] = jnp.zeros((2, CZ), F32)
-    corr[...] = lax.dot_general(
-        fine[...],
-        halved(CZ, NZ),
-        (((1,), (0,)), ((), ())),
-        precision=lax.Precision.HIGHEST,
-        preferred_element_type=F32,
-    )
+    spread_z(fine[...], corr)
     g0 = {}
     for x in range(-2, 10):
         if x == -2:
@@ -533,10 +531,17 @@
         )
 
 
-def swap(v, pairs):
+def swap(v, links):
     n = lax.axis_size("dev")
-    links = [(i * n + j, k * n + l) for (i, j), (k, l) in pairs]
-    return lax.ppermute(v, ("group", "dev"), links + [(j, i) for i, j in links])
+    return lax.ppermute(v, ("group", "dev"), [(i * n + j, k * n + l) for (i, j), (k, l) in links])
+
+
+def both_ways(pairs):
+    return pairs + one_way_back(pairs)
+
+
+def one_way_back(pairs):
+    return [(j, i) for i, j in pairs]
 
 
 def share_chip(v):
@@ -554,31 +559,41 @@
     return [((i, d), (i, d + 1)) for i in range(lax.axis_size("group")) for d in devs]
 
 
+def is_start(d):
+    return d % RUN == 0
+
+
 def is_end(d):
     return d % RUN == RUN - 1
 
 
+def near_end(d):
+    return is_end(d) or before_end(d)
+
+
 def before_end(d):
     return d % RUN == RUN - 2
 
 
 def body(g, b, n):
     block = (BX, BY, NZ)
-    cross, cross2, chip, even, odd, f1z, g, b, w, d = call(
+    cross, chip, even, odd, f1z, g, b, w, d = call(
         load_kernel,
-        [(X_ROWS, NZ)] * 3 + [(Y_ROWS, NZ)] * 2 + [(BX * BY, NZ)] + [block] * 4,
+        [(X_ROWS, NZ)] * 2 + [(Y_ROWS, NZ)] * 2 + [(BX * BY, NZ)] + [block] * 4,
         g, b, n,
         hbm=3,
         vmem=None,
         scratch=[pltpu.VMEM(block, jnp.int32), (2, Y_ROWS, NZ), pltpu.SemaphoreType.DMA((3,))],
     )
-    cross1 = swap(cross, cross_pairs(lambda d: not is_end(d)))
-    even1 = swap(even, dev_pairs(0, lambda d: not before_end(d)))
-    odd1 = swap(odd, dev_pairs(1, lambda d: not before_end(d + 1)))
-    cross2 = swap(cross2, cross_pairs(is_end))
-    even2, odd2, chip = call(again_kernel, [(Y_ROWS, NZ)] * 2 + [(X_ROWS, NZ)], even, odd, chip, even1)
-    even2 = swap(even2, dev_pairs(0, before_end))
-    odd2 = swap(odd2, dev_pairs(1, lambda d: before_end(d + 1)))
+    cross1 = swap(cross, both_ways(cross_pairs(lambda d: not near_end(d))))
+    even1 = swap(even, both_ways(dev_pairs(0, lambda d: not before_end(d))))
+    odd1 = swap(odd, both_ways(dev_pairs(1, lambda d: not before_end(d + 1))))
+    cross2, even2, odd2, chip = call(
+        again_kernel, [(X_ROWS, NZ), (Y_ROWS, NZ), (Y_ROWS, NZ), (X_ROWS, NZ)], cross, even, odd, chip, even1
+    )
+    even2 = swap(even2, both_ways(dev_pairs(0, before_end)))
+    odd2 = swap(odd2, both_ways(dev_pairs(1, lambda d: before_end(d + 1))))
+    cross2 = swap(cross2, both_ways(cross_pairs(near_end)))
     chip = share_chip(chip)
     left, both = call(
         gather_kernel,
@@ -590,9 +605,9 @@
         middle_kernel,
         [(10 * BY, NZ), (BX, NZ), (BX, NZ), (CX * CY, CZ), (CX * CY, CZ), (X_ROWS, NZ), (2, Y_ROWS, NZ)] + [(X2_ROWS, NZ)] * 2,
         g, b, w, d, left, cross2, chip, f1z, both, even2, odd2,
-        scratch=[(16, NZ), (2, 16, NZ), (8 * BY, CZ)],
+        scratch=[(16, NZ), (2, 16, NZ), (4, CX * BY, CZ)],
     )
-    cleft = swap(cross, cross_pairs(lambda d: True))
+    cleft = swap(cross, both_ways(cross_pairs(lambda d: True)))
     cchip = share_chip(near)
     even, even2, odd, f2, f2low, f2high, c1x, c2z = call(
         pack_c_kernel,
@@ -600,9 +615,10 @@
         g, b, w, left, chip, both, f2, f2low, f2high, c1, wc, cleft, cchip,
         scratch=[(13, 8, NZ), (5, 8, NZ), (8, CZ), (2, Z_ROWS, CZ)],
     )
-    even1 = swap(even, dev_pairs(0, lambda d: not before_end(d)))
-    odd = swap(odd, dev_pairs(1, lambda d: True))
-    even2 = swap(even2, dev_pairs(0, before_end))
+    first = dev_pairs(0, is_start)
+    even1 = swap(even, both_ways(dev_pairs(0, lambda d: not (is_start(d) or before_end(d)))) + one_way_back(first))
+    odd = swap(odd, both_ways(dev_pairs(1, lambda d: True)))
+    even2 = swap(even2, both_ways(dev_pairs(0, before_end)) + first)
     (out,) = call(
         last_kernel,
         [block],

time: 43.7 us -> 44.1 us (level)
  the two profiles are of different devices: /device:TPU:25 before, /device:TPU:62 now
where the time goes in v8:
time: 44.1 us; the launch traced here: 43.8 us
  starting transfers between devices  30.2 us (68%)
  waiting for transfers between devices  6.19 us (14%)
  blocking collectives  3.87 us (9%)
  Pallas kernels  3.39 us (8%)
    ppermute x10, starting transfers between devices, swap(): lax.ppermute(v, ('group', 'dev'), [(i * n + j, k * n + l) for (i, j), (k,...  30.2 us
    ppermute x10, waiting for transfers between devices, swap(): lax.ppermute(v, ('group', 'dev'), [(i * n + j, k * n + l) for (i, j), (k,...  6.19 us
    all_gather x2, blocking collectives, share_chip(): return lax.all_gather(v, 'group', axis_index_groups=groups)  3.87 us
    pallas_call x6, Pallas kernels, call(): pl.pallas_call(kernel, out_shape=[make(s, F32) for s in outs], in_specs=[...  3.39 us
  transfers between devices with their start and end apart: 10, of which 3 were waited for; matrix products, arithmetic and copies ran while one was open for 0% of the time, Pallas kernels for 0%

profile of v8, /device:TPU:62, one launch (start us, length us, event | category | flops | bytes accessed | tf_op | source)
XLA Modules:
  0.0 43.8 jit_solution(4158069833104283261)
XLA Ops:
  0.0 1.2 %shard_map.37 = (f32[112,256]{1,0:T(8,128)S(1)}, f32[112,256]{1,0:T(8,128)S(1)}, f32[40,256]{1,0:T(8,128)S(1)}, f32[40,256]{1,0:T(8,128)S(1)}, f32[128,256]{1,0:...) custom-call(f32[8,16,256]{2,1,0:T(8,128)} %g_hbm.1, ...), custom_call_target="tpu_custom_call" | custom-call | tf_op jit(solution)/shard_map/pallas_call | solution.py:19
  1.3 2.2 %collective-permute-start = (f32[112,256]{1,0:T(8,128)S(1)}, f32[112,256]{1,0:T(8,128)S(1)}, u32[]{:S(2)}, u32[]{:S(2)}) collective-permute-start(f32[112,256]{1,0:T(8,128)S(1)} %get-tuple-element.41.cross), channel_id=1, source_target_pairs={{128,256},{129,257},{130,258},{131,259},{132,260},{133,261},{134,2... | collective-permute-start | bytes 344072 | tf_op jit(solution)/shard_map/ppermute | solution.py:536
  3.4 2.0 %collective-permute-start.1 = (f32[40,256]{1,0:T(8,128)S(1)}, f32[40,256]{1,0:T(8,128)S(1)}, u32[]{:S(2)}, u32[]{:S(2)}) collective-permute-start(f32[40,256]{1,0:T(8,128)S(1)} %get-tuple-element.42.even), channel_id=1, source_target_pairs={{0,1},{2,3},{4,5},{6,7},{8,9},{10,11},{12,13},{14,15},{16,17},{18,... | collective-permute-start | bytes 122888 | tf_op jit(solution)/shard_map/ppermute | solution.py:536
  5.5 5.6 %collective-permute-start.2 = (f32[40,256]{1,0:T(8,128)S(1)}, f32[40,256]{1,0:T(8,128)S(1)}, u32[]{:S(2)}, u32[]{:S(2)}) collective-permute-start(f32[40,256]{1,0:T(8,128)S(1)} %get-tuple-element.43.odd), channel_id=1, source_target_pairs={{1,2},{3,4},{5,6},{7,8},{9,10},{11,12},{13,14},{15,16},{17,18},{19... | collective-permute-start | bytes 122888 | tf_op jit(solution)/shard_map/ppermute | solution.py:536
  11.1 0.0 collective-permute-done.1.even.met
  11.2 0.7 %collective-permute-start.4 = (f32[40,256]{1,0:T(8,128)S(1)}, f32[40,256]{1,0:T(8,128)S(1)}, u32[]{:S(2)}, u32[]{:S(2)}) collective-permute-start(f32[40,256]{1,0:T(8,128)S(1)} %get-tuple-element.50), channel_id=1, source_target_pairs={{30,31},{62,63},{94,95},{126,127},{158,159},{190,191},{222,223},{2... | collective-permute-start | bytes 122888 | tf_op jit(solution)/shard_map/ppermute | solution.py:536
  11.8 0.7 %collective-permute-start.5 = (f32[40,256]{1,0:T(8,128)S(1)}, f32[40,256]{1,0:T(8,128)S(1)}, u32[]{:S(2)}, u32[]{:S(2)}) collective-permute-start(f32[40,256]{1,0:T(8,128)S(1)} %get-tuple-element.51), channel_id=1, source_target_pairs={{29,30},{61,62},{93,94},{125,126},{157,158},{189,190},{221,222},{2... | collective-permute-start | bytes 122888 | tf_op jit(solution)/shard_map/ppermute | solution.py:536
  12.5 0.7 %collective-permute-start.3 = (f32[112,256]{1,0:T(8,128)S(1)}, f32[112,256]{1,0:T(8,128)S(1)}, u32[]{:S(2)}, u32[]{:S(2)}) collective-permute-start(f32[112,256]{1,0:T(8,128)S(1)} %get-tuple-element.46), channel_id=1, source_target_pairs={{158,286},{159,287},{190,318},{191,319},{222,350},{223,351},{254,3... | collective-permute-start | bytes 344072 | tf_op jit(solution)/shard_map/ppermute | solution.py:536
  13.2 2.0 %all-gather = f32[224,256]{1,0:T(8,128)S(1)} all-gather(f32[112,256]{1,0:T(8,128)S(1)} %get-tuple-element.47), channel_id=2, replica_groups={{0,128},{256,384},{512,640},{768,896},{1,129},{257,385},{513,641},{769,..., dimensions={0}, use_global_device_ids=true | all-gather | bytes 344064 | tf_op jit(solution)/shard_map/all_gather | solution.py:549
  15.1 0.0 collective-permute-done.cross
  15.2 0.0 collective-permute-done.5.odd2
  15.2 0.0 collective-permute-done.3.cross2
  15.2 0.5 %shard_map.40 = (f32[160,256]{1,0:T(8,128)S(1)}, f32[8,256]{1,0:T(8,128)S(1)}, f32[8,256]{1,0:T(8,128)S(1)}, f32[32,128]{1,0:T(8,128)S(1)}, f32[32,128]{1,0:T(8,...) custom-call(f32[8,16,256]{2,1,0:T(8,128)S(1)} %get-tuple-element.37., ...), custom_call_target="tpu_custom_call" | custom-call | tf_op jit(solution)/shard_map/pallas_call | solution.py:19
  15.7 2.8 %collective-permute-start.6 = (f32[64,256]{1,0:T(8,128)S(1)}, f32[64,256]{1,0:T(8,128)S(1)}, u32[]{:S(2)}, u32[]{:S(2)}) collective-permute-start(f32[64,256]{1,0:T(8,128)S(1)} %get-tuple-element.59), channel_id=1, source_target_pairs={{128,256},{129,257},{130,258},{131,259},{132,260},{133,261},{134,2... | collective-permute-start | bytes 196616 | tf_op jit(solution)/shard_map/ppermute | solution.py:536
  18.5 1.9 %all-gather.1 = f32[128,256]{1,0:T(8,128)S(1)} all-gather(f32[64,256]{1,0:T(8,128)S(1)} %get-tuple-element.60), channel_id=3, replica_groups={{0,128},{256,384},{512,640},{768,896},{1,129},{257,385},{513,641},{769,..., dimensions={0}, use_global_device_ids=true | all-gather | bytes 196608 | tf_op jit(solution)/shard_map/all_gather | solution.py:549
  20.4 0.9 %collective-permute-done.6.cleft = f32[64,256]{1,0:T(8,128)S(1)} collective-permute-done((f32[64,256]{1,0:T(8,128)S(1)}, f32[64,256]{1,0:T(8,128)S(1)}, u32[]{:S(2)}, u32[]{:S(2)}) %collective-permute-start.6) | collective-permute-done | bytes 65568 | tf_op jit(solution)/shard_map/ppermute | solution.py:536
  21.3 0.4 shard_map.41
  21.7 12.4 %collective-permute-start.7 = (f32[72,128]{1,0:T(8,128)S(1)}, f32[72,128]{1,0:T(8,128)S(1)}, u32[]{:S(2)}, u32[]{:S(2)}) collective-permute-start(f32[72,128]{1,0:T(8,128)S(1)} %get-tuple-element.66), channel_id=1, source_target_pairs={{2,3},{4,5},{6,7},{8,9},{10,11},{12,13},{14,15},{16,17},{18,19},{2... | collective-permute-start | bytes 110600 | tf_op jit(solution)/shard_map/ppermute | solution.py:536
  34.1 1.9 %collective-permute-start.8 = (f32[72,128]{1,0:T(8,128)S(1)}, f32[72,128]{1,0:T(8,128)S(1)}, u32[]{:S(2)}, u32[]{:S(2)}) collective-permute-start(f32[72,128]{1,0:T(8,128)S(1)} %get-tuple-element.67), channel_id=1, source_target_pairs={{1,2},{3,4},{5,6},{7,8},{9,10},{11,12},{13,14},{15,16},{17,18},{19... | collective-permute-start | bytes 110600 | tf_op jit(solution)/shard_map/ppermute | solution.py:536
  36.0 1.3 %collective-permute-start.9 = (f32[72,128]{1,0:T(8,128)S(1)}, f32[72,128]{1,0:T(8,128)S(1)}, u32[]{:S(2)}, u32[]{:S(2)}) collective-permute-start(f32[72,128]{1,0:T(8,128)S(1)} %get-tuple-element.68), channel_id=1, source_target_pairs={{30,31},{62,63},{94,95},{126,127},{158,159},{190,191},{222,223},{2... | collective-permute-start | bytes 110600 | tf_op jit(solution)/shard_map/ppermute | solution.py:536
  37.3 0.0 collective-permute-done.7.even1
  37.3 2.6 %collective-permute-done.8.odd = f32[72,128]{1,0:T(8,128)S(1)} collective-permute-done((f32[72,128]{1,0:T(8,128)S(1)}, f32[72,128]{1,0:T(8,128)S(1)}, u32[]{:S(2)}, u32[]{:S(2)}) %collective-permute-start.8) | collective-permute-done | bytes 36896 | tf_op jit(solution)/shard_map/ppermute | solution.py:536
  39.9 2.7 %collective-permute-done.9.even2 = f32[72,128]{1,0:T(8,128)S(1)} collective-permute-done((f32[72,128]{1,0:T(8,128)S(1)}, f32[72,128]{1,0:T(8,128)S(1)}, u32[]{:S(2)}, u32[]{:S(2)}) %collective-permute-start.9) | collective-permute-done | bytes 36896 | tf_op jit(solution)/shard_map/ppermute | solution.py:536
  42.6 1.2 %shard_map.42 = f32[8,16,256]{2,1,0:T(8,128)} custom-call(f32[8,16,256]{2,1,0:T(8,128)S(1)} %get-tuple-element.37.g, f32[8,16,256]{2,1,0:T(8,128)S(1)} %get-tuple-element.38.b, f32[8,16,256]{2,1,0:T(8,128)S(1)} %get-tuple-element.39.w, f32[112,256]{1,0:T(8,128)S(1)} %get-tuple-element.52.left, f32[2,112,256]{2,1,0:T(8,128)S(1)} %bitcast.4, ...), custom_call_target="tpu_custom_call" | custom-call | tf_op jit(solution)/shard_map/pallas_call | solution.py:19
  (4 shorter events, 0.0 us)
Async XLA Ops:
  1.3 13.9 %collective-permute-start = (f32[112,256]{1,0:T(8,128)S(1)}, f32[112,256]{1,0:T(8,128)S(1)}, u32[]{:S(2)}, u32[]{:S(2)}) collective-permute-start(f32[112,256]{1,0:T(8,128)S(1)} %get-tuple-element.41.cross), channel_id=1, source_target_pairs={{128,256},{129,257},{130,258},{131,259},{132,260},{133,261},{134,2... | collective-permute-start | bytes 344072 | tf_op jit(solution)/shard_map/ppermute | solution.py:536
  3.4 7.7 %collective-permute-start.1 = (f32[40,256]{1,0:T(8,128)S(1)}, f32[40,256]{1,0:T(8,128)S(1)}, u32[]{:S(2)}, u32[]{:S(2)}) collective-permute-start(f32[40,256]{1,0:T(8,128)S(1)} %get-tuple-element.42.even), channel_id=1, source_target_pairs={{0,1},{2,3},{4,5},{6,7},{8,9},{10,11},{12,13},{14,15},{16,17},{18,... | collective-permute-start | bytes 122888 | tf_op jit(solution)/shard_map/ppermute | solution.py:536
  5.5 9.7 %collective-permute-start.2 = (f32[40,256]{1,0:T(8,128)S(1)}, f32[40,256]{1,0:T(8,128)S(1)}, u32[]{:S(2)}, u32[]{:S(2)}) collective-permute-start(f32[40,256]{1,0:T(8,128)S(1)} %get-tuple-element.43.odd), channel_id=1, source_target_pairs={{1,2},{3,4},{5,6},{7,8},{9,10},{11,12},{13,14},{15,16},{17,18},{19... | collective-permute-start | bytes 122888 | tf_op jit(solution)/shard_map/ppermute | solution.py:536
  11.2 4.0 %collective-permute-start.4 = (f32[40,256]{1,0:T(8,128)S(1)}, f32[40,256]{1,0:T(8,128)S(1)}, u32[]{:S(2)}, u32[]{:S(2)}) collective-permute-start(f32[40,256]{1,0:T(8,128)S(1)} %get-tuple-element.50), channel_id=1, source_target_pairs={{30,31},{62,63},{94,95},{126,127},{158,159},{190,191},{222,223},{2... | collective-permute-start | bytes 122888 | tf_op jit(solution)/shard_map/ppermute | solution.py:536
  11.8 3.4 %collective-permute-start.5 = (f32[40,256]{1,0:T(8,128)S(1)}, f32[40,256]{1,0:T(8,128)S(1)}, u32[]{:S(2)}, u32[]{:S(2)}) collective-permute-start(f32[40,256]{1,0:T(8,128)S(1)} %get-tuple-element.51), channel_id=1, source_target_pairs={{29,30},{61,62},{93,94},{125,126},{157,158},{189,190},{221,222},{2... | collective-permute-start | bytes 122888 | tf_op jit(solution)/shard_map/ppermute | solution.py:536
  12.5 2.7 %collective-permute-start.3 = (f32[112,256]{1,0:T(8,128)S(1)}, f32[112,256]{1,0:T(8,128)S(1)}, u32[]{:S(2)}, u32[]{:S(2)}) collective-permute-start(f32[112,256]{1,0:T(8,128)S(1)} %get-tuple-element.46), channel_id=1, source_target_pairs={{158,286},{159,287},{190,318},{191,319},{222,350},{223,351},{254,3... | collective-permute-start | bytes 344072 | tf_op jit(solution)/shard_map/ppermute | solution.py:536
  15.7 5.6 %collective-permute-start.6 = (f32[64,256]{1,0:T(8,128)S(1)}, f32[64,256]{1,0:T(8,128)S(1)}, u32[]{:S(2)}, u32[]{:S(2)}) collective-permute-start(f32[64,256]{1,0:T(8,128)S(1)} %get-tuple-element.59), channel_id=1, source_target_pairs={{128,256},{129,257},{130,258},{131,259},{132,260},{133,261},{134,2... | collective-permute-start | bytes 196616 | tf_op jit(solution)/shard_map/ppermute | solution.py:536
  21.7 15.6 %collective-permute-start.7 = (f32[72,128]{1,0:T(8,128)S(1)}, f32[72,128]{1,0:T(8,128)S(1)}, u32[]{:S(2)}, u32[]{:S(2)}) collective-permute-start(f32[72,128]{1,0:T(8,128)S(1)} %get-tuple-element.66), channel_id=1, source_target_pairs={{2,3},{4,5},{6,7},{8,9},{10,11},{12,13},{14,15},{16,17},{18,19},{2... | collective-permute-start | bytes 110600 | tf_op jit(solution)/shard_map/ppermute | solution.py:536
  34.1 5.9 %collective-permute-start.8 = (f32[72,128]{1,0:T(8,128)S(1)}, f32[72,128]{1,0:T(8,128)S(1)}, u32[]{:S(2)}, u32[]{:S(2)}) collective-permute-start(f32[72,128]{1,0:T(8,128)S(1)} %get-tuple-element.67), channel_id=1, source_target_pairs={{1,2},{3,4},{5,6},{7,8},{9,10},{11,12},{13,14},{15,16},{17,18},{19... | collective-permute-start | bytes 110600 | tf_op jit(solution)/shard_map/ppermute | solution.py:536
  36.0 6.6 %collective-permute-start.9 = (f32[72,128]{1,0:T(8,128)S(1)}, f32[72,128]{1,0:T(8,128)S(1)}, u32[]{:S(2)}, u32[]{:S(2)}) collective-permute-start(f32[72,128]{1,0:T(8,128)S(1)} %get-tuple-element.68), channel_id=1, source_target_pairs={{30,31},{62,63},{94,95},{126,127},{158,159},{190,191},{222,223},{2... | collective-permute-start | bytes 110600 | tf_op jit(solution)/shard_map/ppermute | solution.py:536

commit v9 on v8

--- a/solution.py
+++ b/solution.py
@@ -95,6 +95,10 @@
     return ref.at[1 - lax.axis_index("group") % 2]
 
 
+def at_end_of_run():
+    return lax.axis_index("dev") % RUN == RUN - 1
+
+
 def side_of_dev():
     return lax.axis_index("dev") % 2
 
@@ -105,7 +109,7 @@
 
 
 def load_kernel(
-    g_hbm, b_hbm, n_hbm, cross, chip, even, odd, f1z, g, b, w, d, n, both, sems
+    g_hbm, b_hbm, n_hbm, cross, fourth, last, even, odd, f1z, g, b, w, d, n, both, chip, sems
 ):
     copies = [
         pltpu.make_async_copy(src, dst, sems.at[k])
@@ -147,11 +151,18 @@
     p = side_of_dev()
     even[...] = both[1 - p]
     odd[...] = both[p]
+    end = at_end_of_run()
+    fourth[...] = jnp.where(end, cross[...], chip[...])
+    last[...] = chip[...]
+
+    @pl.when(jnp.logical_not(end))
+    def _():
+        last[0:Y_ROWS, :] = both[p]
 
 
 class Wide:
     def __init__(self, g, b, w, left, right):
-        self.own, self.left, self.right = (g, w, b), left, partner(right)
+        self.own, self.left, self.right = (g, w, b), left, right
 
     def _get(self, which, base, x, y):
         if 0 <= x < BX:
@@ -176,11 +187,9 @@
     both[p] = odd
 
 
-def again_kernel(cross, even, odd, chip, met, cross2, even2, odd2, chip2):
+def again_kernel(even, last, met, even2, last2):
     even2[...] = even[...]
-    cross2[...] = cross[...]
-    odd2[...] = odd[...]
-    chip2[...] = chip[...]
+    last2[...] = last[...]
 
 
 def gather_kernel(cross, even, odd, left, both):
@@ -198,13 +207,15 @@
 
 
 def middle_kernel(
-    g, b, w, d, left1, cross2, chip, f1z, both1, even2, odd2,
-    f2, f2low, f2high, c1, wc, left, both, lo, hi, col, line, sums,
+    g, b, w, d, left1, fourth, f1z, both1, even2, last,
+    f2, f2low, f2high, c1, wc, left, right, both, lo, hi, col, line, sums,
 ):
-    left[...] = left1[...] + cross2[...]
-    a = Wide(g, b, w, left, chip)
+    end = at_end_of_run()
+    left[...] = left1[...] + jnp.where(end, fourth[...], 0.0)
+    right[...] = jnp.where(end, last[...], fourth[...])
+    a = Wide(g, b, w, left, right)
     p = side_of_dev()
-    both[p] = both1[p] + odd2[...]
+    both[p] = both1[p] + jnp.where(end, 0.0, last[0:Y_ROWS, :])
     both[1 - p] = both1[1 - p] + even2[...]
     low, high = both.at[0], both.at[1]
     rows = lax.broadcasted_iota(jnp.int32, (BY, NZ), 0)
@@ -334,10 +345,10 @@
 
 
 def pack_c_kernel(
-    g, b, w, left, chip, both, f2in, f2lowin, f2highin, c1, wc, cleft, cchip,
+    g, b, w, left, right, both, f2in, f2lowin, f2highin, c1, wc, cleft, cchip,
     even, even2, odd, f2, f2low, f2high, c1x, c2z, table, terms, rows, sides,
 ):
-    fine = Wide(g, b, w, left, chip)
+    fine = Wide(g, b, w, left, right)
     cright = partner(cchip)
 
     def put(i, values):
@@ -418,10 +429,10 @@
 
 
 def last_kernel(
-    g, b, w, left, chip, both, f2, f2low, f2high, c1x, wc, cleft, cchip, c2z, even1, odd, even2,
+    g, b, w, left, right, both, f2, f2low, f2high, c1x, wc, cleft, cchip, c2z, even1, odd, even2,
     out, cboth, col, line, line3, fine, corr, col2, s1, gline, g1line,
 ):
-    wide = Wide(g, b, w, left, chip)
+    wide = Wide(g, b, w, left, right)
     a = Coarse(c1x, wc, cleft, partner(cchip))
     take(cboth, even1[...] + even2[...], odd[...])
     low, high, clow, chigh = both.at[0], both.at[1], cboth.at[0], cboth.at[1]
@@ -531,17 +542,10 @@
         )
 
 
-def swap(v, links):
+def swap(v, pairs):
     n = lax.axis_size("dev")
-    return lax.ppermute(v, ("group", "dev"), [(i * n + j, k * n + l) for (i, j), (k, l) in links])
-
-
-def both_ways(pairs):
-    return pairs + one_way_back(pairs)
-
-
-def one_way_back(pairs):
-    return [(j, i) for i, j in pairs]
+    links = [(i * n + j, k * n + l) for (i, j), (k, l) in pairs]
+    return lax.ppermute(v, ("group", "dev"), links + [(j, i) for i, j in links])
 
 
 def share_chip(v):
@@ -554,75 +558,68 @@
     return [((i, d), (i + 1, d)) for i in range(1, lax.axis_size("group") - 1, 2) for d in devs]
 
 
+def chip_pairs(keep):
+    devs = [d for d in range(lax.axis_size("dev")) if keep(d)]
+    return [((i, d), (i + 1, d)) for i in range(0, lax.axis_size("group"), 2) for d in devs]
+
+
 def dev_pairs(start, keep):
     devs = [d for d in range(start, lax.axis_size("dev") - 1, 2) if keep(d)]
     return [((i, d), (i, d + 1)) for i in range(lax.axis_size("group")) for d in devs]
 
 
-def is_start(d):
-    return d % RUN == 0
-
-
 def is_end(d):
     return d % RUN == RUN - 1
 
 
-def near_end(d):
-    return is_end(d) or before_end(d)
-
-
 def before_end(d):
     return d % RUN == RUN - 2
 
 
 def body(g, b, n):
     block = (BX, BY, NZ)
-    cross, chip, even, odd, f1z, g, b, w, d = call(
+    cross, fourth, last, even, odd, f1z, g, b, w, d = call(
         load_kernel,
-        [(X_ROWS, NZ)] * 2 + [(Y_ROWS, NZ)] * 2 + [(BX * BY, NZ)] + [block] * 4,
+        [(X_ROWS, NZ)] * 3 + [(Y_ROWS, NZ)] * 2 + [(BX * BY, NZ)] + [block] * 4,
         g, b, n,
         hbm=3,
         vmem=None,
-        scratch=[pltpu.VMEM(block, jnp.int32), (2, Y_ROWS, NZ), pltpu.SemaphoreType.DMA((3,))],
+        scratch=[pltpu.VMEM(block, jnp.int32), (2, Y_ROWS, NZ), (X_ROWS, NZ), pltpu.SemaphoreType.DMA((3,))],
     )
-    cross1 = swap(cross, both_ways(cross_pairs(lambda d: not near_end(d))))
-    even1 = swap(even, both_ways(dev_pairs(0, lambda d: not before_end(d))))
-    odd1 = swap(odd, both_ways(dev_pairs(1, lambda d: not before_end(d + 1))))
-    cross2, even2, odd2, chip = call(
-        again_kernel, [(X_ROWS, NZ), (Y_ROWS, NZ), (Y_ROWS, NZ), (X_ROWS, NZ)], cross, even, odd, chip, even1
-    )
-    even2 = swap(even2, both_ways(dev_pairs(0, before_end)))
-    odd2 = swap(odd2, both_ways(dev_pairs(1, lambda d: before_end(d + 1))))
-    cross2 = swap(cross2, both_ways(cross_pairs(near_end)))
-    chip = share_chip(chip)
+    cross1 = swap(cross, cross_pairs(lambda d: not is_end(d)))
+    even1 = swap(even, dev_pairs(0, lambda d: not before_end(d)))
+    odd1 = swap(odd, dev_pairs(1, lambda d: not before_end(d + 1)))
+    fourth = swap(fourth, chip_pairs(lambda d: not is_end(d)) + cross_pairs(is_end))
+    even2, last = call(again_kernel, [(Y_ROWS, NZ), (X_ROWS, NZ)], even, last, even1)
+    even2 = swap(even2, dev_pairs(0, before_end))
+    last = swap(last, dev_pairs(1, lambda d: before_end(d + 1)) + chip_pairs(is_end))
     left, both = call(
         gather_kernel,
         [(X_ROWS, NZ), (2, Y_ROWS, NZ)],
         cross1, even1, odd1,
         cost=pl.CostEstimate(flops=2**34, bytes_accessed=0, transcendentals=0),
     )
-    f2, f2low, f2high, c1, wc, left, both, cross, near = call(
+    f2, f2low, f2high, c1, wc, left, right, both, cross, near = call(
         middle_kernel,
-        [(10 * BY, NZ), (BX, NZ), (BX, NZ), (CX * CY, CZ), (CX * CY, CZ), (X_ROWS, NZ), (2, Y_ROWS, NZ)] + [(X2_ROWS, NZ)] * 2,
-        g, b, w, d, left, cross2, chip, f1z, both, even2, odd2,
+        [(10 * BY, NZ), (BX, NZ), (BX, NZ), (CX * CY, CZ), (CX * CY, CZ), (X_ROWS, NZ), (X_ROWS, NZ), (2, Y_ROWS, NZ)] + [(X2_ROWS, NZ)] * 2,
+        g, b, w, d, left, fourth, f1z, both, even2, last,
         scratch=[(16, NZ), (2, 16, NZ), (4, CX * BY, CZ)],
     )
-    cleft = swap(cross, both_ways(cross_pairs(lambda d: True)))
+    cleft = swap(cross, cross_pairs(lambda d: True))
     cchip = share_chip(near)
     even, even2, odd, f2, f2low, f2high, c1x, c2z = call(
         pack_c_kernel,
         [(Z_ROWS, CZ)] * 3 + [(10 * BY, NZ), (BX, NZ), (BX, NZ), (3 * CX * CY, CZ), (10 * CY, CZ)],
-        g, b, w, left, chip, both, f2, f2low, f2high, c1, wc, cleft, cchip,
+        g, b, w, left, right, both, f2, f2low, f2high, c1, wc, cleft, cchip,
         scratch=[(13, 8, NZ), (5, 8, NZ), (8, CZ), (2, Z_ROWS, CZ)],
     )
-    first = dev_pairs(0, is_start)
-    even1 = swap(even, both_ways(dev_pairs(0, lambda d: not (is_start(d) or before_end(d)))) + one_way_back(first))
-    odd = swap(odd, both_ways(dev_pairs(1, lambda d: True)))
-    even2 = swap(even2, both_ways(dev_pairs(0, before_end)) + first)
+    even1 = swap(even, dev_pairs(0, lambda d: not before_end(d)))
+    odd = swap(odd, dev_pairs(1, lambda d: True))
+    even2 = swap(even2, dev_pairs(0, before_end))
     (out,) = call(
         last_kernel,
         [block],
-        g, b, w, left, chip, both, f2, f2low, f2high, c1x, wc, cleft, cchip, c2z, even1, odd, even2,
+        g, b, w, left, right, both, f2, f2low, f2high, c1x, wc, cleft, cchip, c2z, even1, odd, even2,
         scratch=[
             (2, Z_ROWS, CZ),
             (16, CZ), (2, 16, CZ), (2, 8, CZ), (6 * BY + 16, CZ), (6 * BY + 16, NZ), (16, NZ), (8, NZ), (2, 16, NZ), (2, 8, NZ),

time: 44.1 us -> 43.8 us (level)
  the two profiles are of different devices: /device:TPU:62 before, /device:TPU:25 now
where the time goes in v9:
time: 43.8 us; the launch traced here: 43.5 us
  starting transfers between devices  36 us (82%)
  Pallas kernels  3.42 us (8%)
  waiting for transfers between devices  1.99 us (5%)
  blocking collectives  1.9 us (4%)
    ppermute x10, starting transfers between devices, swap(): return lax.ppermute(v, ('group', 'dev'), links + [(j, i) for i, j in links])  36 us
    pallas_call x6, Pallas kernels, call(): pl.pallas_call(kernel, out_shape=[make(s, F32) for s in outs], in_specs=[...  3.42 us
    ppermute x10, waiting for transfers between devices, swap(): return lax.ppermute(v, ('group', 'dev'), links + [(j, i) for i, j in links])  1.99 us
    all_gather x1, blocking collectives, share_chip(): return lax.all_gather(v, 'group', axis_index_groups=groups)  1.9 us
  transfers between devices with their start and end apart: 10, of which 2 were waited for; matrix products, arithmetic and copies ran while one was open for 0% of the time, Pallas kernels for 0%

profile of v9, /device:TPU:25, one launch (start us, length us, event | category | flops | bytes accessed | tf_op | source)
XLA Modules:
  0.0 43.5 jit_solution(3402343031558907959)
XLA Ops:
  0.0 1.3 %shard_map.37 = (f32[112,256]{1,0:T(8,128)S(1)}, f32[112,256]{1,0:T(8,128)S(1)}, f32[112,256]{1,0:T(8,128)S(1)}, f32[40,256]{1,0:T(8,128)S(1)}, f32[40,256]{1,0:...) custom-call(f32[8,16,256]{2,1,0:T(8,128)} %g_hbm.1, ...), custom_call_target="tpu_custom_call" | custom-call | tf_op jit(solution)/shard_map/pallas_call | solution.py:19
  1.3 3.7 %collective-permute-start = (f32[112,256]{1,0:T(8,128)S(1)}, f32[112,256]{1,0:T(8,128)S(1)}, u32[]{:S(2)}, u32[]{:S(2)}) collective-permute-start(f32[112,256]{1,0:T(8,128)S(1)} %get-tuple-element.41), channel_id=1, source_target_pairs={{128,256},{129,257},{130,258},{131,259},{132,260},{133,261},{134,2... | collective-permute-start | bytes 344072 | tf_op jit(solution)/shard_map/ppermute | solution.py:548
  5.0 3.5 %collective-permute-start.1 = (f32[40,256]{1,0:T(8,128)S(1)}, f32[40,256]{1,0:T(8,128)S(1)}, u32[]{:S(2)}, u32[]{:S(2)}) collective-permute-start(f32[40,256]{1,0:T(8,128)S(1)} %get-tuple-element.42.even), channel_id=1, source_target_pairs={{0,1},{2,3},{4,5},{6,7},{8,9},{10,11},{12,13},{14,15},{16,17},{18,... | collective-permute-start | bytes 122888 | tf_op jit(solution)/shard_map/ppermute | solution.py:548
  8.5 12.7 %collective-permute-start.2 = (f32[40,256]{1,0:T(8,128)S(1)}, f32[40,256]{1,0:T(8,128)S(1)}, u32[]{:S(2)}, u32[]{:S(2)}) collective-permute-start(f32[40,256]{1,0:T(8,128)S(1)} %get-tuple-element.43), channel_id=1, source_target_pairs={{1,2},{3,4},{5,6},{7,8},{9,10},{11,12},{13,14},{15,16},{17,18},{19... | collective-permute-start | bytes 122888 | tf_op jit(solution)/shard_map/ppermute | solution.py:548
  21.2 2.9 %collective-permute-start.3 = (f32[112,256]{1,0:T(8,128)S(1)}, f32[112,256]{1,0:T(8,128)S(1)}, u32[]{:S(2)}, u32[]{:S(2)}) collective-permute-start(f32[112,256]{1,0:T(8,128)S(1)} %get-tuple-element.45), channel_id=1, source_target_pairs={{0,128},{1,129},{2,130},{3,131},{4,132},{5,133},{6,134},{7,135},{8... | collective-permute-start | bytes 344072 | tf_op jit(solution)/shard_map/ppermute | solution.py:548
  24.1 0.0 collective-permute-done.1.even.met
  24.1 0.7 %collective-permute-start.4 = (f32[40,256]{1,0:T(8,128)S(1)}, f32[40,256]{1,0:T(8,128)S(1)}, u32[]{:S(2)}, u32[]{:S(2)}) collective-permute-start(f32[40,256]{1,0:T(8,128)S(1)} %get-tuple-element.49), channel_id=1, source_target_pairs={{30,31},{62,63},{94,95},{126,127},{158,159},{190,191},{222,223},{2... | collective-permute-start | bytes 122888 | tf_op jit(solution)/shard_map/ppermute | solution.py:548
  24.8 0.7 %collective-permute-start.5 = (f32[112,256]{1,0:T(8,128)S(1)}, f32[112,256]{1,0:T(8,128)S(1)}, u32[]{:S(2)}, u32[]{:S(2)}) collective-permute-start(f32[112,256]{1,0:T(8,128)S(1)} %get-tuple-element.50), channel_id=1, source_target_pairs={{29,30},{61,62},{93,94},{125,126},{157,158},{189,190},{221,222},{2... | collective-permute-start | bytes 344072 | tf_op jit(solution)/shard_map/ppermute | solution.py:548
  25.4 0.0 collective-permute-done.2.odd
  25.5 0.0 collective-permute-done.cross
  25.5 0.0 collective-permute-done.4.even2
  25.5 0.0 collective-permute-done.3.fourth
  25.5 0.5 %shard_map.40 = (f32[160,256]{1,0:T(8,128)S(1)}, f32[8,256]{1,0:T(8,128)S(1)}, f32[8,256]{1,0:T(8,128)S(1)}, f32[32,128]{1,0:T(8,128)S(1)}, f32[32,128]{1,0:T(8,...) custom-call(f32[8,16,256]{2,1,0:T(8,128)S(1)} %get-tuple-element.37., ...), custom_call_target="tpu_custom_call" | custom-call | tf_op jit(solution)/shard_map/pallas_call | solution.py:19
  26.0 3.0 %collective-permute-start.6 = (f32[64,256]{1,0:T(8,128)S(1)}, f32[64,256]{1,0:T(8,128)S(1)}, u32[]{:S(2)}, u32[]{:S(2)}) collective-permute-start(f32[64,256]{1,0:T(8,128)S(1)} %get-tuple-element.59), channel_id=1, source_target_pairs={{128,256},{129,257},{130,258},{131,259},{132,260},{133,261},{134,2... | collective-permute-start | bytes 196616 | tf_op jit(solution)/shard_map/ppermute | solution.py:548
  29.1 1.9 %all-gather = f32[128,256]{1,0:T(8,128)S(1)} all-gather(f32[64,256]{1,0:T(8,128)S(1)} %get-tuple-element.60), channel_id=2, replica_groups={{0,128},{256,384},{512,640},{768,896},{1,129},{257,385},{513,641},{769,..., dimensions={0}, use_global_device_ids=true | all-gather | bytes 196608 | tf_op jit(solution)/shard_map/all_gather | solution.py:553
  31.0 0.7 %collective-permute-done.6.cleft = f32[64,256]{1,0:T(8,128)S(1)} collective-permute-done((f32[64,256]{1,0:T(8,128)S(1)}, f32[64,256]{1,0:T(8,128)S(1)}, u32[]{:S(2)}, u32[]{:S(2)}) %collective-permute-start.6) | collective-permute-done | bytes 65568 | tf_op jit(solution)/shard_map/ppermute | solution.py:548
  31.6 0.4 shard_map.41
  32.1 1.9 %collective-permute-start.7 = (f32[72,128]{1,0:T(8,128)S(1)}, f32[72,128]{1,0:T(8,128)S(1)}, u32[]{:S(2)}, u32[]{:S(2)}) collective-permute-start(f32[72,128]{1,0:T(8,128)S(1)} %get-tuple-element.66), channel_id=1, source_target_pairs={{0,1},{2,3},{4,5},{6,7},{8,9},{10,11},{12,13},{14,15},{16,17},{18,... | collective-permute-start | bytes 110600 | tf_op jit(solution)/shard_map/ppermute | solution.py:548
  34.0 6.3 %collective-permute-start.8 = (f32[72,128]{1,0:T(8,128)S(1)}, f32[72,128]{1,0:T(8,128)S(1)}, u32[]{:S(2)}, u32[]{:S(2)}) collective-permute-start(f32[72,128]{1,0:T(8,128)S(1)} %get-tuple-element.67), channel_id=1, source_target_pairs={{1,2},{3,4},{5,6},{7,8},{9,10},{11,12},{13,14},{15,16},{17,18},{19... | collective-permute-start | bytes 110600 | tf_op jit(solution)/shard_map/ppermute | solution.py:548
  40.3 0.7 %collective-permute-start.9 = (f32[72,128]{1,0:T(8,128)S(1)}, f32[72,128]{1,0:T(8,128)S(1)}, u32[]{:S(2)}, u32[]{:S(2)}) collective-permute-start(f32[72,128]{1,0:T(8,128)S(1)} %get-tuple-element.68), channel_id=1, source_target_pairs={{30,31},{62,63},{94,95},{126,127},{158,159},{190,191},{222,223},{2... | collective-permute-start | bytes 110600 | tf_op jit(solution)/shard_map/ppermute | solution.py:548
  41.0 0.0 collective-permute-done.7.even1
  41.0 1.3 %collective-permute-done.8.odd = f32[72,128]{1,0:T(8,128)S(1)} collective-permute-done((f32[72,128]{1,0:T(8,128)S(1)}, f32[72,128]{1,0:T(8,128)S(1)}, u32[]{:S(2)}, u32[]{:S(2)}) %collective-permute-start.8) | collective-permute-done | bytes 36896 | tf_op jit(solution)/shard_map/ppermute | solution.py:548
  42.3 0.0 collective-permute-done.9.even2
  42.3 1.2 %shard_map.42 = f32[8,16,256]{2,1,0:T(8,128)} custom-call(f32[8,16,256]{2,1,0:T(8,128)S(1)} %get-tuple-element.37.g, f32[8,16,256]{2,1,0:T(8,128)S(1)} %get-tuple-element.38.b, f32[8,16,256]{2,1,0:T(8,128)S(1)} %get-tuple-element.39.w, f32[112,256]{1,0:T(8,128)S(1)} %get-tuple-element.51.left, f32[112,256]{1,0:T(8,128)S(1)} %get-tuple-element.52.right, ...), custom_call_target="tpu_custom_call" | custom-call | tf_op jit(solution)/shard_map/pallas_call | solution.py:19
  (3 shorter events, 0.0 us)
Async XLA Ops:
  1.3 24.2 %collective-permute-start = (f32[112,256]{1,0:T(8,128)S(1)}, f32[112,256]{1,0:T(8,128)S(1)}, u32[]{:S(2)}, u32[]{:S(2)}) collective-permute-start(f32[112,256]{1,0:T(8,128)S(1)} %get-tuple-element.41), channel_id=1, source_target_pairs={{128,256},{129,257},{130,258},{131,259},{132,260},{133,261},{134,2... | collective-permute-start | bytes 344072 | tf_op jit(solution)/shard_map/ppermute | solution.py:548
  5.0 19.1 %collective-permute-start.1 = (f32[40,256]{1,0:T(8,128)S(1)}, f32[40,256]{1,0:T(8,128)S(1)}, u32[]{:S(2)}, u32[]{:S(2)}) collective-permute-start(f32[40,256]{1,0:T(8,128)S(1)} %get-tuple-element.42.even), channel_id=1, source_target_pairs={{0,1},{2,3},{4,5},{6,7},{8,9},{10,11},{12,13},{14,15},{16,17},{18,... | collective-permute-start | bytes 122888 | tf_op jit(solution)/shard_map/ppermute | solution.py:548
  8.5 16.9 %collective-permute-start.2 = (f32[40,256]{1,0:T(8,128)S(1)}, f32[40,256]{1,0:T(8,128)S(1)}, u32[]{:S(2)}, u32[]{:S(2)}) collective-permute-start(f32[40,256]{1,0:T(8,128)S(1)} %get-tuple-element.43), channel_id=1, source_target_pairs={{1,2},{3,4},{5,6},{7,8},{9,10},{11,12},{13,14},{15,16},{17,18},{19... | collective-permute-start | bytes 122888 | tf_op jit(solution)/shard_map/ppermute | solution.py:548
  21.2 4.3 %collective-permute-start.3 = (f32[112,256]{1,0:T(8,128)S(1)}, f32[112,256]{1,0:T(8,128)S(1)}, u32[]{:S(2)}, u32[]{:S(2)}) collective-permute-start(f32[112,256]{1,0:T(8,128)S(1)} %get-tuple-element.45), channel_id=1, source_target_pairs={{0,128},{1,129},{2,130},{3,131},{4,132},{5,133},{6,134},{7,135},{8... | collective-permute-start | bytes 344072 | tf_op jit(solution)/shard_map/ppermute | solution.py:548
  24.1 1.4 %collective-permute-start.4 = (f32[40,256]{1,0:T(8,128)S(1)}, f32[40,256]{1,0:T(8,128)S(1)}, u32[]{:S(2)}, u32[]{:S(2)}) collective-permute-start(f32[40,256]{1,0:T(8,128)S(1)} %get-tuple-element.49), channel_id=1, source_target_pairs={{30,31},{62,63},{94,95},{126,127},{158,159},{190,191},{222,223},{2... | collective-permute-start | bytes 122888 | tf_op jit(solution)/shard_map/ppermute | solution.py:548
  24.8 0.7 %collective-permute-start.5 = (f32[112,256]{1,0:T(8,128)S(1)}, f32[112,256]{1,0:T(8,128)S(1)}, u32[]{:S(2)}, u32[]{:S(2)}) collective-permute-start(f32[112,256]{1,0:T(8,128)S(1)} %get-tuple-element.50), channel_id=1, source_target_pairs={{29,30},{61,62},{93,94},{125,126},{157,158},{189,190},{221,222},{2... | collective-permute-start | bytes 344072 | tf_op jit(solution)/shard_map/ppermute | solution.py:548
  26.0 5.6 %collective-permute-start.6 = (f32[64,256]{1,0:T(8,128)S(1)}, f32[64,256]{1,0:T(8,128)S(1)}, u32[]{:S(2)}, u32[]{:S(2)}) collective-permute-start(f32[64,256]{1,0:T(8,128)S(1)} %get-tuple-element.59), channel_id=1, source_target_pairs={{128,256},{129,257},{130,258},{131,259},{132,260},{133,261},{134,2... | collective-permute-start | bytes 196616 | tf_op jit(solution)/shard_map/ppermute | solution.py:548
  32.1 8.9 %collective-permute-start.7 = (f32[72,128]{1,0:T(8,128)S(1)}, f32[72,128]{1,0:T(8,128)S(1)}, u32[]{:S(2)}, u32[]{:S(2)}) collective-permute-start(f32[72,128]{1,0:T(8,128)S(1)} %get-tuple-element.66), channel_id=1, source_target_pairs={{0,1},{2,3},{4,5},{6,7},{8,9},{10,11},{12,13},{14,15},{16,17},{18,... | collective-permute-start | bytes 110600 | tf_op jit(solution)/shard_map/ppermute | solution.py:548
  34.0 8.3 %collective-permute-start.8 = (f32[72,128]{1,0:T(8,128)S(1)}, f32[72,128]{1,0:T(8,128)S(1)}, u32[]{:S(2)}, u32[]{:S(2)}) collective-permute-start(f32[72,128]{1,0:T(8,128)S(1)} %get-tuple-element.67), channel_id=1, source_target_pairs={{1,2},{3,4},{5,6},{7,8},{9,10},{11,12},{13,14},{15,16},{17,18},{19... | collective-permute-start | bytes 110600 | tf_op jit(solution)/shard_map/ppermute | solution.py:548
  40.3 2.0 %collective-permute-start.9 = (f32[72,128]{1,0:T(8,128)S(1)}, f32[72,128]{1,0:T(8,128)S(1)}, u32[]{:S(2)}, u32[]{:S(2)}) collective-permute-start(f32[72,128]{1,0:T(8,128)S(1)} %get-tuple-element.68), channel_id=1, source_target_pairs={{30,31},{62,63},{94,95},{126,127},{158,159},{190,191},{222,223},{2... | collective-permute-start | bytes 110600 | tf_op jit(solution)/shard_map/ppermute | solution.py:548

commit v10 on v8

--- a/solution.py
+++ b/solution.py
@@ -105,7 +105,7 @@
 
 
 def load_kernel(
-    g_hbm, b_hbm, n_hbm, cross, chip, even, odd, f1z, g, b, w, d, n, both, sems
+    g_hbm, b_hbm, n_hbm, cross, cross2, chip, even, odd, f1z, g, b, w, d, n, both, sems
 ):
     copies = [
         pltpu.make_async_copy(src, dst, sems.at[k])
@@ -147,6 +147,7 @@
     p = side_of_dev()
     even[...] = both[1 - p]
     odd[...] = both[p]
+    cross2[...] = cross[...]
 
 
 class Wide:
@@ -176,11 +177,10 @@
     both[p] = odd
 
 
-def again_kernel(cross, even, odd, chip, met, cross2, even2, odd2, chip2):
+def again_kernel(even, odd, chip, met, even2, odd2, chip2):
+    chip2[...] = chip[...]
     even2[...] = even[...]
-    cross2[...] = cross[...]
     odd2[...] = odd[...]
-    chip2[...] = chip[...]
 
 
 def gather_kernel(cross, even, odd, left, both):
@@ -531,17 +531,17 @@
         )
 
 
-def swap(v, links):
+def send(v, links):
     n = lax.axis_size("dev")
     return lax.ppermute(v, ("group", "dev"), [(i * n + j, k * n + l) for (i, j), (k, l) in links])
 
 
-def both_ways(pairs):
-    return pairs + one_way_back(pairs)
-
-
-def one_way_back(pairs):
-    return [(j, i) for i, j in pairs]
+def back(links):
+    return [(j, i) for i, j in links]
+
+
+def swap(v, pairs):
+    return send(v, pairs + back(pairs))
 
 
 def share_chip(v):
@@ -563,37 +563,35 @@
     return d % RUN == 0
 
 
+def in_middle(d):
+    return not (is_start(d) or before_end(d))
+
+
 def is_end(d):
     return d % RUN == RUN - 1
 
 
-def near_end(d):
-    return is_end(d) or before_end(d)
-
-
 def before_end(d):
     return d % RUN == RUN - 2
 
 
 def body(g, b, n):
     block = (BX, BY, NZ)
-    cross, chip, even, odd, f1z, g, b, w, d = call(
+    cross, cross2, chip, even, odd, f1z, g, b, w, d = call(
         load_kernel,
-        [(X_ROWS, NZ)] * 2 + [(Y_ROWS, NZ)] * 2 + [(BX * BY, NZ)] + [block] * 4,
+        [(X_ROWS, NZ)] * 3 + [(Y_ROWS, NZ)] * 2 + [(BX * BY, NZ)] + [block] * 4,
         g, b, n,
         hbm=3,
         vmem=None,
         scratch=[pltpu.VMEM(block, jnp.int32), (2, Y_ROWS, NZ), pltpu.SemaphoreType.DMA((3,))],
     )
-    cross1 = swap(cross, both_ways(cross_pairs(lambda d: not near_end(d))))
-    even1 = swap(even, both_ways(dev_pairs(0, lambda d: not before_end(d))))
-    odd1 = swap(odd, both_ways(dev_pairs(1, lambda d: not before_end(d + 1))))
-    cross2, even2, odd2, chip = call(
-        again_kernel, [(X_ROWS, NZ), (Y_ROWS, NZ), (Y_ROWS, NZ), (X_ROWS, NZ)], cross, even, odd, chip, even1
-    )
-    even2 = swap(even2, both_ways(dev_pairs(0, before_end)))
-    odd2 = swap(odd2, both_ways(dev_pairs(1, lambda d: before_end(d + 1))))
-    cross2 = swap(cross2, both_ways(cross_pairs(near_end)))
+    cross1 = swap(cross, cross_pairs(lambda d: not is_end(d)))
+    even1 = swap(even, dev_pairs(0, lambda d: not before_end(d)))
+    odd1 = swap(odd, dev_pairs(1, lambda d: not before_end(d + 1)))
+    cross2 = swap(cross2, cross_pairs(is_end))
+    even2, odd2, chip = call(again_kernel, [(Y_ROWS, NZ)] * 2 + [(X_ROWS, NZ)], even, odd, chip, even1)
+    even2 = swap(even2, dev_pairs(0, before_end))
+    odd2 = swap(odd2, dev_pairs(1, lambda d: before_end(d + 1)))
     chip = share_chip(chip)
     left, both = call(
         gather_kernel,
@@ -607,7 +605,7 @@
         g, b, w, d, left, cross2, chip, f1z, both, even2, odd2,
         scratch=[(16, NZ), (2, 16, NZ), (4, CX * BY, CZ)],
     )
-    cleft = swap(cross, both_ways(cross_pairs(lambda d: True)))
+    cleft = swap(cross, cross_pairs(lambda d: True))
     cchip = share_chip(near)
     even, even2, odd, f2, f2low, f2high, c1x, c2z = call(
         pack_c_kernel,
@@ -615,10 +613,10 @@
         g, b, w, left, chip, both, f2, f2low, f2high, c1, wc, cleft, cchip,
         scratch=[(13, 8, NZ), (5, 8, NZ), (8, CZ), (2, Z_ROWS, CZ)],
     )
-    first = dev_pairs(0, is_start)
-    even1 = swap(even, both_ways(dev_pairs(0, lambda d: not (is_start(d) or before_end(d)))) + one_way_back(first))
-    odd = swap(odd, both_ways(dev_pairs(1, lambda d: True)))
-    even2 = swap(even2, both_ways(dev_pairs(0, before_end)) + first)
+    inner, start, end = (dev_pairs(0, keep) for keep in (in_middle, is_start, before_end))
+    even1 = send(even, inner + back(inner) + back(start))
+    odd = swap(odd, dev_pairs(1, lambda d: True))
+    even2 = send(even2, end + back(end) + start)
     (out,) = call(
         last_kernel,
         [block],

time: 44.1 us -> 43.5 us (0.986)
  waiting for transfers between devices: 6.19 us -> 5.57 us
    ppermute x10, waiting for transfers between devices: 6.19 us -> 5.57 us  [send(): lax.ppermute(v, ('group', 'dev'), [(i * n + j, k * n + l) for (i, j), (k,...]
where the time goes in v10:
time: 43.5 us; the launch traced here: 43.2 us
  starting transfers between devices  30.2 us (69%)
  waiting for transfers between devices  5.57 us (13%)
  blocking collectives  3.87 us (9%)
  Pallas kernels  3.39 us (8%)
    ppermute x10, starting transfers between devices, send(): lax.ppermute(v, ('group', 'dev'), [(i * n + j, k * n + l) for (i, j), (k,...  30.2 us
    ppermute x10, waiting for transfers between devices, send(): lax.ppermute(v, ('group', 'dev'), [(i * n + j, k * n + l) for (i, j), (k,...  5.57 us
    all_gather x2, blocking collectives, share_chip(): return lax.all_gather(v, 'group', axis_index_groups=groups)  3.87 us
    pallas_call x6, Pallas kernels, call(): pl.pallas_call(kernel, out_shape=[make(s, F32) for s in outs], in_specs=[...  3.39 us
  transfers between devices with their start and end apart: 10, of which 3 were waited for; matrix products, arithmetic and copies ran while one was open for 0% of the time, Pallas kernels for 0%

profile of v10, /device:TPU:62, one launch (start us, length us, event | category | flops | bytes accessed | tf_op | source)
XLA Modules:
  0.0 43.2 jit_solution(4177233783802912366)
XLA Ops:
  0.0 1.3 %shard_map.37 = (f32[112,256]{1,0:T(8,128)S(1)}, f32[112,256]{1,0:T(8,128)S(1)}, f32[112,256]{1,0:T(8,128)S(1)}, f32[40,256]{1,0:T(8,128)S(1)}, f32[40,256]{1,0:...) custom-call(f32[8,16,256]{2,1,0:T(8,128)} %g_hbm.1, ...), custom_call_target="tpu_custom_call" | custom-call | tf_op jit(solution)/shard_map/pallas_call | solution.py:19
  1.3 2.2 %collective-permute-start = (f32[112,256]{1,0:T(8,128)S(1)}, f32[112,256]{1,0:T(8,128)S(1)}, u32[]{:S(2)}, u32[]{:S(2)}) collective-permute-start(f32[112,256]{1,0:T(8,128)S(1)} %get-tuple-element.41), channel_id=1, source_target_pairs={{128,256},{129,257},{130,258},{131,259},{132,260},{133,261},{134,2... | collective-permute-start | bytes 344072 | tf_op jit(solution)/shard_map/ppermute | solution.py:536
  3.4 2.0 %collective-permute-start.1 = (f32[40,256]{1,0:T(8,128)S(1)}, f32[40,256]{1,0:T(8,128)S(1)}, u32[]{:S(2)}, u32[]{:S(2)}) collective-permute-start(f32[40,256]{1,0:T(8,128)S(1)} %get-tuple-element.42.even), channel_id=1, source_target_pairs={{0,1},{2,3},{4,5},{6,7},{8,9},{10,11},{12,13},{14,15},{16,17},{18,... | collective-permute-start | bytes 122888 | tf_op jit(solution)/shard_map/ppermute | solution.py:536
  5.5 5.6 %collective-permute-start.2 = (f32[40,256]{1,0:T(8,128)S(1)}, f32[40,256]{1,0:T(8,128)S(1)}, u32[]{:S(2)}, u32[]{:S(2)}) collective-permute-start(f32[40,256]{1,0:T(8,128)S(1)} %get-tuple-element.43.odd), channel_id=1, source_target_pairs={{1,2},{3,4},{5,6},{7,8},{9,10},{11,12},{13,14},{15,16},{17,18},{19... | collective-permute-start | bytes 122888 | tf_op jit(solution)/shard_map/ppermute | solution.py:536
  11.1 0.7 %collective-permute-start.3 = (f32[112,256]{1,0:T(8,128)S(1)}, f32[112,256]{1,0:T(8,128)S(1)}, u32[]{:S(2)}, u32[]{:S(2)}) collective-permute-start(f32[112,256]{1,0:T(8,128)S(1)} %get-tuple-element.45), channel_id=1, source_target_pairs={{159,287},{191,319},{223,351},{255,383},{415,543},{447,575},{479,6... | collective-permute-start | bytes 344072 | tf_op jit(solution)/shard_map/ppermute | solution.py:536
  11.8 0.0 collective-permute-done.1.even.met
  11.8 0.7 %collective-permute-start.4 = (f32[40,256]{1,0:T(8,128)S(1)}, f32[40,256]{1,0:T(8,128)S(1)}, u32[]{:S(2)}, u32[]{:S(2)}) collective-permute-start(f32[40,256]{1,0:T(8,128)S(1)} %get-tuple-element.50), channel_id=1, source_target_pairs={{30,31},{62,63},{94,95},{126,127},{158,159},{190,191},{222,223},{2... | collective-permute-start | bytes 122888 | tf_op jit(solution)/shard_map/ppermute | solution.py:536
  12.5 0.7 %collective-permute-start.5 = (f32[40,256]{1,0:T(8,128)S(1)}, f32[40,256]{1,0:T(8,128)S(1)}, u32[]{:S(2)}, u32[]{:S(2)}) collective-permute-start(f32[40,256]{1,0:T(8,128)S(1)} %get-tuple-element.51), channel_id=1, source_target_pairs={{29,30},{61,62},{93,94},{125,126},{157,158},{189,190},{221,222},{2... | collective-permute-start | bytes 122888 | tf_op jit(solution)/shard_map/ppermute | solution.py:536
  13.2 2.0 %all-gather = f32[224,256]{1,0:T(8,128)S(1)} all-gather(f32[112,256]{1,0:T(8,128)S(1)} %get-tuple-element.47), channel_id=2, replica_groups={{0,128},{256,384},{512,640},{768,896},{1,129},{257,385},{513,641},{769,..., dimensions={0}, use_global_device_ids=true | all-gather | bytes 344064 | tf_op jit(solution)/shard_map/all_gather | solution.py:549
  15.1 0.0 collective-permute-done.2.odd
  15.1 0.0 collective-permute-done.cross
  15.2 0.0 collective-permute-done.4.even2
  15.2 0.0 collective-permute-done.3.cross2
  15.2 0.5 %shard_map.40 = (f32[160,256]{1,0:T(8,128)S(1)}, f32[8,256]{1,0:T(8,128)S(1)}, f32[8,256]{1,0:T(8,128)S(1)}, f32[32,128]{1,0:T(8,128)S(1)}, f32[32,128]{1,0:T(8,...) custom-call(f32[8,16,256]{2,1,0:T(8,128)S(1)} %get-tuple-element.37., ...), custom_call_target="tpu_custom_call" | custom-call | tf_op jit(solution)/shard_map/pallas_call | solution.py:19
  15.7 2.8 %collective-permute-start.6 = (f32[64,256]{1,0:T(8,128)S(1)}, f32[64,256]{1,0:T(8,128)S(1)}, u32[]{:S(2)}, u32[]{:S(2)}) collective-permute-start(f32[64,256]{1,0:T(8,128)S(1)} %get-tuple-element.59), channel_id=1, source_target_pairs={{128,256},{129,257},{130,258},{131,259},{132,260},{133,261},{134,2... | collective-permute-start | bytes 196616 | tf_op jit(solution)/shard_map/ppermute | solution.py:536
  18.5 1.9 %all-gather.1 = f32[128,256]{1,0:T(8,128)S(1)} all-gather(f32[64,256]{1,0:T(8,128)S(1)} %get-tuple-element.60), channel_id=3, replica_groups={{0,128},{256,384},{512,640},{768,896},{1,129},{257,385},{513,641},{769,..., dimensions={0}, use_global_device_ids=true | all-gather | bytes 196608 | tf_op jit(solution)/shard_map/all_gather | solution.py:549
  20.4 0.9 %collective-permute-done.6.cleft = f32[64,256]{1,0:T(8,128)S(1)} collective-permute-done((f32[64,256]{1,0:T(8,128)S(1)}, f32[64,256]{1,0:T(8,128)S(1)}, u32[]{:S(2)}, u32[]{:S(2)}) %collective-permute-start.6) | collective-permute-done | bytes 65568 | tf_op jit(solution)/shard_map/ppermute | solution.py:536
  21.3 0.4 shard_map.41
  21.7 12.4 %collective-permute-start.7 = (f32[72,128]{1,0:T(8,128)S(1)}, f32[72,128]{1,0:T(8,128)S(1)}, u32[]{:S(2)}, u32[]{:S(2)}) collective-permute-start(f32[72,128]{1,0:T(8,128)S(1)} %get-tuple-element.66), channel_id=1, source_target_pairs={{2,3},{4,5},{6,7},{8,9},{10,11},{12,13},{14,15},{16,17},{18,19},{2... | collective-permute-start | bytes 110600 | tf_op jit(solution)/shard_map/ppermute | solution.py:536
  34.1 1.9 %collective-permute-start.8 = (f32[72,128]{1,0:T(8,128)S(1)}, f32[72,128]{1,0:T(8,128)S(1)}, u32[]{:S(2)}, u32[]{:S(2)}) collective-permute-start(f32[72,128]{1,0:T(8,128)S(1)} %get-tuple-element.67), channel_id=1, source_target_pairs={{1,2},{3,4},{5,6},{7,8},{9,10},{11,12},{13,14},{15,16},{17,18},{19... | collective-permute-start | bytes 110600 | tf_op jit(solution)/shard_map/ppermute | solution.py:536
  36.0 1.3 %collective-permute-start.9 = (f32[72,128]{1,0:T(8,128)S(1)}, f32[72,128]{1,0:T(8,128)S(1)}, u32[]{:S(2)}, u32[]{:S(2)}) collective-permute-start(f32[72,128]{1,0:T(8,128)S(1)} %get-tuple-element.68), channel_id=1, source_target_pairs={{30,31},{62,63},{94,95},{126,127},{158,159},{190,191},{222,223},{2... | collective-permute-start | bytes 110600 | tf_op jit(solution)/shard_map/ppermute | solution.py:536
  37.3 2.6 %collective-permute-done.8.odd = f32[72,128]{1,0:T(8,128)S(1)} collective-permute-done((f32[72,128]{1,0:T(8,128)S(1)}, f32[72,128]{1,0:T(8,128)S(1)}, u32[]{:S(2)}, u32[]{:S(2)}) %collective-permute-start.8) | collective-permute-done | bytes 36896 | tf_op jit(solution)/shard_map/ppermute | solution.py:536
  39.9 2.1 %collective-permute-done.9.even2 = f32[72,128]{1,0:T(8,128)S(1)} collective-permute-done((f32[72,128]{1,0:T(8,128)S(1)}, f32[72,128]{1,0:T(8,128)S(1)}, u32[]{:S(2)}, u32[]{:S(2)}) %collective-permute-start.9) | collective-permute-done | bytes 36896 | tf_op jit(solution)/shard_map/ppermute | solution.py:536
  42.0 1.2 %shard_map.42 = f32[8,16,256]{2,1,0:T(8,128)} custom-call(f32[8,16,256]{2,1,0:T(8,128)S(1)} %get-tuple-element.37.g, f32[8,16,256]{2,1,0:T(8,128)S(1)} %get-tuple-element.38.b, f32[8,16,256]{2,1,0:T(8,128)S(1)} %get-tuple-element.39.w, f32[112,256]{1,0:T(8,128)S(1)} %get-tuple-element.52.left, f32[2,112,256]{2,1,0:T(8,128)S(1)} %bitcast.4, ...), custom_call_target="tpu_custom_call" | custom-call | tf_op jit(solution)/shard_map/pallas_call | solution.py:19
  (4 shorter events, 0.0 us)
Async XLA Ops:
  1.3 13.9 %collective-permute-start = (f32[112,256]{1,0:T(8,128)S(1)}, f32[112,256]{1,0:T(8,128)S(1)}, u32[]{:S(2)}, u32[]{:S(2)}) collective-permute-start(f32[112,256]{1,0:T(8,128)S(1)} %get-tuple-element.41), channel_id=1, source_target_pairs={{128,256},{129,257},{130,258},{131,259},{132,260},{133,261},{134,2... | collective-permute-start | bytes 344072 | tf_op jit(solution)/shard_map/ppermute | solution.py:536
  3.4 8.3 %collective-permute-start.1 = (f32[40,256]{1,0:T(8,128)S(1)}, f32[40,256]{1,0:T(8,128)S(1)}, u32[]{:S(2)}, u32[]{:S(2)}) collective-permute-start(f32[40,256]{1,0:T(8,128)S(1)} %get-tuple-element.42.even), channel_id=1, source_target_pairs={{0,1},{2,3},{4,5},{6,7},{8,9},{10,11},{12,13},{14,15},{16,17},{18,... | collective-permute-start | bytes 122888 | tf_op jit(solution)/shard_map/ppermute | solution.py:536
  5.5 9.7 %collective-permute-start.2 = (f32[40,256]{1,0:T(8,128)S(1)}, f32[40,256]{1,0:T(8,128)S(1)}, u32[]{:S(2)}, u32[]{:S(2)}) collective-permute-start(f32[40,256]{1,0:T(8,128)S(1)} %get-tuple-element.43.odd), channel_id=1, source_target_pairs={{1,2},{3,4},{5,6},{7,8},{9,10},{11,12},{13,14},{15,16},{17,18},{19... | collective-permute-start | bytes 122888 | tf_op jit(solution)/shard_map/ppermute | solution.py:536
  11.1 4.1 %collective-permute-start.3 = (f32[112,256]{1,0:T(8,128)S(1)}, f32[112,256]{1,0:T(8,128)S(1)}, u32[]{:S(2)}, u32[]{:S(2)}) collective-permute-start(f32[112,256]{1,0:T(8,128)S(1)} %get-tuple-element.45), channel_id=1, source_target_pairs={{159,287},{191,319},{223,351},{255,383},{415,543},{447,575},{479,6... | collective-permute-start | bytes 344072 | tf_op jit(solution)/shard_map/ppermute | solution.py:536
  11.8 3.3 %collective-permute-start.4 = (f32[40,256]{1,0:T(8,128)S(1)}, f32[40,256]{1,0:T(8,128)S(1)}, u32[]{:S(2)}, u32[]{:S(2)}) collective-permute-start(f32[40,256]{1,0:T(8,128)S(1)} %get-tuple-element.50), channel_id=1, source_target_pairs={{30,31},{62,63},{94,95},{126,127},{158,159},{190,191},{222,223},{2... | collective-permute-start | bytes 122888 | tf_op jit(solution)/shard_map/ppermute | solution.py:536
  12.5 2.7 %collective-permute-start.5 = (f32[40,256]{1,0:T(8,128)S(1)}, f32[40,256]{1,0:T(8,128)S(1)}, u32[]{:S(2)}, u32[]{:S(2)}) collective-permute-start(f32[40,256]{1,0:T(8,128)S(1)} %get-tuple-element.51), channel_id=1, source_target_pairs={{29,30},{61,62},{93,94},{125,126},{157,158},{189,190},{221,222},{2... | collective-permute-start | bytes 122888 | tf_op jit(solution)/shard_map/ppermute | solution.py:536
  15.7 5.6 %collective-permute-start.6 = (f32[64,256]{1,0:T(8,128)S(1)}, f32[64,256]{1,0:T(8,128)S(1)}, u32[]{:S(2)}, u32[]{:S(2)}) collective-permute-start(f32[64,256]{1,0:T(8,128)S(1)} %get-tuple-element.59), channel_id=1, source_target_pairs={{128,256},{129,257},{130,258},{131,259},{132,260},{133,261},{134,2... | collective-permute-start | bytes 196616 | tf_op jit(solution)/shard_map/ppermute | solution.py:536
  21.7 15.6 %collective-permute-start.7 = (f32[72,128]{1,0:T(8,128)S(1)}, f32[72,128]{1,0:T(8,128)S(1)}, u32[]{:S(2)}, u32[]{:S(2)}) collective-permute-start(f32[72,128]{1,0:T(8,128)S(1)} %get-tuple-element.66), channel_id=1, source_target_pairs={{2,3},{4,5},{6,7},{8,9},{10,11},{12,13},{14,15},{16,17},{18,19},{2... | collective-permute-start | bytes 110600 | tf_op jit(solution)/shard_map/ppermute | solution.py:536
  34.1 5.9 %collective-permute-start.8 = (f32[72,128]{1,0:T(8,128)S(1)}, f32[72,128]{1,0:T(8,128)S(1)}, u32[]{:S(2)}, u32[]{:S(2)}) collective-permute-start(f32[72,128]{1,0:T(8,128)S(1)} %get-tuple-element.67), channel_id=1, source_target_pairs={{1,2},{3,4},{5,6},{7,8},{9,10},{11,12},{13,14},{15,16},{17,18},{19... | collective-permute-start | bytes 110600 | tf_op jit(solution)/shard_map/ppermute | solution.py:536
  36.0 6.0 %collective-permute-start.9 = (f32[72,128]{1,0:T(8,128)S(1)}, f32[72,128]{1,0:T(8,128)S(1)}, u32[]{:S(2)}, u32[]{:S(2)}) collective-permute-start(f32[72,128]{1,0:T(8,128)S(1)} %get-tuple-element.68), channel_id=1, source_target_pairs={{30,31},{62,63},{94,95},{126,127},{158,159},{190,191},{222,223},{2... | collective-permute-start | bytes 110600 | tf_op jit(solution)/shard_map/ppermute | solution.py:536

commit v11 on v10

--- a/solution.py
+++ b/solution.py
@@ -177,9 +177,12 @@
     both[p] = odd
 
 
-def again_kernel(even, odd, chip, met, even2, odd2, chip2):
+def again_kernel(even, chip, met, even2, chip2):
+    even2[...] = even[...]
     chip2[...] = chip[...]
-    even2[...] = even[...]
+
+
+def later_kernel(odd, met, odd2):
     odd2[...] = odd[...]
 
 
@@ -589,10 +592,11 @@
     even1 = swap(even, dev_pairs(0, lambda d: not before_end(d)))
     odd1 = swap(odd, dev_pairs(1, lambda d: not before_end(d + 1)))
     cross2 = swap(cross2, cross_pairs(is_end))
-    even2, odd2, chip = call(again_kernel, [(Y_ROWS, NZ)] * 2 + [(X_ROWS, NZ)], even, odd, chip, even1)
+    even2, chip = call(again_kernel, [(Y_ROWS, NZ), (X_ROWS, NZ)], even, chip, even1)
     even2 = swap(even2, dev_pairs(0, before_end))
+    chip = share_chip(chip)
+    (odd2,) = call(later_kernel, [(Y_ROWS, NZ)], odd, chip)
     odd2 = swap(odd2, dev_pairs(1, lambda d: before_end(d + 1)))
-    chip = share_chip(chip)
     left, both = call(
         gather_kernel,
         [(X_ROWS, NZ), (2, Y_ROWS, NZ)],

time: 43.5 us -> 43.5 us (level)
    pallas_call x6 -> x7, Pallas kernels: 3.39 us -> 3.39 us  [call(): pl.pallas_call(kernel, out_shape=[make(s, F32) for s in outs], in_specs=[...]
where the time goes in v11:
time: 43.5 us; the launch traced here: 43.2 us
  starting transfers between devices  30.2 us (69%)
  waiting for transfers between devices  5.56 us (13%)
  blocking collectives  3.87 us (9%)
  Pallas kernels  3.39 us (8%)
    ppermute x10, starting transfers between devices, send(): lax.ppermute(v, ('group', 'dev'), [(i * n + j, k * n + l) for (i, j), (k,...  30.2 us
    ppermute x10, waiting for transfers between devices, send(): lax.ppermute(v, ('group', 'dev'), [(i * n + j, k * n + l) for (i, j), (k,...  5.56 us
    all_gather x2, blocking collectives, share_chip(): return lax.all_gather(v, 'group', axis_index_groups=groups)  3.87 us
    pallas_call x7, Pallas kernels, call(): pl.pallas_call(kernel, out_shape=[make(s, F32) for s in outs], in_specs=[...  3.39 us
  transfers between devices with their start and end apart: 10, of which 3 were waited for; matrix products, arithmetic and copies ran while one was open for 0% of the time, Pallas kernels for 0%

profile of v11, /device:TPU:62, one launch (start us, length us, event | category | flops | bytes accessed | tf_op | source)
XLA Modules:
  0.0 43.2 jit_solution(8732656317935910582)
XLA Ops:
  0.0 1.3 %shard_map.37 = (f32[112,256]{1,0:T(8,128)S(1)}, f32[112,256]{1,0:T(8,128)S(1)}, f32[112,256]{1,0:T(8,128)S(1)}, f32[40,256]{1,0:T(8,128)S(1)}, f32[40,256]{1,0:...) custom-call(f32[8,16,256]{2,1,0:T(8,128)} %g_hbm.1, ...), custom_call_target="tpu_custom_call" | custom-call | tf_op jit(solution)/shard_map/pallas_call | solution.py:19
  1.3 2.2 %collective-permute-start = (f32[112,256]{1,0:T(8,128)S(1)}, f32[112,256]{1,0:T(8,128)S(1)}, u32[]{:S(2)}, u32[]{:S(2)}) collective-permute-start(f32[112,256]{1,0:T(8,128)S(1)} %get-tuple-element.40), channel_id=1, source_target_pairs={{128,256},{129,257},{130,258},{131,259},{132,260},{133,261},{134,2... | collective-permute-start | bytes 344072 | tf_op jit(solution)/shard_map/ppermute | solution.py:539
  3.4 2.0 %collective-permute-start.1 = (f32[40,256]{1,0:T(8,128)S(1)}, f32[40,256]{1,0:T(8,128)S(1)}, u32[]{:S(2)}, u32[]{:S(2)}) collective-permute-start(f32[40,256]{1,0:T(8,128)S(1)} %get-tuple-element.41.even), channel_id=1, source_target_pairs={{0,1},{2,3},{4,5},{6,7},{8,9},{10,11},{12,13},{14,15},{16,17},{18,... | collective-permute-start | bytes 122888 | tf_op jit(solution)/shard_map/ppermute | solution.py:539
  5.5 5.6 %collective-permute-start.2 = (f32[40,256]{1,0:T(8,128)S(1)}, f32[40,256]{1,0:T(8,128)S(1)}, u32[]{:S(2)}, u32[]{:S(2)}) collective-permute-start(f32[40,256]{1,0:T(8,128)S(1)} %get-tuple-element.42.odd), channel_id=1, source_target_pairs={{1,2},{3,4},{5,6},{7,8},{9,10},{11,12},{13,14},{15,16},{17,18},{19... | collective-permute-start | bytes 122888 | tf_op jit(solution)/shard_map/ppermute | solution.py:539
  11.1 0.7 %collective-permute-start.3 = (f32[112,256]{1,0:T(8,128)S(1)}, f32[112,256]{1,0:T(8,128)S(1)}, u32[]{:S(2)}, u32[]{:S(2)}) collective-permute-start(f32[112,256]{1,0:T(8,128)S(1)} %get-tuple-element.44), channel_id=1, source_target_pairs={{159,287},{191,319},{223,351},{255,383},{415,543},{447,575},{479,6... | collective-permute-start | bytes 344072 | tf_op jit(solution)/shard_map/ppermute | solution.py:539
  11.8 0.7 %collective-permute-start.4 = (f32[40,256]{1,0:T(8,128)S(1)}, f32[40,256]{1,0:T(8,128)S(1)}, u32[]{:S(2)}, u32[]{:S(2)}) collective-permute-start(f32[40,256]{1,0:T(8,128)S(1)} %get-tuple-element.49), channel_id=1, source_target_pairs={{30,31},{62,63},{94,95},{126,127},{158,159},{190,191},{222,223},{2... | collective-permute-start | bytes 122888 | tf_op jit(solution)/shard_map/ppermute | solution.py:539
  12.5 2.0 %all-gather = f32[224,256]{1,0:T(8,128)S(1)} all-gather(f32[112,256]{1,0:T(8,128)S(1)} %get-tuple-element.46), channel_id=2, replica_groups={{0,128},{256,384},{512,640},{768,896},{1,129},{257,385},{513,641},{769,..., dimensions={0}, use_global_device_ids=true | all-gather | bytes 344064 | tf_op jit(solution)/shard_map/all_gather | solution.py:552
  14.5 0.7 %collective-permute-start.5 = (f32[40,256]{1,0:T(8,128)S(1)}, f32[40,256]{1,0:T(8,128)S(1)}, u32[]{:S(2)}, u32[]{:S(2)}) collective-permute-start(f32[40,256]{1,0:T(8,128)S(1)} %shard_map.40), channel_id=1, source_target_pairs={{29,30},{61,62},{93,94},{125,126},{157,158},{189,190},{221,222},{2... | collective-permute-start | bytes 122888 | tf_op jit(solution)/shard_map/ppermute | solution.py:539
  15.1 0.0 collective-permute-done.2.odd
  15.1 0.0 collective-permute-done.cross
  15.2 0.0 collective-permute-done.5.odd2
  15.2 0.0 collective-permute-done.3.cross2
  15.2 0.5 %shard_map.41 = (f32[160,256]{1,0:T(8,128)S(1)}, f32[8,256]{1,0:T(8,128)S(1)}, f32[8,256]{1,0:T(8,128)S(1)}, f32[32,128]{1,0:T(8,128)S(1)}, f32[32,128]{1,0:T(8,...) custom-call(f32[8,16,256]{2,1,0:T(8,128)S(1)} %get-tuple-element.36., ...), custom_call_target="tpu_custom_call" | custom-call | tf_op jit(solution)/shard_map/pallas_call | solution.py:19
  15.7 2.8 %collective-permute-start.6 = (f32[64,256]{1,0:T(8,128)S(1)}, f32[64,256]{1,0:T(8,128)S(1)}, u32[]{:S(2)}, u32[]{:S(2)}) collective-permute-start(f32[64,256]{1,0:T(8,128)S(1)} %get-tuple-element.57), channel_id=1, source_target_pairs={{128,256},{129,257},{130,258},{131,259},{132,260},{133,261},{134,2... | collective-permute-start | bytes 196616 | tf_op jit(solution)/shard_map/ppermute | solution.py:539
  18.5 1.9 %all-gather.1 = f32[128,256]{1,0:T(8,128)S(1)} all-gather(f32[64,256]{1,0:T(8,128)S(1)} %get-tuple-element.58), channel_id=3, replica_groups={{0,128},{256,384},{512,640},{768,896},{1,129},{257,385},{513,641},{769,..., dimensions={0}, use_global_device_ids=true | all-gather | bytes 196608 | tf_op jit(solution)/shard_map/all_gather | solution.py:552
  20.4 0.9 %collective-permute-done.6.cleft = f32[64,256]{1,0:T(8,128)S(1)} collective-permute-done((f32[64,256]{1,0:T(8,128)S(1)}, f32[64,256]{1,0:T(8,128)S(1)}, u32[]{:S(2)}, u32[]{:S(2)}) %collective-permute-start.6) | collective-permute-done | bytes 65568 | tf_op jit(solution)/shard_map/ppermute | solution.py:539
  21.3 0.4 shard_map.42
  21.7 12.4 %collective-permute-start.7 = (f32[72,128]{1,0:T(8,128)S(1)}, f32[72,128]{1,0:T(8,128)S(1)}, u32[]{:S(2)}, u32[]{:S(2)}) collective-permute-start(f32[72,128]{1,0:T(8,128)S(1)} %get-tuple-element.64), channel_id=1, source_target_pairs={{2,3},{4,5},{6,7},{8,9},{10,11},{12,13},{14,15},{16,17},{18,19},{2... | collective-permute-start | bytes 110600 | tf_op jit(solution)/shard_map/ppermute | solution.py:539
  34.1 1.9 %collective-permute-start.8 = (f32[72,128]{1,0:T(8,128)S(1)}, f32[72,128]{1,0:T(8,128)S(1)}, u32[]{:S(2)}, u32[]{:S(2)}) collective-permute-start(f32[72,128]{1,0:T(8,128)S(1)} %get-tuple-element.65), channel_id=1, source_target_pairs={{1,2},{3,4},{5,6},{7,8},{9,10},{11,12},{13,14},{15,16},{17,18},{19... | collective-permute-start | bytes 110600 | tf_op jit(solution)/shard_map/ppermute | solution.py:539
  36.0 1.3 %collective-permute-start.9 = (f32[72,128]{1,0:T(8,128)S(1)}, f32[72,128]{1,0:T(8,128)S(1)}, u32[]{:S(2)}, u32[]{:S(2)}) collective-permute-start(f32[72,128]{1,0:T(8,128)S(1)} %get-tuple-element.66), channel_id=1, source_target_pairs={{30,31},{62,63},{94,95},{126,127},{158,159},{190,191},{222,223},{2... | collective-permute-start | bytes 110600 | tf_op jit(solution)/shard_map/ppermute | solution.py:539
  37.3 0.0 collective-permute-done.7.even1
  37.3 2.6 %collective-permute-done.8.odd = f32[72,128]{1,0:T(8,128)S(1)} collective-permute-done((f32[72,128]{1,0:T(8,128)S(1)}, f32[72,128]{1,0:T(8,128)S(1)}, u32[]{:S(2)}, u32[]{:S(2)}) %collective-permute-start.8) | collective-permute-done | bytes 36896 | tf_op jit(solution)/shard_map/ppermute | solution.py:539
  40.0 2.1 %collective-permute-done.9.even2 = f32[72,128]{1,0:T(8,128)S(1)} collective-permute-done((f32[72,128]{1,0:T(8,128)S(1)}, f32[72,128]{1,0:T(8,128)S(1)}, u32[]{:S(2)}, u32[]{:S(2)}) %collective-permute-start.9) | collective-permute-done | bytes 36896 | tf_op jit(solution)/shard_map/ppermute | solution.py:539
  42.0 1.2 %shard_map.43 = f32[8,16,256]{2,1,0:T(8,128)} custom-call(f32[8,16,256]{2,1,0:T(8,128)S(1)} %get-tuple-element.36.g, f32[8,16,256]{2,1,0:T(8,128)S(1)} %get-tuple-element.37.b, f32[8,16,256]{2,1,0:T(8,128)S(1)} %get-tuple-element.38.w, f32[112,256]{1,0:T(8,128)S(1)} %get-tuple-element.50.left, f32[2,112,256]{2,1,0:T(8,128)S(1)} %bitcast.5, ...), custom_call_target="tpu_custom_call" | custom-call | tf_op jit(solution)/shard_map/pallas_call | solution.py:19
  (5 shorter events, 0.0 us)
Async XLA Ops:
  1.3 13.9 %collective-permute-start = (f32[112,256]{1,0:T(8,128)S(1)}, f32[112,256]{1,0:T(8,128)S(1)}, u32[]{:S(2)}, u32[]{:S(2)}) collective-permute-start(f32[112,256]{1,0:T(8,128)S(1)} %get-tuple-element.40), channel_id=1, source_target_pairs={{128,256},{129,257},{130,258},{131,259},{132,260},{133,261},{134,2... | collective-permute-start | bytes 344072 | tf_op jit(solution)/shard_map/ppermute | solution.py:539
  3.4 8.3 %collective-permute-start.1 = (f32[40,256]{1,0:T(8,128)S(1)}, f32[40,256]{1,0:T(8,128)S(1)}, u32[]{:S(2)}, u32[]{:S(2)}) collective-permute-start(f32[40,256]{1,0:T(8,128)S(1)} %get-tuple-element.41.even), channel_id=1, source_target_pairs={{0,1},{2,3},{4,5},{6,7},{8,9},{10,11},{12,13},{14,15},{16,17},{18,... | collective-permute-start | bytes 122888 | tf_op jit(solution)/shard_map/ppermute | solution.py:539
  5.5 9.7 %collective-permute-start.2 = (f32[40,256]{1,0:T(8,128)S(1)}, f32[40,256]{1,0:T(8,128)S(1)}, u32[]{:S(2)}, u32[]{:S(2)}) collective-permute-start(f32[40,256]{1,0:T(8,128)S(1)} %get-tuple-element.42.odd), channel_id=1, source_target_pairs={{1,2},{3,4},{5,6},{7,8},{9,10},{11,12},{13,14},{15,16},{17,18},{19... | collective-permute-start | bytes 122888 | tf_op jit(solution)/shard_map/ppermute | solution.py:539
  11.1 4.1 %collective-permute-start.3 = (f32[112,256]{1,0:T(8,128)S(1)}, f32[112,256]{1,0:T(8,128)S(1)}, u32[]{:S(2)}, u32[]{:S(2)}) collective-permute-start(f32[112,256]{1,0:T(8,128)S(1)} %get-tuple-element.44), channel_id=1, source_target_pairs={{159,287},{191,319},{223,351},{255,383},{415,543},{447,575},{479,6... | collective-permute-start | bytes 344072 | tf_op jit(solution)/shard_map/ppermute | solution.py:539
  11.8 3.4 %collective-permute-start.4 = (f32[40,256]{1,0:T(8,128)S(1)}, f32[40,256]{1,0:T(8,128)S(1)}, u32[]{:S(2)}, u32[]{:S(2)}) collective-permute-start(f32[40,256]{1,0:T(8,128)S(1)} %get-tuple-element.49), channel_id=1, source_target_pairs={{30,31},{62,63},{94,95},{126,127},{158,159},{190,191},{222,223},{2... | collective-permute-start | bytes 122888 | tf_op jit(solution)/shard_map/ppermute | solution.py:539
  14.5 0.7 %collective-permute-start.5 = (f32[40,256]{1,0:T(8,128)S(1)}, f32[40,256]{1,0:T(8,128)S(1)}, u32[]{:S(2)}, u32[]{:S(2)}) collective-permute-start(f32[40,256]{1,0:T(8,128)S(1)} %shard_map.40), channel_id=1, source_target_pairs={{29,30},{61,62},{93,94},{125,126},{157,158},{189,190},{221,222},{2... | collective-permute-start | bytes 122888 | tf_op jit(solution)/shard_map/ppermute | solution.py:539
  15.7 5.6 %collective-permute-start.6 = (f32[64,256]{1,0:T(8,128)S(1)}, f32[64,256]{1,0:T(8,128)S(1)}, u32[]{:S(2)}, u32[]{:S(2)}) collective-permute-start(f32[64,256]{1,0:T(8,128)S(1)} %get-tuple-element.57), channel_id=1, source_target_pairs={{128,256},{129,257},{130,258},{131,259},{132,260},{133,261},{134,2... | collective-permute-start | bytes 196616 | tf_op jit(solution)/shard_map/ppermute | solution.py:539
  21.7 15.6 %collective-permute-start.7 = (f32[72,128]{1,0:T(8,128)S(1)}, f32[72,128]{1,0:T(8,128)S(1)}, u32[]{:S(2)}, u32[]{:S(2)}) collective-permute-start(f32[72,128]{1,0:T(8,128)S(1)} %get-tuple-element.64), channel_id=1, source_target_pairs={{2,3},{4,5},{6,7},{8,9},{10,11},{12,13},{14,15},{16,17},{18,19},{2... | collective-permute-start | bytes 110600 | tf_op jit(solution)/shard_map/ppermute | solution.py:539
  34.1 5.9 %collective-permute-start.8 = (f32[72,128]{1,0:T(8,128)S(1)}, f32[72,128]{1,0:T(8,128)S(1)}, u32[]{:S(2)}, u32[]{:S(2)}) collective-permute-start(f32[72,128]{1,0:T(8,128)S(1)} %get-tuple-element.65), channel_id=1, source_target_pairs={{1,2},{3,4},{5,6},{7,8},{9,10},{11,12},{13,14},{15,16},{17,18},{19... | collective-permute-start | bytes 110600 | tf_op jit(solution)/shard_map/ppermute | solution.py:539
  36.0 6.0 %collective-permute-start.9 = (f32[72,128]{1,0:T(8,128)S(1)}, f32[72,128]{1,0:T(8,128)S(1)}, u32[]{:S(2)}, u32[]{:S(2)}) collective-permute-start(f32[72,128]{1,0:T(8,128)S(1)} %get-tuple-element.66), channel_id=1, source_target_pairs={{30,31},{62,63},{94,95},{126,127},{158,159},{190,191},{222,223},{2... | collective-permute-start | bytes 110600 | tf_op jit(solution)/shard_map/ppermute | solution.py:539

commit v12 on v10

--- a/solution.py
+++ b/solution.py
@@ -70,16 +70,15 @@
 
 def pair_z(low, high):
     lane = lax.broadcasted_iota(jnp.int32, low.shape, 1)
-    low = low + pltpu.roll(low, CZ - 1, 1)
-    high = high + pltpu.roll(high, CZ - 1, 1)
     index = (2 * lane) % CZ
-    return jnp.where(lane < CZ // 2, lanes(low, index), lanes(high, index))
-
-
-def spread_z(v, out):
+    first = jnp.where(lane < CZ // 2, lanes(low, index), lanes(high, index))
+    second = jnp.where(lane < CZ // 2, lanes(low, index + 1), lanes(high, index + 1))
+    return first + second
+
+
+def spread_z(v):
     half = lax.broadcasted_iota(jnp.int32, v.shape, 1) // 2
-    out[:, :CZ] = lanes(v, half)
-    out[:, CZ:] = lanes(v, half + CZ // 2)
+    return lanes(v, half), lanes(v, half + CZ // 2)
 
 
 def diag_of(n):
@@ -419,7 +418,7 @@
 
 def last_kernel(
     g, b, w, left, chip, both, f2, f2low, f2high, c1x, wc, cleft, cchip, c2z, even1, odd, even2,
-    out, cboth, col, line, line3, fine, corr, col2, s1, gline, g1line,
+    out, cboth, col, line, line3, corr, col2, s1, gline, g1line,
 ):
     wide = Wide(g, b, w, left, chip)
     a = Coarse(c1x, wc, cleft, partner(cchip))
@@ -462,21 +461,26 @@
             + beside_z(c)
             + beside_y(c, line3[0, x + 2 : x + 3, :], line3[1, x + 2 : x + 3, :])
         )
-        fine[pl.ds((x + 1) * BY, CY, stride=2), :] = c4
-        fine[pl.ds((x + 1) * BY + 1, CY, stride=2), :] = c4
+        for half, v in enumerate(spread_z(c4)):
+            corr[half, pl.ds((x + 1) * BY, CY, stride=2), :] = v
+            corr[half, pl.ds((x + 1) * BY + 1, CY, stride=2), :] = v
     for s, (side, y) in enumerate(sides):
         for x in range(-1, 5):
             col[x + 1 : x + 2, :] = c3[x][y : y + 1]
         mid = line3[s, 1:7, :]
         third = side[Z_R : Z_R + 6, :] + side[Z_V : Z_V + 6, :] * line[s, 2:8, :]
-        fine[6 * BY + 8 * s : 6 * BY + 8 * s + 6, :] = (
+        fourth = (
             KEEP * mid
             + side[Z_C + 2 : Z_C + 8, :]
             + side[Z_W + 2 : Z_W + 8, :]
             * (line3[s, 0:6, :] + line3[s, 2:8, :] + beside_z(mid) + third + col[0:6, :])
         )
-        fine[6 * BY + 8 * s + 6 : 6 * BY + 8 * s + 8, :] = jnp.zeros((2, CZ), F32)
-    spread_z(fine[...], corr)
+        for half, v in enumerate(spread_z(fourth)):
+            corr[half, 6 * BY + 8 * s : 6 * BY + 8 * s + 6, :] = v
+
+    def corr_at(k, n):
+        return jnp.concatenate([corr[0, k : k + n, :], corr[1, k : k + n, :]], axis=1)
+
     g0 = {}
     for x in range(-2, 10):
         if x == -2:
@@ -485,12 +489,12 @@
             f = slab(a.right, 2)
         else:
             f = slab(f2, x + 1)
-        g0[x] = f + slab(corr, (x + 2) // 2)
+        g0[x] = f + corr_at((x + 2) // 2 * BY, BY)
     for s, (cside, side, y, f2side) in enumerate(((clow, low, 0, f2low), (chigh, high, BY - 1, f2high))):
         base = 6 * BY + 8 * s
         for x in range(-1, 9):
             k = base + (x + 2) // 2
-            col2[x + 1 : x + 2, :] = corr[k : k + 1, :]
+            col2[x + 1 : x + 2, :] = corr_at(k, 1)
         gline[s, 1:9, :] = f2side[...] + col2[1:9, :]
         for j, x in enumerate((-1, 8)):
             k = Z_K + 2 * j
@@ -531,17 +535,10 @@
         )
 
 
-def send(v, links):
+def swap(v, pairs):
     n = lax.axis_size("dev")
-    return lax.ppermute(v, ("group", "dev"), [(i * n + j, k * n + l) for (i, j), (k, l) in links])
-
-
-def back(links):
-    return [(j, i) for i, j in links]
-
-
-def swap(v, pairs):
-    return send(v, pairs + back(pairs))
+    links = [(i * n + j, k * n + l) for (i, j), (k, l) in pairs]
+    return lax.ppermute(v, ("group", "dev"), links + [(j, i) for i, j in links])
 
 
 def share_chip(v):
@@ -557,14 +554,6 @@
 def dev_pairs(start, keep):
     devs = [d for d in range(start, lax.axis_size("dev") - 1, 2) if keep(d)]
     return [((i, d), (i, d + 1)) for i in range(lax.axis_size("group")) for d in devs]
-
-
-def is_start(d):
-    return d % RUN == 0
-
-
-def in_middle(d):
-    return not (is_start(d) or before_end(d))
 
 
 def is_end(d):
@@ -613,17 +602,16 @@
         g, b, w, left, chip, both, f2, f2low, f2high, c1, wc, cleft, cchip,
         scratch=[(13, 8, NZ), (5, 8, NZ), (8, CZ), (2, Z_ROWS, CZ)],
     )
-    inner, start, end = (dev_pairs(0, keep) for keep in (in_middle, is_start, before_end))
-    even1 = send(even, inner + back(inner) + back(start))
+    even1 = swap(even, dev_pairs(0, lambda d: not before_end(d)))
     odd = swap(odd, dev_pairs(1, lambda d: True))
-    even2 = send(even2, end + back(end) + start)
+    even2 = swap(even2, dev_pairs(0, before_end))
     (out,) = call(
         last_kernel,
         [block],
         g, b, w, left, chip, both, f2, f2low, f2high, c1x, wc, cleft, cchip, c2z, even1, odd, even2,
         scratch=[
             (2, Z_ROWS, CZ),
-            (16, CZ), (2, 16, CZ), (2, 8, CZ), (6 * BY + 16, CZ), (6 * BY + 16, NZ), (16, NZ), (8, NZ), (2, 16, NZ), (2, 8, NZ),
+            (16, CZ), (2, 16, CZ), (2, 8, CZ), (2, 6 * BY + 16, CZ), (16, NZ), (8, NZ), (2, 16, NZ), (2, 8, NZ),
         ],
         hbm_out=True,
     )

time: 43.5 us -> 43.3 us (level)
  the two profiles are of different devices: /device:TPU:62 before, /device:TPU:25 now
where the time goes in v12:
time: 43.3 us; the launch traced here: 42.6 us
  starting transfers between devices  32.3 us (75%)
  blocking collectives  4.46 us (10%)
  Pallas kernels  3.29 us (8%)
  waiting for transfers between devices  2.38 us (5%)
    ppermute x10, starting transfers between devices, swap(): return lax.ppermute(v, ('group', 'dev'), links + [(j, i) for i, j in links])  32.3 us
    all_gather x2, blocking collectives, share_chip(): return lax.all_gather(v, 'group', axis_index_groups=groups)  4.46 us
    pallas_call x6, Pallas kernels, call(): pl.pallas_call(kernel, out_shape=[make(s, F32) for s in outs], in_specs=[...  3.29 us
    ppermute x10, waiting for transfers between devices, swap(): return lax.ppermute(v, ('group', 'dev'), links + [(j, i) for i, j in links])  2.38 us
  transfers between devices with their start and end apart: 10, of which 2 were waited for; matrix products, arithmetic and copies ran while one was open for 0% of the time, Pallas kernels for 0%

profile of v12, /device:TPU:25, one launch (start us, length us, event | category | flops | bytes accessed | tf_op | source)
XLA Modules:
  0.0 42.6 jit_solution(15173473593078087207)
XLA Ops:
  0.0 1.3 %shard_map.37 = (f32[112,256]{1,0:T(8,128)S(1)}, f32[112,256]{1,0:T(8,128)S(1)}, f32[112,256]{1,0:T(8,128)S(1)}, f32[40,256]{1,0:T(8,128)S(1)}, f32[40,256]{1,0:...) custom-call(f32[8,16,256]{2,1,0:T(8,128)} %g_hbm.1, ...), custom_call_target="tpu_custom_call" | custom-call | tf_op jit(solution)/shard_map/pallas_call | solution.py:19
  1.3 3.7 %collective-permute-start = (f32[112,256]{1,0:T(8,128)S(1)}, f32[112,256]{1,0:T(8,128)S(1)}, u32[]{:S(2)}, u32[]{:S(2)}) collective-permute-start(f32[112,256]{1,0:T(8,128)S(1)} %get-tuple-element.41), channel_id=1, source_target_pairs={{128,256},{129,257},{130,258},{131,259},{132,260},{133,261},{134,2... | collective-permute-start | bytes 344072 | tf_op jit(solution)/shard_map/ppermute | solution.py:541
  4.9 3.5 %collective-permute-start.1 = (f32[40,256]{1,0:T(8,128)S(1)}, f32[40,256]{1,0:T(8,128)S(1)}, u32[]{:S(2)}, u32[]{:S(2)}) collective-permute-start(f32[40,256]{1,0:T(8,128)S(1)} %get-tuple-element.42.even), channel_id=1, source_target_pairs={{0,1},{2,3},{4,5},{6,7},{8,9},{10,11},{12,13},{14,15},{16,17},{18,... | collective-permute-start | bytes 122888 | tf_op jit(solution)/shard_map/ppermute | solution.py:541
  8.5 12.7 %collective-permute-start.2 = (f32[40,256]{1,0:T(8,128)S(1)}, f32[40,256]{1,0:T(8,128)S(1)}, u32[]{:S(2)}, u32[]{:S(2)}) collective-permute-start(f32[40,256]{1,0:T(8,128)S(1)} %get-tuple-element.43.odd), channel_id=1, source_target_pairs={{1,2},{3,4},{5,6},{7,8},{9,10},{11,12},{13,14},{15,16},{17,18},{19... | collective-permute-start | bytes 122888 | tf_op jit(solution)/shard_map/ppermute | solution.py:541
  21.2 0.7 %collective-permute-start.3 = (f32[112,256]{1,0:T(8,128)S(1)}, f32[112,256]{1,0:T(8,128)S(1)}, u32[]{:S(2)}, u32[]{:S(2)}) collective-permute-start(f32[112,256]{1,0:T(8,128)S(1)} %get-tuple-element.45), channel_id=1, source_target_pairs={{159,287},{191,319},{223,351},{255,383},{415,543},{447,575},{479,6... | collective-permute-start | bytes 344072 | tf_op jit(solution)/shard_map/ppermute | solution.py:541
  21.9 0.0 collective-permute-done.1.even.met
  21.9 0.7 %collective-permute-start.4 = (f32[40,256]{1,0:T(8,128)S(1)}, f32[40,256]{1,0:T(8,128)S(1)}, u32[]{:S(2)}, u32[]{:S(2)}) collective-permute-start(f32[40,256]{1,0:T(8,128)S(1)} %get-tuple-element.50), channel_id=1, source_target_pairs={{30,31},{62,63},{94,95},{126,127},{158,159},{190,191},{222,223},{2... | collective-permute-start | bytes 122888 | tf_op jit(solution)/shard_map/ppermute | solution.py:541
  22.6 0.7 %collective-permute-start.5 = (f32[40,256]{1,0:T(8,128)S(1)}, f32[40,256]{1,0:T(8,128)S(1)}, u32[]{:S(2)}, u32[]{:S(2)}) collective-permute-start(f32[40,256]{1,0:T(8,128)S(1)} %get-tuple-element.51), channel_id=1, source_target_pairs={{29,30},{61,62},{93,94},{125,126},{157,158},{189,190},{221,222},{2... | collective-permute-start | bytes 122888 | tf_op jit(solution)/shard_map/ppermute | solution.py:541
  23.3 2.6 %all-gather = f32[224,256]{1,0:T(8,128)S(1)} all-gather(f32[112,256]{1,0:T(8,128)S(1)} %get-tuple-element.47), channel_id=2, replica_groups={{0,128},{256,384},{512,640},{768,896},{1,129},{257,385},{513,641},{769,..., dimensions={0}, use_global_device_ids=true | all-gather | bytes 344064 | tf_op jit(solution)/shard_map/all_gather | solution.py:546
  25.8 0.0 collective-permute-done.2.odd
  25.8 0.0 collective-permute-done.cross
  25.8 0.0 collective-permute-done.4.even2
  25.9 0.0 collective-permute-done.3.cross2
  25.9 0.4 %shard_map.40 = (f32[160,256]{1,0:T(8,128)S(1)}, f32[8,256]{1,0:T(8,128)S(1)}, f32[8,256]{1,0:T(8,128)S(1)}, f32[32,128]{1,0:T(8,128)S(1)}, f32[32,128]{1,0:T(8,...) custom-call(f32[8,16,256]{2,1,0:T(8,128)S(1)} %get-tuple-element.37., ...), custom_call_target="tpu_custom_call" | custom-call | tf_op jit(solution)/shard_map/pallas_call | solution.py:19
  26.3 3.4 %collective-permute-start.6 = (f32[64,256]{1,0:T(8,128)S(1)}, f32[64,256]{1,0:T(8,128)S(1)}, u32[]{:S(2)}, u32[]{:S(2)}) collective-permute-start(f32[64,256]{1,0:T(8,128)S(1)} %get-tuple-element.59), channel_id=1, source_target_pairs={{128,256},{129,257},{130,258},{131,259},{132,260},{133,261},{134,2... | collective-permute-start | bytes 196616 | tf_op jit(solution)/shard_map/ppermute | solution.py:541
  29.7 1.9 %all-gather.1 = f32[128,256]{1,0:T(8,128)S(1)} all-gather(f32[64,256]{1,0:T(8,128)S(1)} %get-tuple-element.60), channel_id=3, replica_groups={{0,128},{256,384},{512,640},{768,896},{1,129},{257,385},{513,641},{769,..., dimensions={0}, use_global_device_ids=true | all-gather | bytes 196608 | tf_op jit(solution)/shard_map/all_gather | solution.py:546
  31.6 0.3 collective-permute-done.6.cleft
  31.9 0.4 shard_map.41
  32.3 1.9 %collective-permute-start.7 = (f32[72,128]{1,0:T(8,128)S(1)}, f32[72,128]{1,0:T(8,128)S(1)}, u32[]{:S(2)}, u32[]{:S(2)}) collective-permute-start(f32[72,128]{1,0:T(8,128)S(1)} %get-tuple-element.66), channel_id=1, source_target_pairs={{0,1},{2,3},{4,5},{6,7},{8,9},{10,11},{12,13},{14,15},{16,17},{18,... | collective-permute-start | bytes 110600 | tf_op jit(solution)/shard_map/ppermute | solution.py:541
  34.2 4.5 %collective-permute-start.8 = (f32[72,128]{1,0:T(8,128)S(1)}, f32[72,128]{1,0:T(8,128)S(1)}, u32[]{:S(2)}, u32[]{:S(2)}) collective-permute-start(f32[72,128]{1,0:T(8,128)S(1)} %get-tuple-element.67), channel_id=1, source_target_pairs={{1,2},{3,4},{5,6},{7,8},{9,10},{11,12},{13,14},{15,16},{17,18},{19... | collective-permute-start | bytes 110600 | tf_op jit(solution)/shard_map/ppermute | solution.py:541
  38.7 0.7 %collective-permute-start.9 = (f32[72,128]{1,0:T(8,128)S(1)}, f32[72,128]{1,0:T(8,128)S(1)}, u32[]{:S(2)}, u32[]{:S(2)}) collective-permute-start(f32[72,128]{1,0:T(8,128)S(1)} %get-tuple-element.68), channel_id=1, source_target_pairs={{30,31},{62,63},{94,95},{126,127},{158,159},{190,191},{222,223},{2... | collective-permute-start | bytes 110600 | tf_op jit(solution)/shard_map/ppermute | solution.py:541
  39.3 0.0 collective-permute-done.7.even1
  39.4 2.0 %collective-permute-done.8.odd = f32[72,128]{1,0:T(8,128)S(1)} collective-permute-done((f32[72,128]{1,0:T(8,128)S(1)}, f32[72,128]{1,0:T(8,128)S(1)}, u32[]{:S(2)}, u32[]{:S(2)}) %collective-permute-start.8) | collective-permute-done | bytes 36896 | tf_op jit(solution)/shard_map/ppermute | solution.py:541
  41.4 1.2 %shard_map.42 = f32[8,16,256]{2,1,0:T(8,128)} custom-call(f32[8,16,256]{2,1,0:T(8,128)S(1)} %get-tuple-element.37.g, f32[8,16,256]{2,1,0:T(8,128)S(1)} %get-tuple-element.38.b, f32[8,16,256]{2,1,0:T(8,128)S(1)} %get-tuple-element.39.w, f32[112,256]{1,0:T(8,128)S(1)} %get-tuple-element.52.left, f32[2,112,256]{2,1,0:T(8,128)S(1)} %bitcast.4, ...), custom_call_target="tpu_custom_call" | custom-call | tf_op jit(solution)/shard_map/pallas_call | solution.py:19
  (4 shorter events, 0.0 us)
Async XLA Ops:
  1.3 24.6 %collective-permute-start = (f32[112,256]{1,0:T(8,128)S(1)}, f32[112,256]{1,0:T(8,128)S(1)}, u32[]{:S(2)}, u32[]{:S(2)}) collective-permute-start(f32[112,256]{1,0:T(8,128)S(1)} %get-tuple-element.41), channel_id=1, source_target_pairs={{128,256},{129,257},{130,258},{131,259},{132,260},{133,261},{134,2... | collective-permute-start | bytes 344072 | tf_op jit(solution)/shard_map/ppermute | solution.py:541
  4.9 16.9 %collective-permute-start.1 = (f32[40,256]{1,0:T(8,128)S(1)}, f32[40,256]{1,0:T(8,128)S(1)}, u32[]{:S(2)}, u32[]{:S(2)}) collective-permute-start(f32[40,256]{1,0:T(8,128)S(1)} %get-tuple-element.42.even), channel_id=1, source_target_pairs={{0,1},{2,3},{4,5},{6,7},{8,9},{10,11},{12,13},{14,15},{16,17},{18,... | collective-permute-start | bytes 122888 | tf_op jit(solution)/shard_map/ppermute | solution.py:541
  8.5 17.3 %collective-permute-start.2 = (f32[40,256]{1,0:T(8,128)S(1)}, f32[40,256]{1,0:T(8,128)S(1)}, u32[]{:S(2)}, u32[]{:S(2)}) collective-permute-start(f32[40,256]{1,0:T(8,128)S(1)} %get-tuple-element.43.odd), channel_id=1, source_target_pairs={{1,2},{3,4},{5,6},{7,8},{9,10},{11,12},{13,14},{15,16},{17,18},{19... | collective-permute-start | bytes 122888 | tf_op jit(solution)/shard_map/ppermute | solution.py:541
  21.2 4.7 %collective-permute-start.3 = (f32[112,256]{1,0:T(8,128)S(1)}, f32[112,256]{1,0:T(8,128)S(1)}, u32[]{:S(2)}, u32[]{:S(2)}) collective-permute-start(f32[112,256]{1,0:T(8,128)S(1)} %get-tuple-element.45), channel_id=1, source_target_pairs={{159,287},{191,319},{223,351},{255,383},{415,543},{447,575},{479,6... | collective-permute-start | bytes 344072 | tf_op jit(solution)/shard_map/ppermute | solution.py:541
  21.9 3.9 %collective-permute-start.4 = (f32[40,256]{1,0:T(8,128)S(1)}, f32[40,256]{1,0:T(8,128)S(1)}, u32[]{:S(2)}, u32[]{:S(2)}) collective-permute-start(f32[40,256]{1,0:T(8,128)S(1)} %get-tuple-element.50), channel_id=1, source_target_pairs={{30,31},{62,63},{94,95},{126,127},{158,159},{190,191},{222,223},{2... | collective-permute-start | bytes 122888 | tf_op jit(solution)/shard_map/ppermute | solution.py:541
  22.6 3.3 %collective-permute-start.5 = (f32[40,256]{1,0:T(8,128)S(1)}, f32[40,256]{1,0:T(8,128)S(1)}, u32[]{:S(2)}, u32[]{:S(2)}) collective-permute-start(f32[40,256]{1,0:T(8,128)S(1)} %get-tuple-element.51), channel_id=1, source_target_pairs={{29,30},{61,62},{93,94},{125,126},{157,158},{189,190},{221,222},{2... | collective-permute-start | bytes 122888 | tf_op jit(solution)/shard_map/ppermute | solution.py:541
  26.3 5.6 %collective-permute-start.6 = (f32[64,256]{1,0:T(8,128)S(1)}, f32[64,256]{1,0:T(8,128)S(1)}, u32[]{:S(2)}, u32[]{:S(2)}) collective-permute-start(f32[64,256]{1,0:T(8,128)S(1)} %get-tuple-element.59), channel_id=1, source_target_pairs={{128,256},{129,257},{130,258},{131,259},{132,260},{133,261},{134,2... | collective-permute-start | bytes 196616 | tf_op jit(solution)/shard_map/ppermute | solution.py:541
  32.3 7.1 %collective-permute-start.7 = (f32[72,128]{1,0:T(8,128)S(1)}, f32[72,128]{1,0:T(8,128)S(1)}, u32[]{:S(2)}, u32[]{:S(2)}) collective-permute-start(f32[72,128]{1,0:T(8,128)S(1)} %get-tuple-element.66), channel_id=1, source_target_pairs={{0,1},{2,3},{4,5},{6,7},{8,9},{10,11},{12,13},{14,15},{16,17},{18,... | collective-permute-start | bytes 110600 | tf_op jit(solution)/shard_map/ppermute | solution.py:541
  34.2 7.2 %collective-permute-start.8 = (f32[72,128]{1,0:T(8,128)S(1)}, f32[72,128]{1,0:T(8,128)S(1)}, u32[]{:S(2)}, u32[]{:S(2)}) collective-permute-start(f32[72,128]{1,0:T(8,128)S(1)} %get-tuple-element.67), channel_id=1, source_target_pairs={{1,2},{3,4},{5,6},{7,8},{9,10},{11,12},{13,14},{15,16},{17,18},{19... | collective-permute-start | bytes 110600 | tf_op jit(solution)/shard_map/ppermute | solution.py:541
  38.7 2.7 %collective-permute-start.9 = (f32[72,128]{1,0:T(8,128)S(1)}, f32[72,128]{1,0:T(8,128)S(1)}, u32[]{:S(2)}, u32[]{:S(2)}) collective-permute-start(f32[72,128]{1,0:T(8,128)S(1)} %get-tuple-element.68), channel_id=1, source_target_pairs={{30,31},{62,63},{94,95},{126,127},{158,159},{190,191},{222,223},{2... | collective-permute-start | bytes 110600 | tf_op jit(solution)/shard_map/ppermute | solution.py:541

commit v13 on v12

--- a/solution.py
+++ b/solution.py
@@ -535,10 +535,17 @@
         )
 
 
+def send(v, links):
+    n = lax.axis_size("dev")
+    return lax.ppermute(v, ("group", "dev"), [(i * n + j, k * n + l) for (i, j), (k, l) in links])
+
+
+def back(links):
+    return [(j, i) for i, j in links]
+
+
 def swap(v, pairs):
-    n = lax.axis_size("dev")
-    links = [(i * n + j, k * n + l) for (i, j), (k, l) in pairs]
-    return lax.ppermute(v, ("group", "dev"), links + [(j, i) for i, j in links])
+    return send(v, pairs + back(pairs))
 
 
 def share_chip(v):
@@ -554,6 +561,14 @@
 def dev_pairs(start, keep):
     devs = [d for d in range(start, lax.axis_size("dev") - 1, 2) if keep(d)]
     return [((i, d), (i, d + 1)) for i in range(lax.axis_size("group")) for d in devs]
+
+
+def is_start(d):
+    return d % RUN == 0
+
+
+def in_middle(d):
+    return not (is_start(d) or before_end(d))
 
 
 def is_end(d):
@@ -602,9 +617,10 @@
         g, b, w, left, chip, both, f2, f2low, f2high, c1, wc, cleft, cchip,
         scratch=[(13, 8, NZ), (5, 8, NZ), (8, CZ), (2, Z_ROWS, CZ)],
     )
-    even1 = swap(even, dev_pairs(0, lambda d: not before_end(d)))
+    inner, start, end = (dev_pairs(0, keep) for keep in (in_middle, is_start, before_end))
+    even1 = send(even, inner + back(inner) + back(start))
     odd = swap(odd, dev_pairs(1, lambda d: True))
-    even2 = swap(even2, dev_pairs(0, before_end))
+    even2 = send(even2, end + back(end) + start)
     (out,) = call(
         last_kernel,
         [block],

time: 43.3 us -> 43.4 us (level)
  the two profiles are of different devices: /device:TPU:25 before, /device:TPU:62 now
where the time goes in v13:
time: 43.4 us; the launch traced here: 43.1 us
  starting transfers between devices  30.2 us (70%)
  waiting for transfers between devices  5.57 us (13%)
  blocking collectives  3.87 us (9%)
  Pallas kernels  3.28 us (8%)
    ppermute x10, starting transfers between devices, send(): lax.ppermute(v, ('group', 'dev'), [(i * n + j, k * n + l) for (i, j), (k,...  30.2 us
    ppermute x10, waiting for transfers between devices, send(): lax.ppermute(v, ('group', 'dev'), [(i * n + j, k * n + l) for (i, j), (k,...  5.57 us
    all_gather x2, blocking collectives, share_chip(): return lax.all_gather(v, 'group', axis_index_groups=groups)  3.87 us
    pallas_call x6, Pallas kernels, call(): pl.pallas_call(kernel, out_shape=[make(s, F32) for s in outs], in_specs=[...  3.28 us
  transfers between devices with their start and end apart: 10, of which 3 were waited for; matrix products, arithmetic and copies ran while one was open for 0% of the time, Pallas kernels for 0%

profile of v13, /device:TPU:62, one launch (start us, length us, event | category | flops | bytes accessed | tf_op | source)
XLA Modules:
  0.0 43.1 jit_solution(12915924248490236063)
XLA Ops:
  0.0 1.3 %shard_map.37 = (f32[112,256]{1,0:T(8,128)S(1)}, f32[112,256]{1,0:T(8,128)S(1)}, f32[112,256]{1,0:T(8,128)S(1)}, f32[40,256]{1,0:T(8,128)S(1)}, f32[40,256]{1,0:...) custom-call(f32[8,16,256]{2,1,0:T(8,128)} %g_hbm.1, ...), custom_call_target="tpu_custom_call" | custom-call | tf_op jit(solution)/shard_map/pallas_call | solution.py:19
  1.3 2.2 %collective-permute-start = (f32[112,256]{1,0:T(8,128)S(1)}, f32[112,256]{1,0:T(8,128)S(1)}, u32[]{:S(2)}, u32[]{:S(2)}) collective-permute-start(f32[112,256]{1,0:T(8,128)S(1)} %get-tuple-element.41), channel_id=1, source_target_pairs={{128,256},{129,257},{130,258},{131,259},{132,260},{133,261},{134,2... | collective-permute-start | bytes 344072 | tf_op jit(solution)/shard_map/ppermute | solution.py:540
  3.4 2.0 %collective-permute-start.1 = (f32[40,256]{1,0:T(8,128)S(1)}, f32[40,256]{1,0:T(8,128)S(1)}, u32[]{:S(2)}, u32[]{:S(2)}) collective-permute-start(f32[40,256]{1,0:T(8,128)S(1)} %get-tuple-element.42.even), channel_id=1, source_target_pairs={{0,1},{2,3},{4,5},{6,7},{8,9},{10,11},{12,13},{14,15},{16,17},{18,... | collective-permute-start | bytes 122888 | tf_op jit(solution)/shard_map/ppermute | solution.py:540
  5.5 5.6 %collective-permute-start.2 = (f32[40,256]{1,0:T(8,128)S(1)}, f32[40,256]{1,0:T(8,128)S(1)}, u32[]{:S(2)}, u32[]{:S(2)}) collective-permute-start(f32[40,256]{1,0:T(8,128)S(1)} %get-tuple-element.43.odd), channel_id=1, source_target_pairs={{1,2},{3,4},{5,6},{7,8},{9,10},{11,12},{13,14},{15,16},{17,18},{19... | collective-permute-start | bytes 122888 | tf_op jit(solution)/shard_map/ppermute | solution.py:540
  11.1 0.7 %collective-permute-start.3 = (f32[112,256]{1,0:T(8,128)S(1)}, f32[112,256]{1,0:T(8,128)S(1)}, u32[]{:S(2)}, u32[]{:S(2)}) collective-permute-start(f32[112,256]{1,0:T(8,128)S(1)} %get-tuple-element.45), channel_id=1, source_target_pairs={{159,287},{191,319},{223,351},{255,383},{415,543},{447,575},{479,6... | collective-permute-start | bytes 344072 | tf_op jit(solution)/shard_map/ppermute | solution.py:540
  11.8 0.0 collective-permute-done.1.even.met
  11.8 0.7 %collective-permute-start.4 = (f32[40,256]{1,0:T(8,128)S(1)}, f32[40,256]{1,0:T(8,128)S(1)}, u32[]{:S(2)}, u32[]{:S(2)}) collective-permute-start(f32[40,256]{1,0:T(8,128)S(1)} %get-tuple-element.50), channel_id=1, source_target_pairs={{30,31},{62,63},{94,95},{126,127},{158,159},{190,191},{222,223},{2... | collective-permute-start | bytes 122888 | tf_op jit(solution)/shard_map/ppermute | solution.py:540
  12.5 0.7 %collective-permute-start.5 = (f32[40,256]{1,0:T(8,128)S(1)}, f32[40,256]{1,0:T(8,128)S(1)}, u32[]{:S(2)}, u32[]{:S(2)}) collective-permute-start(f32[40,256]{1,0:T(8,128)S(1)} %get-tuple-element.51), channel_id=1, source_target_pairs={{29,30},{61,62},{93,94},{125,126},{157,158},{189,190},{221,222},{2... | collective-permute-start | bytes 122888 | tf_op jit(solution)/shard_map/ppermute | solution.py:540
  13.2 2.0 %all-gather = f32[224,256]{1,0:T(8,128)S(1)} all-gather(f32[112,256]{1,0:T(8,128)S(1)} %get-tuple-element.47), channel_id=2, replica_groups={{0,128},{256,384},{512,640},{768,896},{1,129},{257,385},{513,641},{769,..., dimensions={0}, use_global_device_ids=true | all-gather | bytes 344064 | tf_op jit(solution)/shard_map/all_gather | solution.py:553
  15.1 0.0 collective-permute-done.2.odd
  15.1 0.0 collective-permute-done.cross
  15.2 0.0 collective-permute-done.4.even2
  15.2 0.0 collective-permute-done.3.cross2
  15.2 0.4 %shard_map.40 = (f32[160,256]{1,0:T(8,128)S(1)}, f32[8,256]{1,0:T(8,128)S(1)}, f32[8,256]{1,0:T(8,128)S(1)}, f32[32,128]{1,0:T(8,128)S(1)}, f32[32,128]{1,0:T(8,...) custom-call(f32[8,16,256]{2,1,0:T(8,128)S(1)} %get-tuple-element.37., ...), custom_call_target="tpu_custom_call" | custom-call | tf_op jit(solution)/shard_map/pallas_call | solution.py:19
  15.7 2.8 %collective-permute-start.6 = (f32[64,256]{1,0:T(8,128)S(1)}, f32[64,256]{1,0:T(8,128)S(1)}, u32[]{:S(2)}, u32[]{:S(2)}) collective-permute-start(f32[64,256]{1,0:T(8,128)S(1)} %get-tuple-element.59), channel_id=1, source_target_pairs={{128,256},{129,257},{130,258},{131,259},{132,260},{133,261},{134,2... | collective-permute-start | bytes 196616 | tf_op jit(solution)/shard_map/ppermute | solution.py:540
  18.5 1.9 %all-gather.1 = f32[128,256]{1,0:T(8,128)S(1)} all-gather(f32[64,256]{1,0:T(8,128)S(1)} %get-tuple-element.60), channel_id=3, replica_groups={{0,128},{256,384},{512,640},{768,896},{1,129},{257,385},{513,641},{769,..., dimensions={0}, use_global_device_ids=true | all-gather | bytes 196608 | tf_op jit(solution)/shard_map/all_gather | solution.py:553
  20.4 0.9 %collective-permute-done.6.cleft = f32[64,256]{1,0:T(8,128)S(1)} collective-permute-done((f32[64,256]{1,0:T(8,128)S(1)}, f32[64,256]{1,0:T(8,128)S(1)}, u32[]{:S(2)}, u32[]{:S(2)}) %collective-permute-start.6) | collective-permute-done | bytes 65568 | tf_op jit(solution)/shard_map/ppermute | solution.py:540
  21.2 0.4 shard_map.41
  21.6 12.4 %collective-permute-start.7 = (f32[72,128]{1,0:T(8,128)S(1)}, f32[72,128]{1,0:T(8,128)S(1)}, u32[]{:S(2)}, u32[]{:S(2)}) collective-permute-start(f32[72,128]{1,0:T(8,128)S(1)} %get-tuple-element.66), channel_id=1, source_target_pairs={{2,3},{4,5},{6,7},{8,9},{10,11},{12,13},{14,15},{16,17},{18,19},{2... | collective-permute-start | bytes 110600 | tf_op jit(solution)/shard_map/ppermute | solution.py:540
  34.0 1.9 %collective-permute-start.8 = (f32[72,128]{1,0:T(8,128)S(1)}, f32[72,128]{1,0:T(8,128)S(1)}, u32[]{:S(2)}, u32[]{:S(2)}) collective-permute-start(f32[72,128]{1,0:T(8,128)S(1)} %get-tuple-element.67), channel_id=1, source_target_pairs={{1,2},{3,4},{5,6},{7,8},{9,10},{11,12},{13,14},{15,16},{17,18},{19... | collective-permute-start | bytes 110600 | tf_op jit(solution)/shard_map/ppermute | solution.py:540
  35.9 1.3 %collective-permute-start.9 = (f32[72,128]{1,0:T(8,128)S(1)}, f32[72,128]{1,0:T(8,128)S(1)}, u32[]{:S(2)}, u32[]{:S(2)}) collective-permute-start(f32[72,128]{1,0:T(8,128)S(1)} %get-tuple-element.68), channel_id=1, source_target_pairs={{30,31},{62,63},{94,95},{126,127},{158,159},{190,191},{222,223},{2... | collective-permute-start | bytes 110600 | tf_op jit(solution)/shard_map/ppermute | solution.py:540
  37.2 2.6 %collective-permute-done.8.odd = f32[72,128]{1,0:T(8,128)S(1)} collective-permute-done((f32[72,128]{1,0:T(8,128)S(1)}, f32[72,128]{1,0:T(8,128)S(1)}, u32[]{:S(2)}, u32[]{:S(2)}) %collective-permute-start.8) | collective-permute-done | bytes 36896 | tf_op jit(solution)/shard_map/ppermute | solution.py:540
  39.8 2.1 %collective-permute-done.9.even2 = f32[72,128]{1,0:T(8,128)S(1)} collective-permute-done((f32[72,128]{1,0:T(8,128)S(1)}, f32[72,128]{1,0:T(8,128)S(1)}, u32[]{:S(2)}, u32[]{:S(2)}) %collective-permute-start.9) | collective-permute-done | bytes 36896 | tf_op jit(solution)/shard_map/ppermute | solution.py:540
  41.9 1.2 %shard_map.42 = f32[8,16,256]{2,1,0:T(8,128)} custom-call(f32[8,16,256]{2,1,0:T(8,128)S(1)} %get-tuple-element.37.g, f32[8,16,256]{2,1,0:T(8,128)S(1)} %get-tuple-element.38.b, f32[8,16,256]{2,1,0:T(8,128)S(1)} %get-tuple-element.39.w, f32[112,256]{1,0:T(8,128)S(1)} %get-tuple-element.52.left, f32[2,112,256]{2,1,0:T(8,128)S(1)} %bitcast.4, ...), custom_call_target="tpu_custom_call" | custom-call | tf_op jit(solution)/shard_map/pallas_call | solution.py:19
  (4 shorter events, 0.0 us)
Async XLA Ops:
  1.3 13.9 %collective-permute-start = (f32[112,256]{1,0:T(8,128)S(1)}, f32[112,256]{1,0:T(8,128)S(1)}, u32[]{:S(2)}, u32[]{:S(2)}) collective-permute-start(f32[112,256]{1,0:T(8,128)S(1)} %get-tuple-element.41), channel_id=1, source_target_pairs={{128,256},{129,257},{130,258},{131,259},{132,260},{133,261},{134,2... | collective-permute-start | bytes 344072 | tf_op jit(solution)/shard_map/ppermute | solution.py:540
  3.4 8.3 %collective-permute-start.1 = (f32[40,256]{1,0:T(8,128)S(1)}, f32[40,256]{1,0:T(8,128)S(1)}, u32[]{:S(2)}, u32[]{:S(2)}) collective-permute-start(f32[40,256]{1,0:T(8,128)S(1)} %get-tuple-element.42.even), channel_id=1, source_target_pairs={{0,1},{2,3},{4,5},{6,7},{8,9},{10,11},{12,13},{14,15},{16,17},{18,... | collective-permute-start | bytes 122888 | tf_op jit(solution)/shard_map/ppermute | solution.py:540
  5.5 9.7 %collective-permute-start.2 = (f32[40,256]{1,0:T(8,128)S(1)}, f32[40,256]{1,0:T(8,128)S(1)}, u32[]{:S(2)}, u32[]{:S(2)}) collective-permute-start(f32[40,256]{1,0:T(8,128)S(1)} %get-tuple-element.43.odd), channel_id=1, source_target_pairs={{1,2},{3,4},{5,6},{7,8},{9,10},{11,12},{13,14},{15,16},{17,18},{19... | collective-permute-start | bytes 122888 | tf_op jit(solution)/shard_map/ppermute | solution.py:540
  11.1 4.1 %collective-permute-start.3 = (f32[112,256]{1,0:T(8,128)S(1)}, f32[112,256]{1,0:T(8,128)S(1)}, u32[]{:S(2)}, u32[]{:S(2)}) collective-permute-start(f32[112,256]{1,0:T(8,128)S(1)} %get-tuple-element.45), channel_id=1, source_target_pairs={{159,287},{191,319},{223,351},{255,383},{415,543},{447,575},{479,6... | collective-permute-start | bytes 344072 | tf_op jit(solution)/shard_map/ppermute | solution.py:540
  11.8 3.3 %collective-permute-start.4 = (f32[40,256]{1,0:T(8,128)S(1)}, f32[40,256]{1,0:T(8,128)S(1)}, u32[]{:S(2)}, u32[]{:S(2)}) collective-permute-start(f32[40,256]{1,0:T(8,128)S(1)} %get-tuple-element.50), channel_id=1, source_target_pairs={{30,31},{62,63},{94,95},{126,127},{158,159},{190,191},{222,223},{2... | collective-permute-start | bytes 122888 | tf_op jit(solution)/shard_map/ppermute | solution.py:540
  12.5 2.7 %collective-permute-start.5 = (f32[40,256]{1,0:T(8,128)S(1)}, f32[40,256]{1,0:T(8,128)S(1)}, u32[]{:S(2)}, u32[]{:S(2)}) collective-permute-start(f32[40,256]{1,0:T(8,128)S(1)} %get-tuple-element.51), channel_id=1, source_target_pairs={{29,30},{61,62},{93,94},{125,126},{157,158},{189,190},{221,222},{2... | collective-permute-start | bytes 122888 | tf_op jit(solution)/shard_map/ppermute | solution.py:540
  15.7 5.6 %collective-permute-start.6 = (f32[64,256]{1,0:T(8,128)S(1)}, f32[64,256]{1,0:T(8,128)S(1)}, u32[]{:S(2)}, u32[]{:S(2)}) collective-permute-start(f32[64,256]{1,0:T(8,128)S(1)} %get-tuple-element.59), channel_id=1, source_target_pairs={{128,256},{129,257},{130,258},{131,259},{132,260},{133,261},{134,2... | collective-permute-start | bytes 196616 | tf_op jit(solution)/shard_map/ppermute | solution.py:540
  21.6 15.6 %collective-permute-start.7 = (f32[72,128]{1,0:T(8,128)S(1)}, f32[72,128]{1,0:T(8,128)S(1)}, u32[]{:S(2)}, u32[]{:S(2)}) collective-permute-start(f32[72,128]{1,0:T(8,128)S(1)} %get-tuple-element.66), channel_id=1, source_target_pairs={{2,3},{4,5},{6,7},{8,9},{10,11},{12,13},{14,15},{16,17},{18,19},{2... | collective-permute-start | bytes 110600 | tf_op jit(solution)/shard_map/ppermute | solution.py:540
  34.0 5.9 %collective-permute-start.8 = (f32[72,128]{1,0:T(8,128)S(1)}, f32[72,128]{1,0:T(8,128)S(1)}, u32[]{:S(2)}, u32[]{:S(2)}) collective-permute-start(f32[72,128]{1,0:T(8,128)S(1)} %get-tuple-element.67), channel_id=1, source_target_pairs={{1,2},{3,4},{5,6},{7,8},{9,10},{11,12},{13,14},{15,16},{17,18},{19... | collective-permute-start | bytes 110600 | tf_op jit(solution)/shard_map/ppermute | solution.py:540
  35.9 6.0 %collective-permute-start.9 = (f32[72,128]{1,0:T(8,128)S(1)}, f32[72,128]{1,0:T(8,128)S(1)}, u32[]{:S(2)}, u32[]{:S(2)}) collective-permute-start(f32[72,128]{1,0:T(8,128)S(1)} %get-tuple-element.68), channel_id=1, source_target_pairs={{30,31},{62,63},{94,95},{126,127},{158,159},{190,191},{222,223},{2... | collective-permute-start | bytes 110600 | tf_op jit(solution)/shard_map/ppermute | solution.py:540

commit v14 on v12

--- a/solution.py
+++ b/solution.py
@@ -100,11 +100,16 @@
 
 Y_G, Y_P, Y_W, Y_Q, Y_G2, Y_W2 = 0, 8, 16, 24, 32, 34
 Y_ROWS = 40
-X_ROWS = 7 * BY
+X_W = 7 * BY
+X_ROWS = X_W + 2 * CY
+
+
+def tile(base, k):
+    return slice(base + k // 2 * CY, base + (k // 2 + 1) * CY), slice(k % 2 * CZ, (k % 2 + 1) * CZ)
 
 
 def load_kernel(
-    g_hbm, b_hbm, n_hbm, cross, cross2, chip, even, odd, f1z, g, b, w, d, n, both, sems
+    g_hbm, b_hbm, n_hbm, cross, cross2, chip, even, odd, f1z, g, b, w, d, wc, n, both, sums, sems
 ):
     copies = [
         pltpu.make_async_copy(src, dst, sems.at[k])
@@ -124,6 +129,17 @@
         for k in range(2):
             out[(3 + k) * BY : (4 + k) * BY, :] = w[place(layers[k])]
             out[(5 + k) * BY : (6 + k) * BY, :] = b[place(layers[k])]
+    for k in range(CX):
+        points = d[place(2 * k)] + d[place(2 * k + 1)]
+        for half in range(2):
+            sums[half, k * BY : (k + 1) * BY, :] = points[:, half * CZ : (half + 1) * CZ]
+    halves = [sums[k, pl.ds(0, CX * CY, stride=2), :] + sums[k, pl.ds(1, CX * CY, stride=2), :] for k in range(2)]
+    weight = OMEGA / (0.5 * pair_z(*halves) - 18.0)
+    wc[...] = weight
+    for k in range(CX):
+        v = weight[k * CY : (k + 1) * CY]
+        cross[tile(X_W, k)] = v
+        chip[tile(X_W, CX - 1 - k)] = v
     zero = jnp.zeros((BY, NZ), F32)
     for x in range(BX):
         at = place(x)
@@ -187,7 +203,7 @@
     take(both, even[...], odd[...])
 
 
-X2_D = 3 * BY
+X2_D = 2 * BY
 X2_ROWS = X2_D + 16
 
 
@@ -197,8 +213,8 @@
 
 
 def middle_kernel(
-    g, b, w, d, left1, cross2, chip, f1z, both1, even2, odd2,
-    f2, f2low, f2high, c1, wc, left, both, lo, hi, col, line, sums,
+    g, b, w, d, wc, left1, cross2, chip, f1z, both1, even2, odd2,
+    f2, f2low, f2high, c1, left, both, lo, hi, col, line, sums,
 ):
     left[...] = left1[...] + cross2[...]
     a = Wide(g, b, w, left, chip)
@@ -252,8 +268,8 @@
             + beside_y(f, line[0, x + 1 : x + 2, :], line[1, x + 1 : x + 2, :])
         )
         f2[(x + 1) * BY : (x + 2) * BY, :] = sec[x]
-    lo[2 * BY : X2_D, :] = sec[1]
-    hi[2 * BY : X2_D, :] = sec[6]
+    lo[BY:X2_D, :] = sec[1]
+    hi[BY:X2_D, :] = sec[6]
     for x in range(0, 8):
         f = sec[x]
         r = (
@@ -266,26 +282,18 @@
         )
         if x % 2:
             pairs = pairs + r
-            points = points + d[place(x)]
             at = (x // 2) * BY
             for half in range(2):
                 sums[half, at : at + BY, :] = pairs[:, half * CZ : (half + 1) * CZ]
-                sums[2 + half, at : at + BY, :] = points[:, half * CZ : (half + 1) * CZ]
         else:
-            pairs, points = r, d[place(x)]
-    doubled = [
-        sums[k, pl.ds(0, CX * CY, stride=2), :] + sums[k, pl.ds(1, CX * CY, stride=2), :] for k in range(4)
-    ]
-    total = pair_z(doubled[0], doubled[1])
-    diags = pair_z(doubled[2], doubled[3])
-    weight = OMEGA / (0.5 * diags - 18.0)
-    first = weight * (0.5 * total)
+            pairs = r
+    halves = [sums[k, pl.ds(0, CX * CY, stride=2), :] + sums[k, pl.ds(1, CX * CY, stride=2), :] for k in range(2)]
+    first = wc[...] * (0.5 * pair_z(*halves))
     c1[...] = first
-    wc[...] = weight
     for x in range(CX):
-        for out, k in ((lo, x), (hi, CX - 1 - x)):
-            out[k * CY : (k + 1) * CY, 0:CZ] = first[x * CY : (x + 1) * CY]
-            out[k * CY : (k + 1) * CY, CZ:] = weight[x * CY : (x + 1) * CY]
+        v = first[x * CY : (x + 1) * CY]
+        lo[tile(0, x)] = v
+        hi[tile(0, CX - 1 - x)] = v
 
 
 class Coarse:
@@ -299,7 +307,7 @@
         if 0 <= x < CX:
             return slab(self.wc, x, CY)
         ref, k = (self.left, -1 - x) if x < 0 else (self.right, x - CX)
-        return ref[k * CY : (k + 1) * CY, CZ:]
+        return ref[tile(X_W, k)]
 
 
 def corner_terms(a, low, high, relays, put):
@@ -348,10 +356,10 @@
     for k, v in enumerate(parts):
         terms[k] = v
     rows[...] = share
-    a = Coarse(c1x, wc, cleft, cright)
+    a = Coarse(c1x, wc, fine.left, fine.right)
     for x in range(1, CX):
-        c1x[(CX - 1 - x) * CY : (CX - x) * CY, :] = cleft[x * CY : (x + 1) * CY, 0:CZ]
-        c1x[(x + 2 * CX) * CY : (x + 2 * CX + 1) * CY, :] = cright[x * CY : (x + 1) * CY, 0:CZ]
+        c1x[(CX - 1 - x) * CY : (CX - x) * CY, :] = cleft[tile(0, x)]
+        c1x[(x + 2 * CX) * CY : (x + 2 * CX + 1) * CY, :] = cright[tile(0, x)]
     for x in range(1, CX - 1):
         c1x[(x + CX) * CY : (x + CX + 1) * CY, :] = slab(c1, x, CY)
     term = lambda k, e, s: terms[k, 2 * e + s : 2 * e + s + 1, :]
@@ -364,7 +372,7 @@
         )
         for i, cx in ((2 * e, cxe), (2 * e + 4, cxn)):
             at = (cx + CX) * CY
-            given = slab(c1, cx, CY) if 0 <= cx < CX else (cleft if cx < 0 else cright)[0:CY, 0:CZ]
+            given = slab(c1, cx, CY) if 0 <= cx < CX else (cleft if cx < 0 else cright)[tile(0, 0)]
             c1x[at : at + CY, :] = given + a.w(cx) * by_row(CY, {0: row(rows, i), CY - 1: row(rows, i + 1)})
     f2[2 * BY : 8 * BY, :] = f2in[2 * BY : 8 * BY, :]
     for s, (side, sidein) in enumerate(((f2low, f2lowin), (f2high, f2highin))):
@@ -421,7 +429,8 @@
     out, cboth, col, line, line3, corr, col2, s1, gline, g1line,
 ):
     wide = Wide(g, b, w, left, chip)
-    a = Coarse(c1x, wc, cleft, partner(cchip))
+    a = Coarse(c1x, wc, wide.left, wide.right)
+    cright = partner(cchip)
     take(cboth, even1[...] + even2[...], odd[...])
     low, high, clow, chigh = both.at[0], both.at[1], cboth.at[0], cboth.at[1]
     crow = lax.broadcasted_iota(jnp.int32, (CY, CZ), 0)
@@ -484,9 +493,9 @@
     g0 = {}
     for x in range(-2, 10):
         if x == -2:
-            f = slab(cleft, 2)
+            f = slab(cleft, 1)
         elif x == 9:
-            f = slab(a.right, 2)
+            f = slab(cright, 1)
         else:
             f = slab(f2, x + 1)
         g0[x] = f + corr_at((x + 2) // 2 * BY, BY)
@@ -566,13 +575,13 @@
 
 def body(g, b, n):
     block = (BX, BY, NZ)
-    cross, cross2, chip, even, odd, f1z, g, b, w, d = call(
+    cross, cross2, chip, even, odd, f1z, g, b, w, d, wc = call(
         load_kernel,
-        [(X_ROWS, NZ)] * 3 + [(Y_ROWS, NZ)] * 2 + [(BX * BY, NZ)] + [block] * 4,
+        [(X_ROWS, NZ)] * 3 + [(Y_ROWS, NZ)] * 2 + [(BX * BY, NZ)] + [block] * 4 + [(CX * CY, CZ)],
         g, b, n,
         hbm=3,
         vmem=None,
-        scratch=[pltpu.VMEM(block, jnp.int32), (2, Y_ROWS, NZ), pltpu.SemaphoreType.DMA((3,))],
+        scratch=[pltpu.VMEM(block, jnp.int32), (2, Y_ROWS, NZ), (2, CX * BY, CZ), pltpu.SemaphoreType.DMA((3,))],
     )
     cross1 = swap(cross, cross_pairs(lambda d: not is_end(d)))
     even1 = swap(even, dev_pairs(0, lambda d: not before_end(d)))
@@ -588,11 +597,11 @@
         cross1, even1, odd1,
         cost=pl.CostEstimate(flops=2**34, bytes_accessed=0, transcendentals=0),
     )
-    f2, f2low, f2high, c1, wc, left, both, cross, near = call(
+    f2, f2low, f2high, c1, left, both, cross, near = call(
         middle_kernel,
-        [(10 * BY, NZ), (BX, NZ), (BX, NZ), (CX * CY, CZ), (CX * CY, CZ), (X_ROWS, NZ), (2, Y_ROWS, NZ)] + [(X2_ROWS, NZ)] * 2,
-        g, b, w, d, left, cross2, chip, f1z, both, even2, odd2,
-        scratch=[(16, NZ), (2, 16, NZ), (4, CX * BY, CZ)],
+        [(10 * BY, NZ), (BX, NZ), (BX, NZ), (CX * CY, CZ), (X_ROWS, NZ), (2, Y_ROWS, NZ)] + [(X2_ROWS, NZ)] * 2,
+        g, b, w, d, wc, left, cross2, chip, f1z, both, even2, odd2,
+        scratch=[(16, NZ), (2, 16, NZ), (2, CX * BY, CZ)],
     )
     cleft = swap(cross, cross_pairs(lambda d: True))
     cchip = share_chip(near)

time: 43.3 us -> 43.2 us (level)
  the two profiles are of different devices: /device:TPU:25 before, /device:TPU:28 now
where the time goes in v14:
time: 43.2 us; the launch traced here: 42.9 us
  starting transfers between devices  31.5 us (73%)
  blocking collectives  4.55 us (11%)
  waiting for transfers between devices  3.42 us (8%)
  Pallas kernels  3.28 us (8%)
    ppermute x10, starting transfers between devices, swap(): return lax.ppermute(v, ('group', 'dev'), links + [(j, i) for i, j in links])  31.5 us
    all_gather x2, blocking collectives, share_chip(): return lax.all_gather(v, 'group', axis_index_groups=groups)  4.55 us
    ppermute x10, waiting for transfers between devices, swap(): return lax.ppermute(v, ('group', 'dev'), links + [(j, i) for i, j in links])  3.42 us
    pallas_call x6, Pallas kernels, call(): pl.pallas_call(kernel, out_shape=[make(s, F32) for s in outs], in_specs=[...  3.28 us
  transfers between devices with their start and end apart: 10, of which 2 were waited for; matrix products, arithmetic and copies ran while one was open for 0% of the time, Pallas kernels for 0%

profile of v14, /device:TPU:28, one launch (start us, length us, event | category | flops | bytes accessed | tf_op | source)
XLA Modules:
  0.0 42.9 jit_solution(14201022250030856898)
XLA Ops:
  0.0 1.3 %shard_map.37 = (f32[128,256]{1,0:T(8,128)S(1)}, f32[128,256]{1,0:T(8,128)S(1)}, f32[128,256]{1,0:T(8,128)S(1)}, f32[40,256]{1,0:T(8,128)S(1)}, f32[40,256]{1,0:...) custom-call(f32[8,16,256]{2,1,0:T(8,128)} %g_hbm.1, ...), custom_call_target="tpu_custom_call" | custom-call | tf_op jit(solution)/shard_map/pallas_call | solution.py:19
  1.3 1.9 %collective-permute-start = (f32[128,256]{1,0:T(8,128)S(1)}, f32[128,256]{1,0:T(8,128)S(1)}, u32[]{:S(2)}, u32[]{:S(2)}) collective-permute-start(f32[128,256]{1,0:T(8,128)S(1)} %get-tuple-element.42), channel_id=1, source_target_pairs={{128,256},{129,257},{130,258},{131,259},{132,260},{133,261},{134,2... | collective-permute-start | bytes 393224 | tf_op jit(solution)/shard_map/ppermute | solution.py:550
  3.2 3.8 %collective-permute-start.1 = (f32[40,256]{1,0:T(8,128)S(1)}, f32[40,256]{1,0:T(8,128)S(1)}, u32[]{:S(2)}, u32[]{:S(2)}) collective-permute-start(f32[40,256]{1,0:T(8,128)S(1)} %get-tuple-element.43.even), channel_id=1, source_target_pairs={{0,1},{2,3},{4,5},{6,7},{8,9},{10,11},{12,13},{14,15},{16,17},{18,... | collective-permute-start | bytes 122888 | tf_op jit(solution)/shard_map/ppermute | solution.py:550
  7.0 14.4 %collective-permute-start.2 = (f32[40,256]{1,0:T(8,128)S(1)}, f32[40,256]{1,0:T(8,128)S(1)}, u32[]{:S(2)}, u32[]{:S(2)}) collective-permute-start(f32[40,256]{1,0:T(8,128)S(1)} %get-tuple-element.44.odd), channel_id=1, source_target_pairs={{1,2},{3,4},{5,6},{7,8},{9,10},{11,12},{13,14},{15,16},{17,18},{19... | collective-permute-start | bytes 122888 | tf_op jit(solution)/shard_map/ppermute | solution.py:550
  21.5 0.7 %collective-permute-start.3 = (f32[128,256]{1,0:T(8,128)S(1)}, f32[128,256]{1,0:T(8,128)S(1)}, u32[]{:S(2)}, u32[]{:S(2)}) collective-permute-start(f32[128,256]{1,0:T(8,128)S(1)} %get-tuple-element.46), channel_id=1, source_target_pairs={{159,287},{191,319},{223,351},{255,383},{415,543},{447,575},{479,6... | collective-permute-start | bytes 393224 | tf_op jit(solution)/shard_map/ppermute | solution.py:550
  22.2 0.0 collective-permute-done.1.even.met
  22.2 0.7 %collective-permute-start.4 = (f32[40,256]{1,0:T(8,128)S(1)}, f32[40,256]{1,0:T(8,128)S(1)}, u32[]{:S(2)}, u32[]{:S(2)}) collective-permute-start(f32[40,256]{1,0:T(8,128)S(1)} %get-tuple-element.51), channel_id=1, source_target_pairs={{30,31},{62,63},{94,95},{126,127},{158,159},{190,191},{222,223},{2... | collective-permute-start | bytes 122888 | tf_op jit(solution)/shard_map/ppermute | solution.py:550
  22.9 0.7 %collective-permute-start.5 = (f32[40,256]{1,0:T(8,128)S(1)}, f32[40,256]{1,0:T(8,128)S(1)}, u32[]{:S(2)}, u32[]{:S(2)}) collective-permute-start(f32[40,256]{1,0:T(8,128)S(1)} %get-tuple-element.52), channel_id=1, source_target_pairs={{29,30},{61,62},{93,94},{125,126},{157,158},{189,190},{221,222},{2... | collective-permute-start | bytes 122888 | tf_op jit(solution)/shard_map/ppermute | solution.py:550
  23.6 2.0 %all-gather = f32[256,256]{1,0:T(8,128)S(1)} all-gather(f32[128,256]{1,0:T(8,128)S(1)} %get-tuple-element.48), channel_id=2, replica_groups={{0,128},{256,384},{512,640},{768,896},{1,129},{257,385},{513,641},{769,..., dimensions={0}, use_global_device_ids=true | all-gather | bytes 393216 | tf_op jit(solution)/shard_map/all_gather | solution.py:555
  25.6 0.0 collective-permute-done.2.odd
  25.6 0.0 collective-permute-done.cross
  25.6 0.0 collective-permute-done.5.odd2
  25.6 0.0 collective-permute-done.3.cross2
  25.6 0.4 shard_map.40
  26.0 2.2 %collective-permute-start.6 = (f32[48,256]{1,0:T(8,128)S(1)}, f32[48,256]{1,0:T(8,128)S(1)}, u32[]{:S(2)}, u32[]{:S(2)}) collective-permute-start(f32[48,256]{1,0:T(8,128)S(1)} %get-tuple-element.59), channel_id=1, source_target_pairs={{128,256},{129,257},{130,258},{131,259},{132,260},{133,261},{134,2... | collective-permute-start | bytes 147464 | tf_op jit(solution)/shard_map/ppermute | solution.py:550
  28.2 2.6 %all-gather.1 = f32[96,256]{1,0:T(8,128)S(1)} all-gather(f32[48,256]{1,0:T(8,128)S(1)} %get-tuple-element.60), channel_id=3, replica_groups={{0,128},{256,384},{512,640},{768,896},{1,129},{257,385},{513,641},{769,..., dimensions={0}, use_global_device_ids=true | all-gather | bytes 147456 | tf_op jit(solution)/shard_map/all_gather | solution.py:555
  30.8 0.7 %collective-permute-done.6.cleft = f32[48,256]{1,0:T(8,128)S(1)} collective-permute-done((f32[48,256]{1,0:T(8,128)S(1)}, f32[48,256]{1,0:T(8,128)S(1)}, u32[]{:S(2)}, u32[]{:S(2)}) %collective-permute-start.6) | collective-permute-done | bytes 49184 | tf_op jit(solution)/shard_map/ppermute | solution.py:550
  31.5 0.4 shard_map.41
  31.8 1.9 %collective-permute-start.7 = (f32[72,128]{1,0:T(8,128)S(1)}, f32[72,128]{1,0:T(8,128)S(1)}, u32[]{:S(2)}, u32[]{:S(2)}) collective-permute-start(f32[72,128]{1,0:T(8,128)S(1)} %get-tuple-element.66), channel_id=1, source_target_pairs={{0,1},{2,3},{4,5},{6,7},{8,9},{10,11},{12,13},{14,15},{16,17},{18,... | collective-permute-start | bytes 110600 | tf_op jit(solution)/shard_map/ppermute | solution.py:550
  33.8 4.5 %collective-permute-start.8 = (f32[72,128]{1,0:T(8,128)S(1)}, f32[72,128]{1,0:T(8,128)S(1)}, u32[]{:S(2)}, u32[]{:S(2)}) collective-permute-start(f32[72,128]{1,0:T(8,128)S(1)} %get-tuple-element.67), channel_id=1, source_target_pairs={{1,2},{3,4},{5,6},{7,8},{9,10},{11,12},{13,14},{15,16},{17,18},{19... | collective-permute-start | bytes 110600 | tf_op jit(solution)/shard_map/ppermute | solution.py:550
  38.3 0.7 %collective-permute-start.9 = (f32[72,128]{1,0:T(8,128)S(1)}, f32[72,128]{1,0:T(8,128)S(1)}, u32[]{:S(2)}, u32[]{:S(2)}) collective-permute-start(f32[72,128]{1,0:T(8,128)S(1)} %get-tuple-element.68), channel_id=1, source_target_pairs={{30,31},{62,63},{94,95},{126,127},{158,159},{190,191},{222,223},{2... | collective-permute-start | bytes 110600 | tf_op jit(solution)/shard_map/ppermute | solution.py:550
  39.0 0.0 collective-permute-done.7.even1
  39.0 2.8 %collective-permute-done.8.odd = f32[72,128]{1,0:T(8,128)S(1)} collective-permute-done((f32[72,128]{1,0:T(8,128)S(1)}, f32[72,128]{1,0:T(8,128)S(1)}, u32[]{:S(2)}, u32[]{:S(2)}) %collective-permute-start.8) | collective-permute-done | bytes 36896 | tf_op jit(solution)/shard_map/ppermute | solution.py:550
  41.7 1.2 %shard_map.42 = f32[8,16,256]{2,1,0:T(8,128)} custom-call(f32[8,16,256]{2,1,0:T(8,128)S(1)} %get-tuple-element.37.g, f32[8,16,256]{2,1,0:T(8,128)S(1)} %get-tuple-element.38.b, f32[8,16,256]{2,1,0:T(8,128)S(1)} %get-tuple-element.39.w, f32[128,256]{1,0:T(8,128)S(1)} %get-tuple-element.53.left, f32[2,128,256]{2,1,0:T(8,128)S(1)} %bitcast.4, ...), custom_call_target="tpu_custom_call" | custom-call | tf_op jit(solution)/shard_map/pallas_call | solution.py:19
  (4 shorter events, 0.0 us)
Async XLA Ops:
  1.3 24.3 %collective-permute-start = (f32[128,256]{1,0:T(8,128)S(1)}, f32[128,256]{1,0:T(8,128)S(1)}, u32[]{:S(2)}, u32[]{:S(2)}) collective-permute-start(f32[128,256]{1,0:T(8,128)S(1)} %get-tuple-element.42), channel_id=1, source_target_pairs={{128,256},{129,257},{130,258},{131,259},{132,260},{133,261},{134,2... | collective-permute-start | bytes 393224 | tf_op jit(solution)/shard_map/ppermute | solution.py:550
  3.2 19.0 %collective-permute-start.1 = (f32[40,256]{1,0:T(8,128)S(1)}, f32[40,256]{1,0:T(8,128)S(1)}, u32[]{:S(2)}, u32[]{:S(2)}) collective-permute-start(f32[40,256]{1,0:T(8,128)S(1)} %get-tuple-element.43.even), channel_id=1, source_target_pairs={{0,1},{2,3},{4,5},{6,7},{8,9},{10,11},{12,13},{14,15},{16,17},{18,... | collective-permute-start | bytes 122888 | tf_op jit(solution)/shard_map/ppermute | solution.py:550
  7.0 18.5 %collective-permute-start.2 = (f32[40,256]{1,0:T(8,128)S(1)}, f32[40,256]{1,0:T(8,128)S(1)}, u32[]{:S(2)}, u32[]{:S(2)}) collective-permute-start(f32[40,256]{1,0:T(8,128)S(1)} %get-tuple-element.44.odd), channel_id=1, source_target_pairs={{1,2},{3,4},{5,6},{7,8},{9,10},{11,12},{13,14},{15,16},{17,18},{19... | collective-permute-start | bytes 122888 | tf_op jit(solution)/shard_map/ppermute | solution.py:550
  21.5 4.1 %collective-permute-start.3 = (f32[128,256]{1,0:T(8,128)S(1)}, f32[128,256]{1,0:T(8,128)S(1)}, u32[]{:S(2)}, u32[]{:S(2)}) collective-permute-start(f32[128,256]{1,0:T(8,128)S(1)} %get-tuple-element.46), channel_id=1, source_target_pairs={{159,287},{191,319},{223,351},{255,383},{415,543},{447,575},{479,6... | collective-permute-start | bytes 393224 | tf_op jit(solution)/shard_map/ppermute | solution.py:550
  22.2 3.4 %collective-permute-start.4 = (f32[40,256]{1,0:T(8,128)S(1)}, f32[40,256]{1,0:T(8,128)S(1)}, u32[]{:S(2)}, u32[]{:S(2)}) collective-permute-start(f32[40,256]{1,0:T(8,128)S(1)} %get-tuple-element.51), channel_id=1, source_target_pairs={{30,31},{62,63},{94,95},{126,127},{158,159},{190,191},{222,223},{2... | collective-permute-start | bytes 122888 | tf_op jit(solution)/shard_map/ppermute | solution.py:550
  22.9 2.7 %collective-permute-start.5 = (f32[40,256]{1,0:T(8,128)S(1)}, f32[40,256]{1,0:T(8,128)S(1)}, u32[]{:S(2)}, u32[]{:S(2)}) collective-permute-start(f32[40,256]{1,0:T(8,128)S(1)} %get-tuple-element.52), channel_id=1, source_target_pairs={{29,30},{61,62},{93,94},{125,126},{157,158},{189,190},{221,222},{2... | collective-permute-start | bytes 122888 | tf_op jit(solution)/shard_map/ppermute | solution.py:550
  26.0 5.4 %collective-permute-start.6 = (f32[48,256]{1,0:T(8,128)S(1)}, f32[48,256]{1,0:T(8,128)S(1)}, u32[]{:S(2)}, u32[]{:S(2)}) collective-permute-start(f32[48,256]{1,0:T(8,128)S(1)} %get-tuple-element.59), channel_id=1, source_target_pairs={{128,256},{129,257},{130,258},{131,259},{132,260},{133,261},{134,2... | collective-permute-start | bytes 147464 | tf_op jit(solution)/shard_map/ppermute | solution.py:550
  31.8 7.1 %collective-permute-start.7 = (f32[72,128]{1,0:T(8,128)S(1)}, f32[72,128]{1,0:T(8,128)S(1)}, u32[]{:S(2)}, u32[]{:S(2)}) collective-permute-start(f32[72,128]{1,0:T(8,128)S(1)} %get-tuple-element.66), channel_id=1, source_target_pairs={{0,1},{2,3},{4,5},{6,7},{8,9},{10,11},{12,13},{14,15},{16,17},{18,... | collective-permute-start | bytes 110600 | tf_op jit(solution)/shard_map/ppermute | solution.py:550
  33.8 8.0 %collective-permute-start.8 = (f32[72,128]{1,0:T(8,128)S(1)}, f32[72,128]{1,0:T(8,128)S(1)}, u32[]{:S(2)}, u32[]{:S(2)}) collective-permute-start(f32[72,128]{1,0:T(8,128)S(1)} %get-tuple-element.67), channel_id=1, source_target_pairs={{1,2},{3,4},{5,6},{7,8},{9,10},{11,12},{13,14},{15,16},{17,18},{19... | collective-permute-start | bytes 110600 | tf_op jit(solution)/shard_map/ppermute | solution.py:550
  38.3 3.4 %collective-permute-start.9 = (f32[72,128]{1,0:T(8,128)S(1)}, f32[72,128]{1,0:T(8,128)S(1)}, u32[]{:S(2)}, u32[]{:S(2)}) collective-permute-start(f32[72,128]{1,0:T(8,128)S(1)} %get-tuple-element.68), channel_id=1, source_target_pairs={{30,31},{62,63},{94,95},{126,127},{158,159},{190,191},{222,223},{2... | collective-permute-start | bytes 110600 | tf_op jit(solution)/shard_map/ppermute | solution.py:550

commit v15 on v14

--- a/solution.py
+++ b/solution.py
@@ -544,10 +544,17 @@
         )
 
 
+def send(v, links):
+    n = lax.axis_size("dev")
+    return lax.ppermute(v, ("group", "dev"), [(i * n + j, k * n + l) for (i, j), (k, l) in links])
+
+
+def back(links):
+    return [(j, i) for i, j in links]
+
+
 def swap(v, pairs):
-    n = lax.axis_size("dev")
-    links = [(i * n + j, k * n + l) for (i, j), (k, l) in pairs]
-    return lax.ppermute(v, ("group", "dev"), links + [(j, i) for i, j in links])
+    return send(v, pairs + back(pairs))
 
 
 def share_chip(v):
@@ -563,6 +570,14 @@
 def dev_pairs(start, keep):
     devs = [d for d in range(start, lax.axis_size("dev") - 1, 2) if keep(d)]
     return [((i, d), (i, d + 1)) for i in range(lax.axis_size("group")) for d in devs]
+
+
+def is_start(d):
+    return d % RUN == 0
+
+
+def in_middle(d):
+    return not (is_start(d) or before_end(d))
 
 
 def is_end(d):
@@ -611,9 +626,10 @@
         g, b, w, left, chip, both, f2, f2low, f2high, c1, wc, cleft, cchip,
         scratch=[(13, 8, NZ), (5, 8, NZ), (8, CZ), (2, Z_ROWS, CZ)],
     )
-    even1 = swap(even, dev_pairs(0, lambda d: not before_end(d)))
+    inner, start, end = (dev_pairs(0, keep) for keep in (in_middle, is_start, before_end))
+    even1 = send(even, inner + back(inner) + back(start))
     odd = swap(odd, dev_pairs(1, lambda d: True))
-    even2 = swap(even2, dev_pairs(0, before_end))
+    even2 = send(even2, end + back(end) + start)
     (out,) = call(
         last_kernel,
         [block],

time: 43.2 us -> 43.2 us (level)
  the two profiles are of different devices: /device:TPU:28 before, /device:TPU:62 now
where the time goes in v15:
time: 43.2 us; the launch traced here: 42.9 us
  starting transfers between devices  30.2 us (70%)
  waiting for transfers between devices  5.4 us (12%)
  blocking collectives  3.87 us (9%)
  Pallas kernels  3.29 us (8%)
    ppermute x10, starting transfers between devices, send(): lax.ppermute(v, ('group', 'dev'), [(i * n + j, k * n + l) for (i, j), (k,...  30.2 us
    ppermute x10, waiting for transfers between devices, send(): lax.ppermute(v, ('group', 'dev'), [(i * n + j, k * n + l) for (i, j), (k,...  5.4 us
    all_gather x2, blocking collectives, share_chip(): return lax.all_gather(v, 'group', axis_index_groups=groups)  3.87 us
    pallas_call x6, Pallas kernels, call(): pl.pallas_call(kernel, out_shape=[make(s, F32) for s in outs], in_specs=[...  3.29 us
  transfers between devices with their start and end apart: 10, of which 3 were waited for; matrix products, arithmetic and copies ran while one was open for 0% of the time, Pallas kernels for 0%

profile of v15, /device:TPU:62, one launch (start us, length us, event | category | flops | bytes accessed | tf_op | source)
XLA Modules:
  0.0 42.9 jit_solution(8889270067999799060)
XLA Ops:
  0.0 1.3 %shard_map.37 = (f32[128,256]{1,0:T(8,128)S(1)}, f32[128,256]{1,0:T(8,128)S(1)}, f32[128,256]{1,0:T(8,128)S(1)}, f32[40,256]{1,0:T(8,128)S(1)}, f32[40,256]{1,0:...) custom-call(f32[8,16,256]{2,1,0:T(8,128)} %g_hbm.1, ...), custom_call_target="tpu_custom_call" | custom-call | tf_op jit(solution)/shard_map/pallas_call | solution.py:19
  1.3 2.2 %collective-permute-start = (f32[128,256]{1,0:T(8,128)S(1)}, f32[128,256]{1,0:T(8,128)S(1)}, u32[]{:S(2)}, u32[]{:S(2)}) collective-permute-start(f32[128,256]{1,0:T(8,128)S(1)} %get-tuple-element.42), channel_id=1, source_target_pairs={{128,256},{129,257},{130,258},{131,259},{132,260},{133,261},{134,2... | collective-permute-start | bytes 393224 | tf_op jit(solution)/shard_map/ppermute | solution.py:549
  3.5 2.0 %collective-permute-start.1 = (f32[40,256]{1,0:T(8,128)S(1)}, f32[40,256]{1,0:T(8,128)S(1)}, u32[]{:S(2)}, u32[]{:S(2)}) collective-permute-start(f32[40,256]{1,0:T(8,128)S(1)} %get-tuple-element.43.even), channel_id=1, source_target_pairs={{0,1},{2,3},{4,5},{6,7},{8,9},{10,11},{12,13},{14,15},{16,17},{18,... | collective-permute-start | bytes 122888 | tf_op jit(solution)/shard_map/ppermute | solution.py:549
  5.5 5.6 %collective-permute-start.2 = (f32[40,256]{1,0:T(8,128)S(1)}, f32[40,256]{1,0:T(8,128)S(1)}, u32[]{:S(2)}, u32[]{:S(2)}) collective-permute-start(f32[40,256]{1,0:T(8,128)S(1)} %get-tuple-element.44.odd), channel_id=1, source_target_pairs={{1,2},{3,4},{5,6},{7,8},{9,10},{11,12},{13,14},{15,16},{17,18},{19... | collective-permute-start | bytes 122888 | tf_op jit(solution)/shard_map/ppermute | solution.py:549
  11.1 0.7 %collective-permute-start.3 = (f32[128,256]{1,0:T(8,128)S(1)}, f32[128,256]{1,0:T(8,128)S(1)}, u32[]{:S(2)}, u32[]{:S(2)}) collective-permute-start(f32[128,256]{1,0:T(8,128)S(1)} %get-tuple-element.46), channel_id=1, source_target_pairs={{159,287},{191,319},{223,351},{255,383},{415,543},{447,575},{479,6... | collective-permute-start | bytes 393224 | tf_op jit(solution)/shard_map/ppermute | solution.py:549
  11.8 0.0 collective-permute-done.1.even.met
  11.9 0.7 %collective-permute-start.4 = (f32[40,256]{1,0:T(8,128)S(1)}, f32[40,256]{1,0:T(8,128)S(1)}, u32[]{:S(2)}, u32[]{:S(2)}) collective-permute-start(f32[40,256]{1,0:T(8,128)S(1)} %get-tuple-element.51), channel_id=1, source_target_pairs={{30,31},{62,63},{94,95},{126,127},{158,159},{190,191},{222,223},{2... | collective-permute-start | bytes 122888 | tf_op jit(solution)/shard_map/ppermute | solution.py:549
  12.5 0.7 %collective-permute-start.5 = (f32[40,256]{1,0:T(8,128)S(1)}, f32[40,256]{1,0:T(8,128)S(1)}, u32[]{:S(2)}, u32[]{:S(2)}) collective-permute-start(f32[40,256]{1,0:T(8,128)S(1)} %get-tuple-element.52), channel_id=1, source_target_pairs={{29,30},{61,62},{93,94},{125,126},{157,158},{189,190},{221,222},{2... | collective-permute-start | bytes 122888 | tf_op jit(solution)/shard_map/ppermute | solution.py:549
  13.2 2.0 %all-gather = f32[256,256]{1,0:T(8,128)S(1)} all-gather(f32[128,256]{1,0:T(8,128)S(1)} %get-tuple-element.48), channel_id=2, replica_groups={{0,128},{256,384},{512,640},{768,896},{1,129},{257,385},{513,641},{769,..., dimensions={0}, use_global_device_ids=true | all-gather | bytes 393216 | tf_op jit(solution)/shard_map/all_gather | solution.py:562
  15.2 0.0 collective-permute-done.2.odd
  15.2 0.0 collective-permute-done.4.even2
  15.2 0.0 collective-permute-done.5.odd2
  15.3 0.4 shard_map.40
  15.7 2.8 %collective-permute-start.6 = (f32[48,256]{1,0:T(8,128)S(1)}, f32[48,256]{1,0:T(8,128)S(1)}, u32[]{:S(2)}, u32[]{:S(2)}) collective-permute-start(f32[48,256]{1,0:T(8,128)S(1)} %get-tuple-element.59), channel_id=1, source_target_pairs={{128,256},{129,257},{130,258},{131,259},{132,260},{133,261},{134,2... | collective-permute-start | bytes 147464 | tf_op jit(solution)/shard_map/ppermute | solution.py:549
  18.5 1.9 %all-gather.1 = f32[96,256]{1,0:T(8,128)S(1)} all-gather(f32[48,256]{1,0:T(8,128)S(1)} %get-tuple-element.60), channel_id=3, replica_groups={{0,128},{256,384},{512,640},{768,896},{1,129},{257,385},{513,641},{769,..., dimensions={0}, use_global_device_ids=true | all-gather | bytes 147456 | tf_op jit(solution)/shard_map/all_gather | solution.py:562
  20.4 0.7 %collective-permute-done.6.cleft = f32[48,256]{1,0:T(8,128)S(1)} collective-permute-done((f32[48,256]{1,0:T(8,128)S(1)}, f32[48,256]{1,0:T(8,128)S(1)}, u32[]{:S(2)}, u32[]{:S(2)}) %collective-permute-start.6) | collective-permute-done | bytes 49184 | tf_op jit(solution)/shard_map/ppermute | solution.py:549
  21.1 0.4 shard_map.41
  21.5 12.4 %collective-permute-start.7 = (f32[72,128]{1,0:T(8,128)S(1)}, f32[72,128]{1,0:T(8,128)S(1)}, u32[]{:S(2)}, u32[]{:S(2)}) collective-permute-start(f32[72,128]{1,0:T(8,128)S(1)} %get-tuple-element.66), channel_id=1, source_target_pairs={{2,3},{4,5},{6,7},{8,9},{10,11},{12,13},{14,15},{16,17},{18,19},{2... | collective-permute-start | bytes 110600 | tf_op jit(solution)/shard_map/ppermute | solution.py:549
  33.8 1.9 %collective-permute-start.8 = (f32[72,128]{1,0:T(8,128)S(1)}, f32[72,128]{1,0:T(8,128)S(1)}, u32[]{:S(2)}, u32[]{:S(2)}) collective-permute-start(f32[72,128]{1,0:T(8,128)S(1)} %get-tuple-element.67), channel_id=1, source_target_pairs={{1,2},{3,4},{5,6},{7,8},{9,10},{11,12},{13,14},{15,16},{17,18},{19... | collective-permute-start | bytes 110600 | tf_op jit(solution)/shard_map/ppermute | solution.py:549
  35.8 1.3 %collective-permute-start.9 = (f32[72,128]{1,0:T(8,128)S(1)}, f32[72,128]{1,0:T(8,128)S(1)}, u32[]{:S(2)}, u32[]{:S(2)}) collective-permute-start(f32[72,128]{1,0:T(8,128)S(1)} %get-tuple-element.68), channel_id=1, source_target_pairs={{30,31},{62,63},{94,95},{126,127},{158,159},{190,191},{222,223},{2... | collective-permute-start | bytes 110600 | tf_op jit(solution)/shard_map/ppermute | solution.py:549
  37.1 0.0 collective-permute-done.7.even1
  37.1 2.6 %collective-permute-done.8.odd = f32[72,128]{1,0:T(8,128)S(1)} collective-permute-done((f32[72,128]{1,0:T(8,128)S(1)}, f32[72,128]{1,0:T(8,128)S(1)}, u32[]{:S(2)}, u32[]{:S(2)}) %collective-permute-start.8) | collective-permute-done | bytes 36896 | tf_op jit(solution)/shard_map/ppermute | solution.py:549
  39.7 2.1 %collective-permute-done.9.even2 = f32[72,128]{1,0:T(8,128)S(1)} collective-permute-done((f32[72,128]{1,0:T(8,128)S(1)}, f32[72,128]{1,0:T(8,128)S(1)}, u32[]{:S(2)}, u32[]{:S(2)}) %collective-permute-start.9) | collective-permute-done | bytes 36896 | tf_op jit(solution)/shard_map/ppermute | solution.py:549
  41.8 1.2 %shard_map.42 = f32[8,16,256]{2,1,0:T(8,128)} custom-call(f32[8,16,256]{2,1,0:T(8,128)S(1)} %get-tuple-element.37.g, f32[8,16,256]{2,1,0:T(8,128)S(1)} %get-tuple-element.38.b, f32[8,16,256]{2,1,0:T(8,128)S(1)} %get-tuple-element.39.w, f32[128,256]{1,0:T(8,128)S(1)} %get-tuple-element.53.left, f32[2,128,256]{2,1,0:T(8,128)S(1)} %bitcast.4, ...), custom_call_target="tpu_custom_call" | custom-call | tf_op jit(solution)/shard_map/pallas_call | solution.py:19
  (4 shorter events, 0.0 us)
Async XLA Ops:
  1.3 13.9 %collective-permute-start = (f32[128,256]{1,0:T(8,128)S(1)}, f32[128,256]{1,0:T(8,128)S(1)}, u32[]{:S(2)}, u32[]{:S(2)}) collective-permute-start(f32[128,256]{1,0:T(8,128)S(1)} %get-tuple-element.42), channel_id=1, source_target_pairs={{128,256},{129,257},{130,258},{131,259},{132,260},{133,261},{134,2... | collective-permute-start | bytes 393224 | tf_op jit(solution)/shard_map/ppermute | solution.py:549
  3.5 8.3 %collective-permute-start.1 = (f32[40,256]{1,0:T(8,128)S(1)}, f32[40,256]{1,0:T(8,128)S(1)}, u32[]{:S(2)}, u32[]{:S(2)}) collective-permute-start(f32[40,256]{1,0:T(8,128)S(1)} %get-tuple-element.43.even), channel_id=1, source_target_pairs={{0,1},{2,3},{4,5},{6,7},{8,9},{10,11},{12,13},{14,15},{16,17},{18,... | collective-permute-start | bytes 122888 | tf_op jit(solution)/shard_map/ppermute | solution.py:549
  5.5 9.7 %collective-permute-start.2 = (f32[40,256]{1,0:T(8,128)S(1)}, f32[40,256]{1,0:T(8,128)S(1)}, u32[]{:S(2)}, u32[]{:S(2)}) collective-permute-start(f32[40,256]{1,0:T(8,128)S(1)} %get-tuple-element.44.odd), channel_id=1, source_target_pairs={{1,2},{3,4},{5,6},{7,8},{9,10},{11,12},{13,14},{15,16},{17,18},{19... | collective-permute-start | bytes 122888 | tf_op jit(solution)/shard_map/ppermute | solution.py:549
  11.1 4.1 %collective-permute-start.3 = (f32[128,256]{1,0:T(8,128)S(1)}, f32[128,256]{1,0:T(8,128)S(1)}, u32[]{:S(2)}, u32[]{:S(2)}) collective-permute-start(f32[128,256]{1,0:T(8,128)S(1)} %get-tuple-element.46), channel_id=1, source_target_pairs={{159,287},{191,319},{223,351},{255,383},{415,543},{447,575},{479,6... | collective-permute-start | bytes 393224 | tf_op jit(solution)/shard_map/ppermute | solution.py:549
  11.9 3.4 %collective-permute-start.4 = (f32[40,256]{1,0:T(8,128)S(1)}, f32[40,256]{1,0:T(8,128)S(1)}, u32[]{:S(2)}, u32[]{:S(2)}) collective-permute-start(f32[40,256]{1,0:T(8,128)S(1)} %get-tuple-element.51), channel_id=1, source_target_pairs={{30,31},{62,63},{94,95},{126,127},{158,159},{190,191},{222,223},{2... | collective-permute-start | bytes 122888 | tf_op jit(solution)/shard_map/ppermute | solution.py:549
  12.5 2.7 %collective-permute-start.5 = (f32[40,256]{1,0:T(8,128)S(1)}, f32[40,256]{1,0:T(8,128)S(1)}, u32[]{:S(2)}, u32[]{:S(2)}) collective-permute-start(f32[40,256]{1,0:T(8,128)S(1)} %get-tuple-element.52), channel_id=1, source_target_pairs={{29,30},{61,62},{93,94},{125,126},{157,158},{189,190},{221,222},{2... | collective-permute-start | bytes 122888 | tf_op jit(solution)/shard_map/ppermute | solution.py:549
  15.7 5.4 %collective-permute-start.6 = (f32[48,256]{1,0:T(8,128)S(1)}, f32[48,256]{1,0:T(8,128)S(1)}, u32[]{:S(2)}, u32[]{:S(2)}) collective-permute-start(f32[48,256]{1,0:T(8,128)S(1)} %get-tuple-element.59), channel_id=1, source_target_pairs={{128,256},{129,257},{130,258},{131,259},{132,260},{133,261},{134,2... | collective-permute-start | bytes 147464 | tf_op jit(solution)/shard_map/ppermute | solution.py:549
  21.5 15.6 %collective-permute-start.7 = (f32[72,128]{1,0:T(8,128)S(1)}, f32[72,128]{1,0:T(8,128)S(1)}, u32[]{:S(2)}, u32[]{:S(2)}) collective-permute-start(f32[72,128]{1,0:T(8,128)S(1)} %get-tuple-element.66), channel_id=1, source_target_pairs={{2,3},{4,5},{6,7},{8,9},{10,11},{12,13},{14,15},{16,17},{18,19},{2... | collective-permute-start | bytes 110600 | tf_op jit(solution)/shard_map/ppermute | solution.py:549
  33.8 5.9 %collective-permute-start.8 = (f32[72,128]{1,0:T(8,128)S(1)}, f32[72,128]{1,0:T(8,128)S(1)}, u32[]{:S(2)}, u32[]{:S(2)}) collective-permute-start(f32[72,128]{1,0:T(8,128)S(1)} %get-tuple-element.67), channel_id=1, source_target_pairs={{1,2},{3,4},{5,6},{7,8},{9,10},{11,12},{13,14},{15,16},{17,18},{19... | collective-permute-start | bytes 110600 | tf_op jit(solution)/shard_map/ppermute | solution.py:549
  35.8 6.0 %collective-permute-start.9 = (f32[72,128]{1,0:T(8,128)S(1)}, f32[72,128]{1,0:T(8,128)S(1)}, u32[]{:S(2)}, u32[]{:S(2)}) collective-permute-start(f32[72,128]{1,0:T(8,128)S(1)} %get-tuple-element.68), channel_id=1, source_target_pairs={{30,31},{62,63},{94,95},{126,127},{158,159},{190,191},{222,223},{2... | collective-permute-start | bytes 110600 | tf_op jit(solution)/shard_map/ppermute | solution.py:549
